TPU v7x, 32 devices: a whole 2x2x4 slice. The times are simulated.
32 devices in a mesh: grp: 2 (over x), tm: 16 (over z, y, core).
Axes of the slice: x: 2, y: 2, z: 4, core: 2. Of those that a mesh axis runs over, the one named last changes fastest.
Arguments:
- frames_in: bfloat16 [16384, 1536], P(('grp', 'tm')), parts along dimension 0, may hold values from -6 to 6
- frame_time: int32 [64], P('grp'), parts along dimension 0, may hold values from 0 to 31, each once
- norm_gain: float32 [1536], replicated, may hold values from 0.25 to 1.75
- w_query: bfloat16 [1536, 768], replicated, may hold values from -2 to 2
- w_key: bfloat16 [1536, 768], replicated, may hold values from -2 to 2
- w_value: bfloat16 [1536, 768], replicated, may hold values from -0.15625 to 0.15625
- w_output: bfloat16 [768, 1536], replicated, may hold values from -0.21875 to 0.21875
Outputs:
- attended: bfloat16 [16384, 1536], P(('grp', 'tm')), parts along dimension 0
There are 2 independent parts, one for each index of `grp`. A program takes and returns all parts, laid end to end along the dimension named above; an argument that names none is the same for every part. Nothing has to cross between parts.
Inputs may be any that keep to these rules, and one draw needn't show every extreme that they name: `frame_time`: each of 0 to 31 stands once.
All inputs are finite; a program needn't handle non-finite values.
Results may differ from a plain program's by a relative error of at most 0.004.
The roundings to bfloat16 on the way count: a program that leaves them out, or rounds other values in their place, can miss the bound.
Values may be sent and summed in bfloat16 or wider, within the bound.
No kernel may reach another device: no remote copies, remote signals or barrier semaphores. Data moves between devices by JAX's collectives and lax.ppermute only.
A program may use at most 128 MiB of HBM per device.

v0:
```python
import jax
import jax.numpy as jnp
from jax import lax
from jax.sharding import PartitionSpec as P

HEADS = 6
HD = 128
HH = 16
WW = 16
WIN = 8
POOL = 4


def normed_rows(frames_in, norm_gain):
    values_f = frames_in.astype(jnp.float32)
    scale = lax.rsqrt(jnp.mean(values_f * values_f, axis=-1, keepdims=True) + 1e-06)
    return (values_f * scale * norm_gain).astype(jnp.bfloat16)


def to_windows(array, count):
    shaped = array.reshape(count, HH // WIN, WIN, WW // WIN, WIN, HEADS, HD)
    shaped = shaped.transpose(0, 1, 3, 2, 4, 5, 6)
    return shaped.reshape(count, HH // WIN * (WW // WIN), WIN * WIN, HEADS, HD)


def from_windows(array, count):
    shaped = array.reshape(count, HH // WIN, WW // WIN, WIN, WIN, HEADS * HD)
    shaped = shaped.transpose(0, 1, 3, 2, 4, 5)
    return shaped.reshape(count * HH * WW, HEADS * HD)


def pooled(array, count):
    pool_rows = HH // POOL * (WW // POOL)
    shaped = array.reshape(count, HH // POOL, POOL, WW // POOL, POOL, HEADS * HD).astype(
        jnp.float32
    )
    return jnp.mean(shaped, axis=(2, 4)).reshape(count * pool_rows, HEADS * HD).astype(jnp.bfloat16)


def on_device(frames_in, frame_time, norm_gain, w_query, w_key, w_value, w_output):
    count = frames_in.shape[0] // (HH * WW)
    pool_rows = HH // POOL * (WW // POOL)
    all_frames = frame_time.shape[0]
    normed = normed_rows(frames_in, norm_gain)
    query = jnp.dot(normed, w_query, preferred_element_type=jnp.float32).astype(jnp.bfloat16)
    keys = jnp.dot(normed, w_key, preferred_element_type=jnp.float32).astype(jnp.bfloat16)
    values = jnp.dot(normed, w_value, preferred_element_type=jnp.float32).astype(jnp.bfloat16)
    pooled_keys = pooled(keys, count)
    pooled_values = pooled(values, count)
    own_time = lax.dynamic_slice_in_dim(frame_time, lax.axis_index("tm") * count, count)
    query_win = to_windows(query, count)
    factor = 1.0 / HD**0.5
    local_s = (
        jnp.einsum(
            "fnqhd,fnkhd->fnhqk",
            query_win,
            to_windows(keys, count),
            preferred_element_type=jnp.float32,
        )
        * factor
    )
    top = jnp.max(local_s, -1)
    local_w = jnp.exp(local_s - top[..., None])
    local_acc = jnp.einsum(
        "fnhqk,fnkhd->fnhqd",
        local_w.astype(jnp.bfloat16),
        to_windows(values, count),
        preferred_element_type=jnp.float32,
    )
    whole_keys, whole_values = (
        lax.all_gather(pooled_keys, "tm", axis=0, tiled=True),
        lax.all_gather(pooled_values, "tm", axis=0, tiled=True),
    )
    rows = whole_keys.shape[0]
    slot = jnp.arange(rows, dtype=jnp.int32) // pool_rows
    match = slot[:, None] == jnp.arange(all_frames, dtype=jnp.int32)[None, :]
    key_time = jnp.sum(jnp.where(match, frame_time[None, :], 0), axis=1)
    best = top
    total = jnp.sum(local_w, -1)
    acc = local_acc
    scores = (
        jnp.einsum(
            "fnqhd,khd->fnhqk",
            query_win,
            whole_keys.reshape(rows, HEADS, HD),
            preferred_element_type=jnp.float32,
        )
        * factor
    )
    valid = (key_time[None, :] < own_time[:, None])[:, None, None, None, :]
    scores = jnp.where(valid, scores, -1e30)
    new_best = jnp.maximum(best, jnp.max(scores, -1))
    keep = jnp.exp(best - new_best)
    weights = jnp.where(valid, jnp.exp(scores - new_best[..., None]), 0.0)
    total = total * keep + jnp.sum(weights, -1)
    acc = acc * keep[..., None] + jnp.einsum(
        "fnhqk,khd->fnhqd",
        weights.astype(jnp.bfloat16),
        whole_values.reshape(rows, HEADS, HD),
        preferred_element_type=jnp.float32,
    )
    final = (new_best, total, acc)
    best, total, acc = final
    mixed = (acc / total[..., None]).transpose(0, 1, 3, 2, 4).astype(jnp.bfloat16)
    mixed = from_windows(mixed, count)
    return jnp.dot(mixed, w_output, preferred_element_type=jnp.float32).astype(jnp.bfloat16)


def solution(mesh):
    placed = (P(("grp", "tm"), None), P("grp"), P(), P(), P(), P(), P())
    return jax.shard_map(
        on_device, mesh=mesh, in_specs=placed, out_specs=P(("grp", "tm"), None), check_vma=False
    )
```

profile of v0, /device:TPU:0, one launch (start us, length us, event | category | flops | bytes accessed | tf_op | source)
XLA Modules:
  0.0 85.3 jit_solution(2821864571280386767)
XLA Ops:
  0.0 0.0 copy-start
  0.0 0.9 %dynamic_slice.3 = s32[2]{0:T(128)S(1)} dynamic-slice(s32[32]{0:T(128)} %param.8, s32[]{:T(128)S(6)} %select_n.25), dynamic_slice_sizes={2} | dynamic-slice | bytes 20 | tf_op jit(solution)/shard_map/dynamic_slice | solution.py:50
  0.9 0.7 select_reduce_fusion
  1.6 0.1 broadcast_compare_fusion
  1.7 1.8 %fusion.3 = f32[512]{0:T(512)S(1)} fusion(bf16[512,1536]{1,0:T(8,128)(2,1)} %param.7), kind=kLoop, calls=%fused_computation.7 | loop fusion | flops 2358784 | bytes 1574912 | tf_op jit(solution)/shard_map/reduce_sum | solution.py:16
  3.5 3.6 %convolution_convert_fusion.2 = bf16[512,768]{1,0:T(8,128)(2,1)S(1)} fusion(bf16[1536,768]{1,0:T(8,128)(2,1)} %param.11, bf16[512,1536]{1,0:T(8,128)(2,1)} %param.7, f32[1536]{0:T(1024)} %param.9, f32[512]{0:T(512)S(1)} %add_rsqrt_fusion), kind=kOutput, calls=%fused_computation.20 | convolution fusion | flops 1211498496 | bytes 4726784 | tf_op jit(solution)/shard_map/dot_general | solution.py:46
  7.1 0.0 copy-start.3
  7.1 1.5 %reshape.124 = f32[2,4,4,4,4,768]{5,4,3,2,1,0:T(4,128)} reshape(bf16[512,768]{1,0:T(8,128)(2,1)S(1)} %convolution_convert_fusion.2) | data formatting | bytes 2359296 | tf_op jit(solution)/shard_map/convert_element_type | solution.py:34
  8.6 0.0 copy-start.9
  8.6 1.9 %reduce_sum.60 = f32[2,4,4,768]{3,2,1,0:T(4,128)S(1)} reduce(f32[2,4,4,4,4,768]{5,4,3,2,1,0:T(4,128)} %reshape.124, f32[]{:T(128)} %constant.15.clone.1), dimensions={2,4}, to_apply=%region_3.0 | reduce | flops 368640 | bytes 1671172 | tf_op jit(solution)/shard_map/reduce_sum | solution.py:37
  10.6 0.0 copy-done.3
  10.6 26.7 %all_gather.6 = bf16[512,768]{1,0:T(8,128)(2,1)} all-gather(bf16[32,768]{1,0:T(8,128)(2,1)S(1)} %convert_element_type.60), channel_id=1, replica_groups=mesh['grp'=2,'tm'=16] {'tm'}, dimensions={0}, use_global_device_ids=true | all-gather | bytes 835584 | tf_op jit(solution)/shard_map/all_gather | solution.py:71
  37.3 1.4 %copy.75 = bf16[512,768]{0,1:T(8,128)(2,1)S(1)} copy(bf16[512,768]{1,0:T(8,128)(2,1)} %all_gather.6) | data formatting | bytes 1572864 | tf_op jit(solution)/shard_map/all_gather | solution.py:71
  38.7 0.0 copy-done.9
  38.7 3.6 %convolution_convert_fusion.3 = bf16[512,768]{1,0:T(8,128)(2,1)S(1)} fusion(bf16[1536,768]{1,0:T(8,128)(2,1)} %param.10, bf16[512,1536]{1,0:T(8,128)(2,1)} %param.7, f32[1536]{0:T(1024)S(1)} %copy-done.9, f32[512]{0:T(512)S(1)} %add_rsqrt_fusion), kind=kOutput, calls=%fused_computation.21 | convolution fusion | flops 1211498496 | bytes 4726784 | tf_op jit(solution)/shard_map/dot_general | solution.py:45
  42.3 0.2 copy.70
  42.6 0.0 copy-start.4
  42.6 1.1 %fusion = (f32[2,4,6,64]{3,1,0,2:T(4,128)S(1)}, f32[6,512,2,4,64]{1,4,3,2,0:T(8,128)S(1)}) fusion(pred[2,512]{1,0:T(4,128)(4,1)S(1)} %broadcast_compare_fusion, bf16[512,6,128,1,1]{0,2,4,3,1:T(8,128)(2,1)S(1)} %bitcast.70, bf16[2,4,64,6,128]{4,2,1,0,3:T(8,128)(2,1)S(1)} %bitcast.68), kind=kOutput, calls=%fused_computation.2 | convolution fusion | flops 407368704 | bytes 7877632 | tf_op jit(solution)/shard_map/fnqhd,khd->fnhqk/dot_general | solution.py:82
  43.7 0.0 copy-done.4
  43.7 0.2 copy.71
  43.9 0.6 fusion.23
  44.5 0.0 copy-start.1
  44.6 0.0 copy-start.7
  44.6 0.0 copy-start.8
  44.6 3.1 %fusion.1 = (f32[2,4,6,64]{3,1,0,2:T(4,128)S(1)}, bf16[2,4,6,64,512]{4,3,1,0,2:T(8,128)(2,1)}) fusion(f32[6,512,2,4,64]{1,4,3,2,0:T(8,128)S(1)} %get-tuple-element.12, f32[2,4,6,64]{3,1,0,2:T(4,128)S(1)} %copy.80, pred[2,512]{1,0:T(4,128)(4,1)S(1)} %broadcast_compare_fusion), kind=kLoop, calls=%fused_computation.3 | loop fusion | flops 9434112 | bytes 9462784 | tf_op jit(solution)/shard_map/reduce_sum | solution.py:95
  47.7 0.0 copy-done.1
  47.7 0.4 fusion.10
  48.1 0.0 copy-done.7
  48.1 0.2 copy-done.8
  48.4 1.5 %convolution_convert_fusion.1 = bf16[512,768]{1,0:T(8,128)(2,1)S(1)} fusion(bf16[1536,768]{1,0:T(8,128)(2,1)S(1)} %copy-done.8, bf16[512,1536]{1,0:T(8,128)(2,1)S(1)} %copy-done.7, f32[1536]{0:T(1024)S(1)} %copy-done.9, f32[512]{0:T(512)S(1)} %add_rsqrt_fusion), kind=kOutput, calls=%fused_computation.19 | convolution fusion | flops 1211498496 | bytes 4726784 | tf_op jit(solution)/shard_map/dot_general | solution.py:47
  49.8 0.0 copy-start.5
  49.9 1.5 %reshape.125 = f32[2,4,4,4,4,768]{5,4,3,2,1,0:T(4,128)} reshape(bf16[512,768]{1,0:T(8,128)(2,1)S(1)} %convolution_convert_fusion.1) | data formatting | bytes 2359296 | tf_op jit(solution)/shard_map/convert_element_type | solution.py:34
  51.4 1.9 %reduce_sum.61 = f32[2,4,4,768]{3,2,1,0:T(4,128)S(1)} reduce(f32[2,4,4,4,4,768]{5,4,3,2,1,0:T(4,128)} %reshape.125, f32[]{:T(128)} %constant.15.clone.1), dimensions={2,4}, to_apply=%region_5.6 | reduce | flops 368640 | bytes 1671172 | tf_op jit(solution)/shard_map/reduce_sum | solution.py:37
  53.3 0.0 copy-done.5
  53.3 19.8 %all_gather.7 = bf16[512,768]{1,0:T(8,128)(2,1)S(1)} all-gather(bf16[32,768]{1,0:T(8,128)(2,1)S(1)} %convert_element_type.64), channel_id=1, replica_groups=mesh['grp'=2,'tm'=16] {'tm'}, dimensions={0}, use_global_device_ids=true | all-gather | bytes 835584 | tf_op jit(solution)/shard_map/all_gather | solution.py:72
  73.1 1.2 %copy.78 = bf16[512,768]{0,1:T(8,128)(2,1)} copy(bf16[512,768]{1,0:T(8,128)(2,1)S(1)} %all_gather.7) | data formatting | bytes 1572864 | tf_op jit(solution)/shard_map/all_gather | solution.py:72
  74.3 0.0 copy-start.6
  74.3 0.0 copy-start.2
  74.3 3.3 %fusion.6 = f32[6,128,2,4,64]{1,4,0,3,2:T(8,128)S(1)} fusion(bf16[512,6,128,1,1]{0,2,1,4,3:T(8,128)(2,1)} %bitcast.76, bf16[2,4,6,64,512]{4,3,1,0,2:T(8,128)(2,1)} %get-tuple-element.8), kind=kOutput, calls=%fused_computation.10 | convolution fusion | flops 402653184 | bytes 5505024 | tf_op jit(solution)/shard_map/fnhqk,khd->fnhqd/dot_general | solution.py:96
  77.5 0.0 copy-done.6
  77.5 0.2 copy.73
  77.8 0.0 copy-done.2
  77.8 1.5 %fusion.9 = bf16[2,4,64,6,128]{4,2,3,1,0:T(8,128)(2,1)S(1)} fusion(f32[6,128,2,4,64]{1,4,0,3,2:T(8,128)S(1)} %fusion.6, bf16[2,4,64,6,128]{4,2,3,1,0:T(8,128)(2,1)S(1)} %bitcast.75, f32[2,4,6,64,64]{3,4,2,1,0:T(8,128)S(1)} %copy-done.2, f32[2,4,64,6]{2,3,1,0:T(8,128)S(1)} %get-tuple-element.5, f32[2,4,64,6]{2,3,1,0:T(8,128)S(1)} %get-tuple-element.6, ...), kind=kOutput, calls=%fused_computation.15 | convolution fusion | flops 52297728 | bytes 3969024 | tf_op jit(solution)/shard_map/fnhqk,fnkhd->fnhqd/dot_general | solution.py:64
  79.3 0.6 copy.84
  79.8 1.8 %reshape.122 = bf16[2,2,2,8,8,768]{5,4,3,2,1,0:T(8,128)(2,1)} reshape(bf16[2,4,64,6,128]{4,3,2,1,0:T(8,128)(2,1)S(1)} %copy.84) | data formatting | bytes 1572864 | tf_op jit(solution)/shard_map/reshape | solution.py:27
  81.6 1.2 %copy.85 = bf16[2,2,8,2,8,768]{5,4,3,2,1,0:T(8,128)(2,1)S(1)} copy(bf16[2,2,8,2,8,768]{5,4,2,3,1,0:T(8,128)(2,1)} %bitcast.71) | data formatting | bytes 1572864 | tf_op jit(solution)/shard_map/transpose | solution.py:28
  82.8 0.0 copy-done
  82.8 2.5 %convolution_convert_fusion = bf16[512,1536]{1,0:T(8,128)(2,1)} fusion(bf16[512,768]{1,0:T(8,128)(2,1)S(1)} %bitcast.77, bf16[768,1536]{1,0:T(8,128)(2,1)S(1)} %copy-done), kind=kOutput, calls=%fused_computation.12 | convolution fusion | flops 1208745984 | bytes 4718592 | tf_op jit(solution)/shard_map/dot_general | solution.py:106
  (9 shorter events, 0.1 us)
Async XLA Ops:
  0.0 82.8 %copy-start = (bf16[768,1536]{1,0:T(8,128)(2,1)S(1)}, bf16[768,1536]{1,0:T(8,128)(2,1)}, u32[]{:S(2)}) copy-start(bf16[768,1536]{1,0:T(8,128)(2,1)} %param.13) | copy-start | bytes 7077892
  7.1 3.5 %copy-start.3 = (bf16[512,768]{1,0:T(8,128)(2,1)}, bf16[512,768]{1,0:T(8,128)(2,1)S(1)}, u32[]{:S(2)}) copy-start(bf16[512,768]{1,0:T(8,128)(2,1)S(1)} %convolution_convert_fusion.2) | copy-start | bytes 2359300
  8.6 30.1 %copy-start.9 = (f32[1536]{0:T(1024)S(1)}, f32[1536]{0:T(1024)}, u32[]{:S(2)}) copy-start(f32[1536]{0:T(1024)} %param.9) | copy-start | bytes 18436
  42.6 1.1 %copy-start.4 = (bf16[512,768]{1,0:T(8,128)(2,1)S(1)}, bf16[512,768]{1,0:T(8,128)(2,1)}, u32[]{:S(2)}) copy-start(bf16[512,768]{1,0:T(8,128)(2,1)} %copy-done.3) | copy-start | bytes 2359300
  44.5 3.2 %copy-start.1 = (f32[2,4,6,64,64]{3,4,2,1,0:T(8,128)}, f32[2,4,6,64,64]{3,4,2,1,0:T(8,128)S(1)}, u32[]{:S(2)}) copy-start(f32[2,4,6,64,64]{3,4,2,1,0:T(8,128)S(1)} %get-tuple-element.10) | copy-start | bytes 2359300
  44.6 3.6 %copy-start.7 = (bf16[512,1536]{1,0:T(8,128)(2,1)S(1)}, bf16[512,1536]{1,0:T(8,128)(2,1)}, u32[]{:S(2)}) copy-start(bf16[512,1536]{1,0:T(8,128)(2,1)} %param.7) | copy-start | bytes 4718596
  44.6 3.8 %copy-start.8 = (bf16[1536,768]{1,0:T(8,128)(2,1)S(1)}, bf16[1536,768]{1,0:T(8,128)(2,1)}, u32[]{:S(2)}) copy-start(bf16[1536,768]{1,0:T(8,128)(2,1)} %param.12) | copy-start | bytes 7077892
  49.8 3.5 %copy-start.5 = (bf16[512,768]{1,0:T(8,128)(2,1)}, bf16[512,768]{1,0:T(8,128)(2,1)S(1)}, u32[]{:S(2)}) copy-start(bf16[512,768]{1,0:T(8,128)(2,1)S(1)} %convolution_convert_fusion.1) | copy-start | bytes 2359300
  74.3 3.3 %copy-start.6 = (bf16[512,768]{1,0:T(8,128)(2,1)S(1)}, bf16[512,768]{1,0:T(8,128)(2,1)}, u32[]{:S(2)}) copy-start(bf16[512,768]{1,0:T(8,128)(2,1)} %copy-done.5) | copy-start | bytes 2359300
  74.3 3.5 %copy-start.2 = (f32[2,4,6,64,64]{3,4,2,1,0:T(8,128)S(1)}, f32[2,4,6,64,64]{3,4,2,1,0:T(8,128)}, u32[]{:S(2)}) copy-start(f32[2,4,6,64,64]{3,4,2,1,0:T(8,128)} %copy-done.1) | copy-start | bytes 2359300
where the time goes:
time: 85.7 us; the launch traced here: 85.3 us
  blocking collectives  46.5 us (54%)
  matrix products  17.6 us (21%)
  local copies, waits for them, and re-layouts  11 us (13%)
  other arithmetic  9.99 us (12%)
    all_gather x1, blocking collectives, on_device(): lax.all_gather(pooled_keys, 'tm', axis=0, tiled=True)  26.7 us
    all_gather x1, blocking collectives, on_device(): lax.all_gather(pooled_values, 'tm', axis=0, tiled=True)  19.8 us
    reduce_sum x2, other arithmetic, pooled(): jnp.mean(shaped, axis=(2, 4)).reshape(count * pool_rows, HEADS * HD)  3.78 us
    dot_general x1, matrix products, on_device(): jnp.dot(normed, w_key, preferred_element_type=jnp.float32)  3.6 us
    dot_general x1, matrix products, on_device(): jnp.dot(normed, w_query, preferred_element_type=jnp.float32)  3.59 us
    dot_general x1, matrix products, on_device(): jnp.einsum('fnhqk,khd->fnhqd', weights.astype(jnp.bfloat16), whole_values...  3.25 us
    reduce_sum x1, other arithmetic, on_device(): total = total * keep + jnp.sum(weights, -1)  3.13 us
    convert_element_type x2, local copies, waits for them, and re-layouts, pooled(): array.reshape(count, HH // POOL, POOL, WW // POOL, POOL, HEADS * HD)  3.03 us

commit v1 on v0

v1 whole, which is shorter than its diff:
```python
import functools
import math

import jax
import jax.numpy as jnp
from jax import lax
from jax.experimental import pallas as pl
from jax.experimental.pallas import tpu as pltpu
from jax.sharding import PartitionSpec as P

HEADS = 6
HD = 128
HH = 16
WW = 16
WIN = 8
POOL = 4
TOKENS = HH * WW
SLOTS = TOKENS // (POOL * POOL)
FAR = -1e30
SCALE = HD**-0.5 * math.log2(math.e)
F32 = jnp.float32
BF16 = jnp.bfloat16
VMEM = pl.BlockSpec(memory_space=pltpu.VMEM)
SMEM = pl.BlockSpec(memory_space=pltpu.SMEM)
HBM = pl.BlockSpec(memory_space=pl.ANY)


def exchange_plan(n):
    high = [1 << b for b in range(n.bit_length() - 2, 0, -1)]
    first = [high[0]] + high[2:] + high[1:2]
    second = high[1:2] + high[:1] + high[2:]
    held = [[0], [0]]
    for a, b in zip(first, second):
        held = [held[0] + [m ^ a for m in held[0]], held[1] + [m ^ b for m in held[1]]]
    return list(zip(first, second)), held


def norm_kernel(frames_hbm, gain_ref, wk_hbm, wv_hbm, normed_ref, pooled_ref, x_buf, wk_buf, wv_buf, x_sem, w_sem):
    rows, width = x_buf.shape
    parts = x_sem.shape[0]
    step = rows // parts
    loads = [
        pltpu.make_async_copy(frames_hbm.at[pl.ds(i * step, step)], x_buf.at[pl.ds(i * step, step)], x_sem.at[i])
        for i in range(parts)
    ]
    weights = [
        pltpu.make_async_copy(wk_hbm, wk_buf, w_sem.at[0]),
        pltpu.make_async_copy(wv_hbm, wv_buf, w_sem.at[1]),
    ]
    for copy in loads + weights:
        copy.start()
    gain = gain_ref[...]
    pair = 2 * WW
    per_window = WIN * WIN
    for i in range(parts):
        loads[i].wait()
        for g in range(i * step // pair, (i + 1) * step // pair):
            x = x_buf[pl.ds(g * pair, pair), :].astype(F32)
            scale = lax.rsqrt(jnp.mean(x * x, axis=-1, keepdims=True) + 1e-06)
            y = x * scale * gain
            frame, row = divmod(2 * g, HH)
            wr, r = divmod(row, WIN)
            for wc in range(WW // WIN):
                both = jnp.concatenate(
                    [y[wc * WIN : (wc + 1) * WIN], y[WW + wc * WIN : WW + (wc + 1) * WIN]], axis=0
                )
                base = frame * TOKENS + (wr * (WW // WIN) + wc) * per_window + r * WIN
                normed_ref[pl.ds(base, 2 * WIN), :] = both.astype(BF16)
    count = rows // TOKENS
    out_rows = count * SLOTS
    slot = lax.broadcasted_iota(jnp.int32, (out_rows, rows), 0)
    token = lax.broadcasted_iota(jnp.int32, (out_rows, rows), 1)
    r, c = token % per_window // WIN, token % WIN
    home = token // per_window * 4 + r // POOL * 2 + c // POOL
    pick = jnp.where(home == slot, 1.0 / (POOL * POOL), 0.0).astype(BF16)
    mean = jnp.dot(pick, normed_ref[...], preferred_element_type=F32)
    high = mean.astype(BF16)
    low = (mean - high.astype(F32)).astype(BF16)
    both = jnp.concatenate([high, low], axis=0)
    for i, buf in enumerate((wk_buf, wv_buf)):
        weights[i].wait()
        z = jnp.dot(both, buf[...], preferred_element_type=F32)
        cols = HEADS * HD
        pooled_ref[:, i * cols : (i + 1) * cols] = (z[:out_rows] + z[out_rows:]).astype(BF16)


def norm_and_pool(frames, gain, w_key, w_value):
    rows, width = frames.shape
    out_rows = rows // TOKENS * SLOTS
    cols = HEADS * HD
    return pl.pallas_call(
        norm_kernel,
        out_shape=(
            jax.ShapeDtypeStruct((rows, width), BF16),
            jax.ShapeDtypeStruct((out_rows, 2 * cols), BF16),
        ),
        in_specs=[HBM, VMEM, HBM, HBM],
        out_specs=(VMEM, VMEM),
        scratch_shapes=[
            pltpu.VMEM((rows, width), BF16),
            pltpu.VMEM((width, cols), BF16),
            pltpu.VMEM((width, cols), BF16),
            pltpu.SemaphoreType.DMA((4,)),
            pltpu.SemaphoreType.DMA((2,)),
        ],
        compiler_params=pltpu.CompilerParams(vmem_limit_bytes=24 << 20),
        cost_estimate=pl.CostEstimate(flops=400_000_000, bytes_accessed=8_000_000, transcendentals=0),
        name="norm_and_pool",
    )(frames, gain.reshape(1, width), w_key, w_value)


def own_block(me, mask_pair):
    a, b = mask_pair
    return me ^ (a if a == b else jnp.where(me % 2 == 0, a, b))


def mask_columns(time_ref, masks, count):
    me = lax.axis_index("tm")
    lane = lax.broadcasted_iota(jnp.int32, (SLOTS, HD), 1)
    own = [time_ref[me * count + f] for f in range(count)]
    tiles = []
    for pair in masks:
        source = own_block(me, pair)
        for g in range(count):
            t = time_ref[source * count + g]
            tile = jnp.zeros((SLOTS, HD), F32)
            for f in range(count):
                tile = jnp.where(lane == f, jnp.where(t < own[f], 0.0, FAR), tile)
            tiles.append(tile)
    return jnp.concatenate(tiles, axis=0).astype(BF16)


def frame_columns(tokens):
    frame = lax.broadcasted_iota(jnp.int32, (tokens, HD), 0) // TOKENS
    lane = lax.broadcasted_iota(jnp.int32, (tokens, HD), 1)
    return jnp.where(frame == lane, 1.0, 0.0).astype(BF16)


def dot_nt(a, b):
    return lax.dot_general(a, b, (((1,), (1,)), ((), ())), preferred_element_type=F32)


def dot_tn(a, b):
    return lax.dot_general(a, b, (((0,), (0,)), ((), ())), preferred_element_type=F32)


def head(h, base=0):
    return slice(base + h * HD, base + (h + 1) * HD)


def first_kernel(masks, time_ref, q_ref, k_ref, v_ref, near_ref, other_ref, acc_ref, m_ref, l_ref):
    tokens = q_ref.shape[0]
    count = tokens // TOKENS
    per_window = WIN * WIN
    cols = HEADS * HD
    bias = mask_columns(time_ref, masks, count)
    frames = frame_columns(tokens)
    left = lax.broadcasted_iota(jnp.int32, (per_window, 2 * per_window), 1) < per_window
    for h in range(HEADS):
        q = q_ref[:, head(h)]
        far_k = jnp.concatenate([near_ref[:, head(h)], other_ref[:, head(h)]], axis=0)
        far_v = jnp.concatenate([near_ref[:, head(h, cols)], other_ref[:, head(h, cols)]], axis=0)
        far_s = dot_nt(jnp.concatenate([far_k, bias], axis=1), jnp.concatenate([q, frames], axis=1))
        parts = []
        for w in range(tokens // (2 * per_window)):
            two = pl.ds(w * 2 * per_window, 2 * per_window)
            s = dot_nt(k_ref[two, head(h)], q_ref[two, head(h)])
            parts.append(jnp.where(left, s[:per_window], s[per_window:]))
        local_s = jnp.concatenate(parts, axis=1)
        top = jnp.maximum(jnp.max(local_s, axis=0, keepdims=True), jnp.max(far_s, axis=0, keepdims=True))
        local_w = jnp.exp2((local_s - top) * SCALE)
        far_w = jnp.exp2((far_s - top) * SCALE)
        total = jnp.sum(local_w, axis=0, keepdims=True) + jnp.sum(far_w, axis=0, keepdims=True)
        acc = dot_tn(far_v, far_w.astype(BF16))
        parts = []
        for w in range(tokens // (2 * per_window)):
            two = pl.ds(w * 2 * per_window, 2 * per_window)
            p = local_w[:, w * 2 * per_window : (w + 1) * 2 * per_window]
            p = jnp.concatenate([jnp.where(left, p, 0.0), jnp.where(left, 0.0, p)], axis=0).astype(BF16)
            parts.append(dot_tn(v_ref[two, head(h)], p))
        acc_ref[head(h), :] = acc + jnp.concatenate(parts, axis=1)
        m_ref[h : h + 1, :] = top
        l_ref[h : h + 1, :] = total


def far_step(h, q_ref, far_ref, bias, frames, m, l, acc):
    cols = HEADS * HD
    s = dot_nt(
        jnp.concatenate([far_ref[:, head(h)], bias], axis=1),
        jnp.concatenate([q_ref[:, head(h)], frames], axis=1),
    )
    top = jnp.maximum(m, jnp.max(s, axis=0, keepdims=True))
    w = jnp.exp2((s - top) * SCALE)
    keep = jnp.exp2((m - top) * SCALE)
    l = l * keep + jnp.sum(w, axis=0, keepdims=True)
    acc = acc * keep + dot_tn(far_ref[:, head(h, cols)], w.astype(BF16))
    return top, l, acc


def middle_kernel(masks, time_ref, q_ref, far_ref, acc_in, m_in, l_in, acc_ref, m_ref, l_ref):
    tokens = q_ref.shape[0]
    bias = mask_columns(time_ref, masks, tokens // TOKENS)
    frames = frame_columns(tokens)
    for h in range(HEADS):
        m, l, acc = far_step(
            h, q_ref, far_ref, bias, frames, m_in[h : h + 1, :], l_in[h : h + 1, :], acc_in[head(h), :]
        )
        acc_ref[head(h), :] = acc
        m_ref[h : h + 1, :] = m
        l_ref[h : h + 1, :] = l


def last_kernel(masks, time_ref, q_ref, far_ref, acc_in, m_in, l_in, wo_ref, out_ref, mixed, rows_buf):
    tokens = q_ref.shape[0]
    bias = mask_columns(time_ref, masks, tokens // TOKENS)
    frames = frame_columns(tokens)
    for h in range(HEADS):
        m, l, acc = far_step(
            h, q_ref, far_ref, bias, frames, m_in[h : h + 1, :], l_in[h : h + 1, :], acc_in[head(h), :]
        )
        mixed[:, head(h)] = jnp.transpose(acc * (1.0 / l))
    per_window = WIN * WIN
    for row in range(tokens // WW):
        frame, rest = divmod(row, HH)
        wr, r = divmod(rest, WIN)
        base = frame * TOKENS + wr * (WW // WIN) * per_window + r * WIN
        line = jnp.concatenate([mixed[pl.ds(base + wc * per_window, WIN), :] for wc in range(WW // WIN)], axis=0)
        rows_buf[pl.ds(row * WW, WW), :] = line.astype(BF16)
    out_ref[...] = jnp.dot(rows_buf[...], wo_ref[...], preferred_element_type=F32).astype(BF16)


def on_device(n, frames_in, frame_time, norm_gain, w_query, w_key, w_value, w_output):
    rows = frames_in.shape[0]
    cols = HEADS * HD
    phases, held = exchange_plan(n)
    normed, block = norm_and_pool(frames_in, norm_gain, w_key, w_value)

    def send(x, pair):
        return lax.ppermute(x, "tm", [(i, i ^ pair[i % 2]) for i in range(n)])

    for pair in phases[:-1]:
        block = jnp.concatenate([block, send(block, pair)], axis=0)
    late = send(block, phases[-1])
    other = send(block, (1, 1))
    other_late = send(late, (1, 1))
    half = len(held[0]) // 2
    own = list(zip(held[0], held[1]))
    far = [(a ^ 1, b ^ 1) for b, a in own]

    query, keys, values = (
        jnp.dot(normed, w, preferred_element_type=F32).astype(BF16) for w in (w_query, w_key, w_value)
    )
    state = (
        jax.ShapeDtypeStruct((cols, rows), F32),
        jax.ShapeDtypeStruct((8, rows), F32),
        jax.ShapeDtypeStruct((8, rows), F32),
    )
    params = pltpu.CompilerParams(vmem_limit_bytes=32 << 20)
    acc, m, l = pl.pallas_call(
        functools.partial(first_kernel, own[:half] + far[:half]),
        out_shape=state,
        in_specs=[SMEM] + [VMEM] * 5,
        out_specs=(VMEM, VMEM, VMEM),
        compiler_params=params,
        cost_estimate=pl.CostEstimate(flops=900_000_000, bytes_accessed=5_000_000, transcendentals=1_000_000),
        name="local_and_first",
    )(frame_time, query, keys, values, block, other)
    acc, m, l = pl.pallas_call(
        functools.partial(middle_kernel, own[half:]),
        out_shape=state,
        in_specs=[SMEM] + [VMEM] * 5,
        out_specs=(VMEM, VMEM, VMEM),
        input_output_aliases={3: 0, 4: 1, 5: 2},
        compiler_params=params,
        cost_estimate=pl.CostEstimate(flops=500_000_000, bytes_accessed=5_000_000, transcendentals=400_000),
        name="middle",
    )(frame_time, query, late, acc, m, l)
    return pl.pallas_call(
        functools.partial(last_kernel, far[half:]),
        out_shape=jax.ShapeDtypeStruct((rows, w_output.shape[1]), BF16),
        in_specs=[SMEM] + [VMEM] * 6,
        out_specs=VMEM,
        scratch_shapes=[pltpu.VMEM((rows, cols), F32), pltpu.VMEM((rows, cols), BF16)],
        compiler_params=params,
        cost_estimate=pl.CostEstimate(flops=1_700_000_000, bytes_accessed=8_000_000, transcendentals=400_000),
        name="last_and_output",
    )(frame_time, query, other_late, acc, m, l, w_output)


def solution(mesh):
    placed = (P(("grp", "tm"), None), P("grp"), P(), P(), P(), P(), P())
    return jax.shard_map(
        functools.partial(on_device, mesh.shape["tm"]),
        mesh=mesh,
        in_specs=placed,
        out_specs=P(("grp", "tm"), None),
        check_vma=False,
    )
```

time: 85.7 us -> 42.3 us (0.49)
  blocking collectives: 46.5 us -> 0 us
  Pallas kernels: 0 us -> 14.2 us
  matrix products: 17.6 us -> 4.14 us
  other arithmetic: 9.99 us -> 0.01 us
  waiting for transfers between devices: 0 us -> 9.25 us
  starting transfers between devices: 0 us -> 8.25 us
  local copies, waits for them, and re-layouts: 11 us -> 5.63 us
    all_gather x2 -> x0, blocking collectives: 46.5 us -> none  [the longest x1 26.7 us: on_device(): lax.all_gather(pooled_keys, 'tm', axis=0, tiled=True)]
    pallas_call x0 -> x4, Pallas kernels: none -> 14.2 us  [the longest x1 4.92 us: on_device(): pl.pallas_call(functools.partial(last_kernel, far[half:]), out_shape=jax....]
    dot_general x8 -> x3, matrix products: 17.6 us -> 4.14 us  [on_device(): jnp.dot(normed, w, preferred_element_type=F32).astype(BF16)]
    reduce_sum x6 -> x0, other arithmetic: 9.82 us -> none  [the longest x2 3.78 us: pooled(): jnp.mean(shaped, axis=(2, 4)).reshape(count * pool_rows, HEADS * HD)]
    ppermute x0 -> x5, waiting for transfers between devices: none -> 9.25 us  [send(): return lax.ppermute(x, 'tm', [(i, i ^ pair[i % 2]) for i in range(n)])]
    ppermute x0 -> x5, starting transfers between devices: none -> 8.25 us  [send(): return lax.ppermute(x, 'tm', [(i, i ^ pair[i % 2]) for i in range(n)])]
    unnamed x20 -> x14, local copies, waits for them, and re-layouts: 0.31 us -> 4.77 us
    convert_element_type x5 -> x0, local copies, waits for them, and re-layouts: 3.62 us -> none  [the longest x2 3.03 us: pooled(): array.reshape(count, HH // POOL, POOL, WW // POOL, POOL, HEADS * HD)]
  transfers between devices with their start and end apart: 0 -> 5, of which waited for: 0 -> 3; matrix products, arithmetic and copies ran while one was open for 0% -> 10% of each run, Pallas kernels for 0% -> 14%
where the time goes in v1:
time: 42.3 us; the launch traced here: 41.6 us
  Pallas kernels  14.2 us (34%)
  waiting for transfers between devices  9.25 us (22%)
  starting transfers between devices  8.25 us (20%)
  local copies, waits for them, and re-layouts  5.63 us (13%)
  matrix products  4.14 us (10%)
    ppermute x5, waiting for transfers between devices, send(): return lax.ppermute(x, 'tm', [(i, i ^ pair[i % 2]) for i in range(n)])  9.25 us
    ppermute x5, starting transfers between devices, send(): return lax.ppermute(x, 'tm', [(i, i ^ pair[i % 2]) for i in range(n)])  8.25 us
    pallas_call x1, Pallas kernels, on_device(): pl.pallas_call(functools.partial(last_kernel, far[half:]), out_shape=jax....  4.92 us
    unnamed x14, local copies, waits for them, and re-layouts  4.77 us
    dot_general x3, matrix products, on_device(): jnp.dot(normed, w, preferred_element_type=F32).astype(BF16)  4.14 us
    pallas_call x1, Pallas kernels, norm_and_pool(): pl.pallas_call(norm_kernel, out_shape=(jax.ShapeDtypeStruct((rows, width)...  3.39 us
    pallas_call x1, Pallas kernels, on_device(): pl.pallas_call(functools.partial(first_kernel, own[:half] + far[:half]),...  3.36 us
    pallas_call x1, Pallas kernels, on_device(): pl.pallas_call(functools.partial(middle_kernel, own[half:]), out_shape=st...  2.56 us
  transfers between devices with their start and end apart: 5, of which 3 were waited for; matrix products, arithmetic and copies ran while one was open for 10% of the time, Pallas kernels for 14%

profile of v1, /device:TPU:0, one launch (start us, length us, event | category | flops | bytes accessed | tf_op | source)
XLA Modules:
  0.0 41.6 jit_solution(15026666864796642907)
XLA Ops:
  0.0 0.0 copy-start
  0.0 0.9 %reshape.3.gain_ref = f32[1,1536]{1,0:T(1,128)S(1)} reshape(f32[1536]{0:T(1024)} %param.9) | data formatting | bytes 12288 | tf_op jit(solution)/shard_map/reshape | solution.py:109
  0.9 0.0 copy-start.1
  0.9 1.7 %copy-done.1 = bf16[1536,768]{1,0:T(8,128)(2,1)S(1)} copy-done((bf16[1536,768]{1,0:T(8,128)(2,1)S(1)}, bf16[1536,768]{1,0:T(8,128)(2,1)}, u32[]{:S(2)}) %copy-start.1) | copy-done | bytes 2359320
  2.5 0.0 copy-start.2
  2.5 1.7 %copy-done.2 = bf16[1536,768]{1,0:T(8,128)(2,1)S(1)} copy-done((bf16[1536,768]{1,0:T(8,128)(2,1)S(1)}, bf16[1536,768]{1,0:T(8,128)(2,1)}, u32[]{:S(2)}) %copy-start.2) | copy-done | bytes 2359320
  4.2 0.0 copy-start.4
  4.2 1.4 %copy-done.4 = bf16[512,1536]{1,0:T(8,128)(2,1)S(1)} copy-done((bf16[512,1536]{1,0:T(8,128)(2,1)S(1)}, bf16[512,1536]{1,0:T(8,128)(2,1)}, u32[]{:S(2)}) %copy-start.4) | copy-done | bytes 1572888
  5.6 3.4 %norm_and_pool.1 = (bf16[512,1536]{1,0:T(8,128)(2,1)S(1)}, bf16[32,1536]{1,0:T(8,128)(2,1)S(1)}) custom-call(bf16[512,1536]{1,0:T(8,128)(2,1)S(1)} %copy-done.4, f32[1,1536]{1,0:T(1,128)S(1)} %reshape.3.gain_ref, bf16[1536,768]{1,0:T(8,128)(2,1)S(1)} %copy-done.2, bf16[1536,768]{1,0:T(8,128)(2,1)S(1)} %copy-done.1), custom_call_target="tpu_custom_call" | custom-call | flops 400000000 | bytes 8000000 | tf_op jit(solution)/shard_map/norm_and_pool/pallas_call | solution.py:91
  9.0 4.1 %collective-permute-start = (bf16[32,1536]{1,0:T(8,128)(2,1)S(1)}, bf16[32,1536]{1,0:T(8,128)(2,1)S(1)}, u32[]{:S(2)}, u32[]{:S(2)}) collective-permute-start(bf16[32,1536]{1,0:T(8,128)(2,1)S(1)} %get-tuple-element.14), channel_id=1, source_target_pairs={{0,8},{1,5},{2,10},{3,7},{4,12},{5,1},{6,14},{7,3},{8,0},{9,13},{1... | collective-permute-start | bytes 294920 | tf_op jit(solution)/shard_map/ppermute | solution.py:239
  13.1 1.4 %convolution_convert_fusion.v_ref = bf16[512,768]{1,0:T(8,128)(2,1)S(1)} fusion(bf16[512,1536]{1,0:T(8,128)(2,1)S(1)} %get-tuple-element.13, bf16[1536,768]{1,0:T(8,128)(2,1)S(1)} %copy-done.1), kind=kOutput, calls=%fused_computation | convolution fusion | flops 1208352768 | bytes 4718592 | tf_op jit(solution)/shard_map/dot_general | solution.py:251
  14.5 1.2 %collective-permute-done = bf16[32,1536]{1,0:T(8,128)(2,1)S(1)} collective-permute-done((bf16[32,1536]{1,0:T(8,128)(2,1)S(1)}, bf16[32,1536]{1,0:T(8,128)(2,1)S(1)}, u32[]{:S(2)}, u32[]{:S(2)}) %collective-permute-start) | collective-permute-done | bytes 98336 | tf_op jit(solution)/shard_map/ppermute | solution.py:239
  15.7 2.0 %collective-permute-start.1 = (bf16[64,1536]{1,0:T(8,128)(2,1)S(1)}, bf16[64,1536]{1,0:T(8,128)(2,1)S(1)}, u32[]{:S(2)}, u32[]{:S(2)}) collective-permute-start(bf16[64,1536]{1,0:T(8,128)(2,1)S(1)} %pad_maximum_fusion), channel_id=1, source_target_pairs={{0,2},{1,9},{2,0},{3,11},{4,6},{5,13},{6,4},{7,15},{8,10},{9,1},{1... | collective-permute-start | bytes 589832 | tf_op jit(solution)/shard_map/ppermute | solution.py:239
  17.7 3.8 %collective-permute-done.1 = bf16[64,1536]{1,0:T(8,128)(2,1)S(1)} collective-permute-done((bf16[64,1536]{1,0:T(8,128)(2,1)S(1)}, bf16[64,1536]{1,0:T(8,128)(2,1)S(1)}, u32[]{:S(2)}, u32[]{:S(2)}) %collective-permute-start.1) | collective-permute-done | bytes 196640 | tf_op jit(solution)/shard_map/ppermute | solution.py:239
  21.5 2.1 %collective-permute-start.2 = (bf16[128,1536]{1,0:T(8,128)(2,1)S(1)}, bf16[128,1536]{1,0:T(8,128)(2,1)S(1)}, u32[]{:S(2)}, u32[]{:S(2)}) collective-permute-start(bf16[128,1536]{1,0:T(8,128)(2,1)S(1)} %constant_dynamic-update-slice_fusion.near_ref), channel_id=1, source_target_pairs={{0,4},{1,3},{2,6},{3,1},{4,0},{5,7},{6,2},{7,5},{8,12},{9,11},{10,... | collective-permute-start | bytes 1179656 | tf_op jit(solution)/shard_map/ppermute | solution.py:239
  23.6 1.4 %convolution_convert_fusion.1.k_ref = bf16[512,768]{1,0:T(8,128)(2,1)S(1)} fusion(bf16[512,1536]{1,0:T(8,128)(2,1)S(1)} %get-tuple-element.13, bf16[1536,768]{1,0:T(8,128)(2,1)S(1)} %copy-done.2), kind=kOutput, calls=%fused_computation.1 | convolution fusion | flops 1208352768 | bytes 4718592 | tf_op jit(solution)/shard_map/dot_general | solution.py:251
  25.0 0.0 copy-start.5
  25.0 0.1 collective-permute-start.4
  25.1 4.3 %collective-permute-done.2.far_ref = bf16[128,1536]{1,0:T(8,128)(2,1)S(1)} collective-permute-done((bf16[128,1536]{1,0:T(8,128)(2,1)S(1)}, bf16[128,1536]{1,0:T(8,128)(2,1)S(1)}, u32[]{:S(2)}, u32[]{:S(2)}) %collective-permute-start.2) | collective-permute-done | bytes 393248 | tf_op jit(solution)/shard_map/ppermute | solution.py:239
  29.3 0.0 collective-permute-start.3
  29.3 0.0 copy-done
  29.3 1.4 %convolution_convert_fusion.2.q_ref = bf16[512,768]{1,0:T(8,128)(2,1)S(1)} fusion(bf16[512,1536]{1,0:T(8,128)(2,1)S(1)} %get-tuple-element.13, bf16[1536,768]{1,0:T(8,128)(2,1)S(1)} %copy-done), kind=kOutput, calls=%fused_computation.2 | convolution fusion | flops 1208352768 | bytes 4718592 | tf_op jit(solution)/shard_map/dot_general | solution.py:251
  30.7 0.0 collective-permute-done.4.other_ref
  30.7 0.0 copy-done.5
  30.8 3.4 %local_and_first.1 = (f32[768,512]{1,0:T(8,128)S(1)}, f32[8,512]{1,0:T(8,128)S(1)}, f32[8,512]{1,0:T(8,128)S(1)}) custom-call(s32[32]{0:T(128)S(1)} %copy-done.5, bf16[512,768]{1,0:T(8,128)(2,1)S(1)} %convolution_convert_fusion.2.q_ref, bf16[512,768]{1,0:T(8,128)(2,1)S(1)} %convolution_convert_fusion.1.k_ref, ...), custom_call_target="tpu_custom_call" | custom-call | flops 900000000 | bytes 5000000 | tf_op jit(solution)/shard_map/local_and_first/pallas_call | solution.py:259
  34.1 0.0 copy-start.3
  34.1 2.6 %middle.1 = (f32[768,512]{1,0:T(8,128)S(1)}, f32[8,512]{1,0:T(8,128)S(1)}, f32[8,512]{1,0:T(8,128)S(1)}) custom-call(s32[32]{0:T(128)S(1)} %copy-done.5, bf16[512,768]{1,0:T(8,128)(2,1)S(1)} %convolution_convert_fusion.2.q_ref, bf16[128,1536]{1,0:T(8,128)(2,1)S(1)} %collective-permute-done.2.far_ref, ...), custom_call_target="tpu_custom_call", output_to_operand_aliasing={{0}: (3, {}), {1}: (4, {}), {2}: (5, {})} | custom-call | flops 500000000 | bytes 5000000 | tf_op jit(solution)/shard_map/middle/pallas_call | solution.py:268
  36.7 0.0 collective-permute-done.3.far_ref
  36.7 0.0 copy-done.3
  36.7 4.9 %last_and_output.1 = bf16[512,1536]{1,0:T(8,128)(2,1)} custom-call(s32[32]{0:T(128)S(1)} %copy-done.5, bf16[512,768]{1,0:T(8,128)(2,1)S(1)} %convolution_convert_fusion.2.q_ref, bf16[128,1536]{1,0:T(8,128)(2,1)S(1)} %collective-permute-done.3.far_ref, f32[768,512]{1,0:T(8,128)S(1)} %get-tuple-element.18.acc_in, f32[8,512]{1,0:T(8,128)S(1)} %get-tuple-element.19.m_in, ...), custom_call_target="tpu_custom_call" | custom-call | flops 1700000000 | bytes 8000000 | tf_op jit(solution)/shard_map/last_and_output/pallas_call | solution.py:278
  (4 shorter events, 0.0 us)
Async XLA Ops:
  0.0 29.3 %copy-start = (bf16[1536,768]{1,0:T(8,128)(2,1)S(1)}, bf16[1536,768]{1,0:T(8,128)(2,1)}, u32[]{:S(2)}) copy-start(bf16[1536,768]{1,0:T(8,128)(2,1)} %param.10) | copy-start | bytes 7077892
  0.9 1.7 %copy-start.1 = (bf16[1536,768]{1,0:T(8,128)(2,1)S(1)}, bf16[1536,768]{1,0:T(8,128)(2,1)}, u32[]{:S(2)}) copy-start(bf16[1536,768]{1,0:T(8,128)(2,1)} %wv_hbm.1) | copy-start | bytes 7077892
  2.5 1.7 %copy-start.2 = (bf16[1536,768]{1,0:T(8,128)(2,1)S(1)}, bf16[1536,768]{1,0:T(8,128)(2,1)}, u32[]{:S(2)}) copy-start(bf16[1536,768]{1,0:T(8,128)(2,1)} %wk_hbm.1) | copy-start | bytes 7077892
  4.2 1.4 %copy-start.4 = (bf16[512,1536]{1,0:T(8,128)(2,1)S(1)}, bf16[512,1536]{1,0:T(8,128)(2,1)}, u32[]{:S(2)}) copy-start(bf16[512,1536]{1,0:T(8,128)(2,1)} %frames_hbm.1) | copy-start | bytes 4718596
  9.0 6.7 %collective-permute-start = (bf16[32,1536]{1,0:T(8,128)(2,1)S(1)}, bf16[32,1536]{1,0:T(8,128)(2,1)S(1)}, u32[]{:S(2)}, u32[]{:S(2)}) collective-permute-start(bf16[32,1536]{1,0:T(8,128)(2,1)S(1)} %get-tuple-element.14), channel_id=1, source_target_pairs={{0,8},{1,5},{2,10},{3,7},{4,12},{5,1},{6,14},{7,3},{8,0},{9,13},{1... | collective-permute-start | bytes 294920 | tf_op jit(solution)/shard_map/ppermute | solution.py:239
  15.7 5.7 %collective-permute-start.1 = (bf16[64,1536]{1,0:T(8,128)(2,1)S(1)}, bf16[64,1536]{1,0:T(8,128)(2,1)S(1)}, u32[]{:S(2)}, u32[]{:S(2)}) collective-permute-start(bf16[64,1536]{1,0:T(8,128)(2,1)S(1)} %pad_maximum_fusion), channel_id=1, source_target_pairs={{0,2},{1,9},{2,0},{3,11},{4,6},{5,13},{6,4},{7,15},{8,10},{9,1},{1... | collective-permute-start | bytes 589832 | tf_op jit(solution)/shard_map/ppermute | solution.py:239
  21.5 7.9 %collective-permute-start.2 = (bf16[128,1536]{1,0:T(8,128)(2,1)S(1)}, bf16[128,1536]{1,0:T(8,128)(2,1)S(1)}, u32[]{:S(2)}, u32[]{:S(2)}) collective-permute-start(bf16[128,1536]{1,0:T(8,128)(2,1)S(1)} %constant_dynamic-update-slice_fusion.near_ref), channel_id=1, source_target_pairs={{0,4},{1,3},{2,6},{3,1},{4,0},{5,7},{6,2},{7,5},{8,12},{9,11},{10,... | collective-permute-start | bytes 1179656 | tf_op jit(solution)/shard_map/ppermute | solution.py:239
  25.0 5.8 %copy-start.5 = (s32[32]{0:T(128)S(1)}, s32[32]{0:T(128)}, u32[]{:S(2)}) copy-start(s32[32]{0:T(128)} %time_ref.5) | copy-start | bytes 388
  25.0 5.8 %collective-permute-start.4 = (bf16[128,1536]{1,0:T(8,128)(2,1)S(1)}, bf16[128,1536]{1,0:T(8,128)(2,1)S(1)}, u32[]{:S(2)}, u32[]{:S(2)}) collective-permute-start(bf16[128,1536]{1,0:T(8,128)(2,1)S(1)} %constant_dynamic-update-slice_fusion.near_ref), channel_id=1, source_target_pairs={{0,1},{1,0},{2,3},{3,2},{4,5},{5,4},{6,7},{7,6},{8,9},{9,8},{10,11... | collective-permute-start | bytes 1179656 | tf_op jit(solution)/shard_map/ppermute | solution.py:239
  29.3 7.4 %collective-permute-start.3 = (bf16[128,1536]{1,0:T(8,128)(2,1)S(1)}, bf16[128,1536]{1,0:T(8,128)(2,1)S(1)}, u32[]{:S(2)}, u32[]{:S(2)}) collective-permute-start(bf16[128,1536]{1,0:T(8,128)(2,1)S(1)} %collective-permute-done.2.far_ref), channel_id=1, source_target_pairs={{0,1},{1,0},{2,3},{3,2},{4,5},{5,4},{6,7},{7,6},{8,9},{9,8},{10,11... | collective-permute-start | bytes 1179656 | tf_op jit(solution)/shard_map/ppermute | solution.py:239
  34.1 2.6 %copy-start.3 = (bf16[768,1536]{1,0:T(8,128)(2,1)S(1)}, bf16[768,1536]{1,0:T(8,128)(2,1)}, u32[]{:S(2)}) copy-start(bf16[768,1536]{1,0:T(8,128)(2,1)} %wo_ref.1) | copy-start | bytes 7077892

commit v2 on v1

--- a/solution.py
+++ b/solution.py
@@ -35,21 +35,34 @@
     return list(zip(first, second)), held
 
 
-def norm_kernel(frames_hbm, gain_ref, wk_hbm, wv_hbm, normed_ref, pooled_ref, x_buf, wk_buf, wv_buf, x_sem, w_sem):
+def norm_kernel(
+    frames_hbm, gain_hbm, wk_hbm, wv_hbm, normed_ref, pooled_ref, x_buf, gain_buf, wk_buf, wv_buf, x_sem, g_sem, w_sem
+):
     rows, width = x_buf.shape
     parts = x_sem.shape[0]
     step = rows // parts
+    slabs = w_sem.shape[1]
+    deep = width // slabs
+    gain_load = pltpu.make_async_copy(gain_hbm, gain_buf.at[0], g_sem)
     loads = [
         pltpu.make_async_copy(frames_hbm.at[pl.ds(i * step, step)], x_buf.at[pl.ds(i * step, step)], x_sem.at[i])
         for i in range(parts)
     ]
     weights = [
-        pltpu.make_async_copy(wk_hbm, wk_buf, w_sem.at[0]),
-        pltpu.make_async_copy(wv_hbm, wv_buf, w_sem.at[1]),
+        [
+            pltpu.make_async_copy(w.at[pl.ds(j * deep, deep)], buf.at[pl.ds(j * deep, deep)], w_sem.at[i, j])
+            for j in range(slabs)
+        ]
+        for i, (w, buf) in enumerate(((wk_hbm, wk_buf), (wv_hbm, wv_buf)))
     ]
-    for copy in loads + weights:
+    gain_load.start()
+    for copy in loads:
         copy.start()
-    gain = gain_ref[...]
+    for j in range(slabs):
+        for i in range(2):
+            weights[i][j].start()
+    gain_load.wait()
+    gain = gain_buf[...]
     pair = 2 * WW
     per_window = WIN * WIN
     for i in range(parts):
@@ -77,11 +90,15 @@
     high = mean.astype(BF16)
     low = (mean - high.astype(F32)).astype(BF16)
     both = jnp.concatenate([high, low], axis=0)
-    for i, buf in enumerate((wk_buf, wv_buf)):
-        weights[i].wait()
-        z = jnp.dot(both, buf[...], preferred_element_type=F32)
-        cols = HEADS * HD
-        pooled_ref[:, i * cols : (i + 1) * cols] = (z[:out_rows] + z[out_rows:]).astype(BF16)
+    cols = HEADS * HD
+    total = [0.0, 0.0]
+    for j in range(slabs):
+        for i, buf in enumerate((wk_buf, wv_buf)):
+            weights[i][j].wait()
+            part = slice(j * deep, (j + 1) * deep)
+            total[i] += jnp.dot(both[:, part], buf[part, :], preferred_element_type=F32)
+    for i in range(2):
+        pooled_ref[:, i * cols : (i + 1) * cols] = (total[i][:out_rows] + total[i][out_rows:]).astype(BF16)
 
 
 def norm_and_pool(frames, gain, w_key, w_value):
@@ -94,19 +111,21 @@
             jax.ShapeDtypeStruct((rows, width), BF16),
             jax.ShapeDtypeStruct((out_rows, 2 * cols), BF16),
         ),
-        in_specs=[HBM, VMEM, HBM, HBM],
+        in_specs=[HBM] * 4,
         out_specs=(VMEM, VMEM),
         scratch_shapes=[
             pltpu.VMEM((rows, width), BF16),
+            pltpu.VMEM((1, width), F32),
             pltpu.VMEM((width, cols), BF16),
             pltpu.VMEM((width, cols), BF16),
             pltpu.SemaphoreType.DMA((4,)),
-            pltpu.SemaphoreType.DMA((2,)),
+            pltpu.SemaphoreType.DMA,
+            pltpu.SemaphoreType.DMA((2, 4)),
         ],
         compiler_params=pltpu.CompilerParams(vmem_limit_bytes=24 << 20),
         cost_estimate=pl.CostEstimate(flops=400_000_000, bytes_accessed=8_000_000, transcendentals=0),
         name="norm_and_pool",
-    )(frames, gain.reshape(1, width), w_key, w_value)
+    )(*(pltpu.with_memory_space_constraint(x, pltpu.HBM) for x in (frames, gain, w_key, w_value)))
 
 
 def own_block(me, mask_pair):
@@ -234,22 +253,29 @@
     cols = HEADS * HD
     phases, held = exchange_plan(n)
     normed, block = norm_and_pool(frames_in, norm_gain, w_key, w_value)
+    block, w_query, w_key, w_value = lax.optimization_barrier((block, w_query, w_key, w_value))
 
     def send(x, pair):
         return lax.ppermute(x, "tm", [(i, i ^ pair[i % 2]) for i in range(n)])
 
-    for pair in phases[:-1]:
+    projected = []
+    weights = [w_query, w_key, w_value]
+    share = -(-len(weights) // max(len(phases) - 1, 1))
+    for i, pair in enumerate(phases[:-1]):
         block = jnp.concatenate([block, send(block, pair)], axis=0)
+        take = 1 if i == 0 else share
+        done = [jnp.dot(normed, w, preferred_element_type=F32).astype(BF16) for w in weights[:take]]
+        weights = weights[take:]
+        block, *done = lax.optimization_barrier((block, *done))
+        projected += done
+    projected += [jnp.dot(normed, w, preferred_element_type=F32).astype(BF16) for w in weights]
+    query, keys, values = projected
     late = send(block, phases[-1])
     other = send(block, (1, 1))
-    other_late = send(late, (1, 1))
     half = len(held[0]) // 2
     own = list(zip(held[0], held[1]))
     far = [(a ^ 1, b ^ 1) for b, a in own]
 
-    query, keys, values = (
-        jnp.dot(normed, w, preferred_element_type=F32).astype(BF16) for w in (w_query, w_key, w_value)
-    )
     state = (
         jax.ShapeDtypeStruct((cols, rows), F32),
         jax.ShapeDtypeStruct((8, rows), F32),
@@ -265,6 +291,8 @@
         cost_estimate=pl.CostEstimate(flops=900_000_000, bytes_accessed=5_000_000, transcendentals=1_000_000),
         name="local_and_first",
     )(frame_time, query, keys, values, block, other)
+    late, acc, m, l = lax.optimization_barrier((late, acc, m, l))
+    other_late = send(late, (1, 1))
     acc, m, l = pl.pallas_call(
         functools.partial(middle_kernel, own[half:]),
         out_shape=state,

time: 42.3 us -> 33.8 us (0.80); the launches traced: 41.6 us -> 33.6 us
  local copies, waits for them, and re-layouts: 5.63 us -> 0.3 us
  waiting for transfers between devices: 9.25 us -> 5.92 us
  Pallas kernels: 14.2 us -> 15.7 us
  starting transfers between devices: 8.25 us -> 7.41 us
    unnamed x14 -> x10, local copies, waits for them, and re-layouts: 4.77 us -> 0.3 us
    ppermute x5, waiting for transfers between devices: 9.25 us -> 5.92 us  [send(): return lax.ppermute(x, 'tm', [(i, i ^ pair[i % 2]) for i in range(n)])]
    pallas_call x1, Pallas kernels: 3.39 us -> 4.91 us  [norm_and_pool(): pl.pallas_call(norm_kernel, out_shape=(jax.ShapeDtypeStruct((rows, width)...]
    reshape x1 -> x0, local copies, waits for them, and re-layouts: 0.85 us -> none  [norm_and_pool(): gain.reshape(1, width)]
    ppermute x5, starting transfers between devices: 8.25 us -> 7.41 us  [send(): return lax.ppermute(x, 'tm', [(i, i ^ pair[i % 2]) for i in range(n)])]
  transfers between devices with their start and end apart: 5 -> 5, of which waited for: 3 -> 3; matrix products, arithmetic and copies ran while one was open for 10% -> 12% of each run, Pallas kernels for 14% -> 18%
where the time goes in v2:
time: 33.8 us; the launch traced here: 33.6 us
  Pallas kernels  15.7 us (46%)
  starting transfers between devices  7.41 us (22%)
  waiting for transfers between devices  5.92 us (18%)
  matrix products  4.14 us (12%)
    ppermute x5, starting transfers between devices, send(): return lax.ppermute(x, 'tm', [(i, i ^ pair[i % 2]) for i in range(n)])  7.41 us
    ppermute x5, waiting for transfers between devices, send(): return lax.ppermute(x, 'tm', [(i, i ^ pair[i % 2]) for i in range(n)])  5.92 us
    pallas_call x1, Pallas kernels, on_device(): pl.pallas_call(functools.partial(last_kernel, far[half:]), out_shape=jax....  4.92 us
    pallas_call x1, Pallas kernels, norm_and_pool(): pl.pallas_call(norm_kernel, out_shape=(jax.ShapeDtypeStruct((rows, width)...  4.91 us
    dot_general x3, matrix products, on_device(): jnp.dot(normed, w, preferred_element_type=F32).astype(BF16)  4.14 us
    pallas_call x1, Pallas kernels, on_device(): pl.pallas_call(functools.partial(first_kernel, own[:half] + far[:half]),...  3.35 us
    pallas_call x1, Pallas kernels, on_device(): pl.pallas_call(functools.partial(middle_kernel, own[half:]), out_shape=st...  2.56 us
  transfers between devices with their start and end apart: 5, of which 3 were waited for; matrix products, arithmetic and copies ran while one was open for 12% of the time, Pallas kernels for 18%

profile of v2, /device:TPU:0, one launch (start us, length us, event | category | flops | bytes accessed | tf_op | source)
XLA Modules:
  0.0 33.6 jit_solution(13796539472809621359)
XLA Ops:
  0.0 0.0 copy-start
  0.0 4.9 %norm_and_pool.1 = (bf16[512,1536]{1,0:T(8,128)(2,1)S(1)}, bf16[32,1536]{1,0:T(8,128)(2,1)S(1)}) custom-call(bf16[512,1536]{1,0:T(8,128)(2,1)} %frames_hbm.1, f32[1536]{0:T(1024)} %gain_hbm.1, bf16[1536,768]{1,0:T(8,128)(2,1)} %wk_hbm.1, bf16[1536,768]{1,0:T(8,128)(2,1)} %wv_hbm.1), custom_call_target="tpu_custom_call" | custom-call | flops 400000000 | bytes 8000000 | tf_op jit(solution)/shard_map/norm_and_pool/pallas_call | solution.py:108
  4.9 4.1 %collective-permute-start = (bf16[32,1536]{1,0:T(8,128)(2,1)S(1)}, bf16[32,1536]{1,0:T(8,128)(2,1)S(1)}, u32[]{:S(2)}, u32[]{:S(2)}) collective-permute-start(bf16[32,1536]{1,0:T(8,128)(2,1)S(1)} %get-tuple-element.27), channel_id=1, source_target_pairs={{0,8},{1,5},{2,10},{3,7},{4,12},{5,1},{6,14},{7,3},{8,0},{9,13},{1... | collective-permute-start | bytes 294920 | tf_op jit(solution)/shard_map/ppermute | solution.py:259
  9.0 0.0 copy-done
  9.0 0.0 copy-start.3
  9.0 1.4 %convolution_convert_fusion.2.q_ref = bf16[512,768]{1,0:T(8,128)(2,1)S(1)} fusion(bf16[512,1536]{1,0:T(8,128)(2,1)S(1)} %get-tuple-element.28, bf16[1536,768]{1,0:T(8,128)(2,1)S(1)} %copy-done), kind=kOutput, calls=%fused_computation.2 | convolution fusion | flops 1208352768 | bytes 4718592 | tf_op jit(solution)/shard_map/dot_general | solution.py:267
  10.4 0.3 copy-done.3
  10.7 0.0 copy-start.4
  10.7 1.4 %convolution_convert_fusion.1.k_ref = bf16[512,768]{1,0:T(8,128)(2,1)S(1)} fusion(bf16[512,1536]{1,0:T(8,128)(2,1)S(1)} %get-tuple-element.28, bf16[1536,768]{1,0:T(8,128)(2,1)S(1)} %copy-done.3), kind=kOutput, calls=%fused_computation.1 | convolution fusion | flops 1208352768 | bytes 4718592 | tf_op jit(solution)/shard_map/dot_general | solution.py:267
  12.1 0.0 collective-permute-done
  12.1 0.0 copy-start.2
  12.1 1.6 %collective-permute-start.1 = (bf16[64,1536]{1,0:T(8,128)(2,1)S(1)}, bf16[64,1536]{1,0:T(8,128)(2,1)S(1)}, u32[]{:S(2)}, u32[]{:S(2)}) collective-permute-start(bf16[64,1536]{1,0:T(8,128)(2,1)S(1)} %pad_maximum_fusion.1), channel_id=1, source_target_pairs={{0,2},{1,9},{2,0},{3,11},{4,6},{5,13},{6,4},{7,15},{8,10},{9,1},{1... | collective-permute-start | bytes 589832 | tf_op jit(solution)/shard_map/ppermute | solution.py:259
  13.7 0.0 copy-done.4
  13.7 1.4 %convolution_convert_fusion.v_ref = bf16[512,768]{1,0:T(8,128)(2,1)S(1)} fusion(bf16[512,1536]{1,0:T(8,128)(2,1)S(1)} %get-tuple-element.28, bf16[1536,768]{1,0:T(8,128)(2,1)S(1)} %copy-done.4), kind=kOutput, calls=%fused_computation | convolution fusion | flops 1208352768 | bytes 4718592 | tf_op jit(solution)/shard_map/dot_general | solution.py:267
  15.1 2.8 %collective-permute-done.1 = bf16[64,1536]{1,0:T(8,128)(2,1)S(1)} collective-permute-done((bf16[64,1536]{1,0:T(8,128)(2,1)S(1)}, bf16[64,1536]{1,0:T(8,128)(2,1)S(1)}, u32[]{:S(2)}, u32[]{:S(2)}) %collective-permute-start.1) | collective-permute-done | bytes 196640 | tf_op jit(solution)/shard_map/ppermute | solution.py:259
  17.9 0.5 %collective-permute-start.3 = (bf16[128,1536]{1,0:T(8,128)(2,1)S(1)}, bf16[128,1536]{1,0:T(8,128)(2,1)S(1)}, u32[]{:S(2)}, u32[]{:S(2)}) collective-permute-start(bf16[128,1536]{1,0:T(8,128)(2,1)S(1)} %pad_maximum_fusion.near_ref), channel_id=1, source_target_pairs={{0,1},{1,0},{2,3},{3,2},{4,5},{5,4},{6,7},{7,6},{8,9},{9,8},{10,11... | collective-permute-start | bytes 1179656 | tf_op jit(solution)/shard_map/ppermute | solution.py:259
  18.4 1.3 %collective-permute-start.2 = (bf16[128,1536]{1,0:T(8,128)(2,1)S(1)}, bf16[128,1536]{1,0:T(8,128)(2,1)S(1)}, u32[]{:S(2)}, u32[]{:S(2)}) collective-permute-start(bf16[128,1536]{1,0:T(8,128)(2,1)S(1)} %pad_maximum_fusion.near_ref), channel_id=1, source_target_pairs={{0,4},{1,3},{2,6},{3,1},{4,0},{5,7},{6,2},{7,5},{8,12},{9,11},{10,... | collective-permute-start | bytes 1179656 | tf_op jit(solution)/shard_map/ppermute | solution.py:259
  19.6 0.1 collective-permute-done.3.other_ref
  19.7 0.0 copy-done.2
  19.7 3.3 %local_and_first.1 = (f32[768,512]{1,0:T(8,128)S(1)}, f32[8,512]{1,0:T(8,128)S(1)}, f32[8,512]{1,0:T(8,128)S(1)}) custom-call(s32[32]{0:T(128)S(1)} %copy-done.2, bf16[512,768]{1,0:T(8,128)(2,1)S(1)} %convolution_convert_fusion.2.q_ref, bf16[512,768]{1,0:T(8,128)(2,1)S(1)} %convolution_convert_fusion.1.k_ref, ...), custom_call_target="tpu_custom_call" | custom-call | flops 900000000 | bytes 5000000 | tf_op jit(solution)/shard_map/local_and_first/pallas_call | solution.py:285
  23.1 0.0 copy-start.1
  23.1 3.1 %collective-permute-done.2.far_ref = bf16[128,1536]{1,0:T(8,128)(2,1)S(1)} collective-permute-done((bf16[128,1536]{1,0:T(8,128)(2,1)S(1)}, bf16[128,1536]{1,0:T(8,128)(2,1)S(1)}, u32[]{:S(2)}, u32[]{:S(2)}) %collective-permute-start.2) | collective-permute-done | bytes 393248 | tf_op jit(solution)/shard_map/ppermute | solution.py:259
  26.1 0.0 collective-permute-start.4
  26.1 2.6 %middle.1 = (f32[768,512]{1,0:T(8,128)S(1)}, f32[8,512]{1,0:T(8,128)S(1)}, f32[8,512]{1,0:T(8,128)S(1)}) custom-call(s32[32]{0:T(128)S(1)} %copy-done.2, bf16[512,768]{1,0:T(8,128)(2,1)S(1)} %convolution_convert_fusion.2.q_ref, bf16[128,1536]{1,0:T(8,128)(2,1)S(1)} %collective-permute-done.2.far_ref, ...), custom_call_target="tpu_custom_call", output_to_operand_aliasing={{0}: (3, {}), {1}: (4, {}), {2}: (5, {})} | custom-call | flops 500000000 | bytes 5000000 | tf_op jit(solution)/shard_map/middle/pallas_call | solution.py:296
  28.7 0.0 collective-permute-done.4.far_ref
  28.7 0.0 copy-done.1
  28.7 4.9 %last_and_output.1 = bf16[512,1536]{1,0:T(8,128)(2,1)} custom-call(s32[32]{0:T(128)S(1)} %copy-done.2, bf16[512,768]{1,0:T(8,128)(2,1)S(1)} %convolution_convert_fusion.2.q_ref, bf16[128,1536]{1,0:T(8,128)(2,1)S(1)} %collective-permute-done.4.far_ref, f32[768,512]{1,0:T(8,128)S(1)} %get-tuple-element.44.acc_in, f32[8,512]{1,0:T(8,128)S(1)} %get-tuple-element.45.m_in, ...), custom_call_target="tpu_custom_call" | custom-call | flops 1700000000 | bytes 8000000 | tf_op jit(solution)/shard_map/last_and_output/pallas_call | solution.py:306
  (2 shorter events, 0.0 us)
Async XLA Ops:
  0.0 9.0 %copy-start = (bf16[1536,768]{1,0:T(8,128)(2,1)S(1)}, bf16[1536,768]{1,0:T(8,128)(2,1)}, u32[]{:S(2)}) copy-start(bf16[1536,768]{1,0:T(8,128)(2,1)} %param.10) | copy-start | bytes 7077892
  4.9 7.2 %collective-permute-start = (bf16[32,1536]{1,0:T(8,128)(2,1)S(1)}, bf16[32,1536]{1,0:T(8,128)(2,1)S(1)}, u32[]{:S(2)}, u32[]{:S(2)}) collective-permute-start(bf16[32,1536]{1,0:T(8,128)(2,1)S(1)} %get-tuple-element.27), channel_id=1, source_target_pairs={{0,8},{1,5},{2,10},{3,7},{4,12},{5,1},{6,14},{7,3},{8,0},{9,13},{1... | collective-permute-start | bytes 294920 | tf_op jit(solution)/shard_map/ppermute | solution.py:259
  9.0 1.7 %copy-start.3 = (bf16[1536,768]{1,0:T(8,128)(2,1)S(1)}, bf16[1536,768]{1,0:T(8,128)(2,1)}, u32[]{:S(2)}) copy-start(bf16[1536,768]{1,0:T(8,128)(2,1)} %wk_hbm.1) | copy-start | bytes 7077892
  10.7 3.0 %copy-start.4 = (bf16[1536,768]{1,0:T(8,128)(2,1)S(1)}, bf16[1536,768]{1,0:T(8,128)(2,1)}, u32[]{:S(2)}) copy-start(bf16[1536,768]{1,0:T(8,128)(2,1)} %wv_hbm.1) | copy-start | bytes 7077892
  12.1 7.6 %copy-start.2 = (s32[32]{0:T(128)S(1)}, s32[32]{0:T(128)}, u32[]{:S(2)}) copy-start(s32[32]{0:T(128)} %time_ref.5) | copy-start | bytes 388
  12.1 5.7 %collective-permute-start.1 = (bf16[64,1536]{1,0:T(8,128)(2,1)S(1)}, bf16[64,1536]{1,0:T(8,128)(2,1)S(1)}, u32[]{:S(2)}, u32[]{:S(2)}) collective-permute-start(bf16[64,1536]{1,0:T(8,128)(2,1)S(1)} %pad_maximum_fusion.1), channel_id=1, source_target_pairs={{0,2},{1,9},{2,0},{3,11},{4,6},{5,13},{6,4},{7,15},{8,10},{9,1},{1... | collective-permute-start | bytes 589832 | tf_op jit(solution)/shard_map/ppermute | solution.py:259
  17.9 1.8 %collective-permute-start.3 = (bf16[128,1536]{1,0:T(8,128)(2,1)S(1)}, bf16[128,1536]{1,0:T(8,128)(2,1)S(1)}, u32[]{:S(2)}, u32[]{:S(2)}) collective-permute-start(bf16[128,1536]{1,0:T(8,128)(2,1)S(1)} %pad_maximum_fusion.near_ref), channel_id=1, source_target_pairs={{0,1},{1,0},{2,3},{3,2},{4,5},{5,4},{6,7},{7,6},{8,9},{9,8},{10,11... | collective-permute-start | bytes 1179656 | tf_op jit(solution)/shard_map/ppermute | solution.py:259
  18.4 7.8 %collective-permute-start.2 = (bf16[128,1536]{1,0:T(8,128)(2,1)S(1)}, bf16[128,1536]{1,0:T(8,128)(2,1)S(1)}, u32[]{:S(2)}, u32[]{:S(2)}) collective-permute-start(bf16[128,1536]{1,0:T(8,128)(2,1)S(1)} %pad_maximum_fusion.near_ref), channel_id=1, source_target_pairs={{0,4},{1,3},{2,6},{3,1},{4,0},{5,7},{6,2},{7,5},{8,12},{9,11},{10,... | collective-permute-start | bytes 1179656 | tf_op jit(solution)/shard_map/ppermute | solution.py:259
  23.1 5.7 %copy-start.1 = (bf16[768,1536]{1,0:T(8,128)(2,1)S(1)}, bf16[768,1536]{1,0:T(8,128)(2,1)}, u32[]{:S(2)}) copy-start(bf16[768,1536]{1,0:T(8,128)(2,1)} %wo_ref.1) | copy-start | bytes 7077892
  26.1 2.6 %collective-permute-start.4 = (bf16[128,1536]{1,0:T(8,128)(2,1)S(1)}, bf16[128,1536]{1,0:T(8,128)(2,1)S(1)}, u32[]{:S(2)}, u32[]{:S(2)}) collective-permute-start(bf16[128,1536]{1,0:T(8,128)(2,1)S(1)} %collective-permute-done.2.far_ref), channel_id=1, source_target_pairs={{0,1},{1,0},{2,3},{3,2},{4,5},{5,4},{6,7},{7,6},{8,9},{9,8},{10,11... | collective-permute-start | bytes 1179656 | tf_op jit(solution)/shard_map/ppermute | solution.py:259

commit v3 on v2

--- a/solution.py
+++ b/solution.py
@@ -41,32 +41,27 @@
     rows, width = x_buf.shape
     parts = x_sem.shape[0]
     step = rows // parts
-    slabs = w_sem.shape[1]
-    deep = width // slabs
     gain_load = pltpu.make_async_copy(gain_hbm, gain_buf.at[0], g_sem)
     loads = [
         pltpu.make_async_copy(frames_hbm.at[pl.ds(i * step, step)], x_buf.at[pl.ds(i * step, step)], x_sem.at[i])
         for i in range(parts)
     ]
     weights = [
-        [
-            pltpu.make_async_copy(w.at[pl.ds(j * deep, deep)], buf.at[pl.ds(j * deep, deep)], w_sem.at[i, j])
-            for j in range(slabs)
-        ]
-        for i, (w, buf) in enumerate(((wk_hbm, wk_buf), (wv_hbm, wv_buf)))
+        pltpu.make_async_copy(wk_hbm, wk_buf, w_sem.at[0]),
+        pltpu.make_async_copy(wv_hbm, wv_buf, w_sem.at[1]),
     ]
-    gain_load.start()
     for copy in loads:
         copy.start()
-    for j in range(slabs):
-        for i in range(2):
-            weights[i][j].start()
-    gain_load.wait()
-    gain = gain_buf[...]
+    gain_load.start()
+    weights[0].start()
     pair = 2 * WW
     per_window = WIN * WIN
     for i in range(parts):
         loads[i].wait()
+        if i == 0:
+            weights[1].start()
+            gain_load.wait()
+            gain = gain_buf[...]
         for g in range(i * step // pair, (i + 1) * step // pair):
             x = x_buf[pl.ds(g * pair, pair), :].astype(F32)
             scale = lax.rsqrt(jnp.mean(x * x, axis=-1, keepdims=True) + 1e-06)
@@ -91,14 +86,10 @@
     low = (mean - high.astype(F32)).astype(BF16)
     both = jnp.concatenate([high, low], axis=0)
     cols = HEADS * HD
-    total = [0.0, 0.0]
-    for j in range(slabs):
-        for i, buf in enumerate((wk_buf, wv_buf)):
-            weights[i][j].wait()
-            part = slice(j * deep, (j + 1) * deep)
-            total[i] += jnp.dot(both[:, part], buf[part, :], preferred_element_type=F32)
-    for i in range(2):
-        pooled_ref[:, i * cols : (i + 1) * cols] = (total[i][:out_rows] + total[i][out_rows:]).astype(BF16)
+    for i, buf in enumerate((wk_buf, wv_buf)):
+        weights[i].wait()
+        z = jnp.dot(both, buf[...], preferred_element_type=F32)
+        pooled_ref[:, i * cols : (i + 1) * cols] = (z[:out_rows] + z[out_rows:]).astype(BF16)
 
 
 def norm_and_pool(frames, gain, w_key, w_value):
@@ -118,9 +109,9 @@
             pltpu.VMEM((1, width), F32),
             pltpu.VMEM((width, cols), BF16),
             pltpu.VMEM((width, cols), BF16),
-            pltpu.SemaphoreType.DMA((4,)),
+            pltpu.SemaphoreType.DMA((2,)),
             pltpu.SemaphoreType.DMA,
-            pltpu.SemaphoreType.DMA((2, 4)),
+            pltpu.SemaphoreType.DMA((2,)),
         ],
         compiler_params=pltpu.CompilerParams(vmem_limit_bytes=24 << 20),
         cost_estimate=pl.CostEstimate(flops=400_000_000, bytes_accessed=8_000_000, transcendentals=0),
@@ -169,83 +160,119 @@
 
 def first_kernel(masks, time_ref, q_ref, k_ref, v_ref, near_ref, other_ref, acc_ref, m_ref, l_ref):
     tokens = q_ref.shape[0]
-    count = tokens // TOKENS
     per_window = WIN * WIN
     cols = HEADS * HD
-    bias = mask_columns(time_ref, masks, count)
+    bias = mask_columns(time_ref, masks, tokens // TOKENS)
     frames = frame_columns(tokens)
     left = lax.broadcasted_iota(jnp.int32, (per_window, 2 * per_window), 1) < per_window
-    for h in range(HEADS):
+    pairs = [slice(w, w + 2 * per_window) for w in range(0, tokens, 2 * per_window)]
+
+    def scores(h):
         q = q_ref[:, head(h)]
         far_k = jnp.concatenate([near_ref[:, head(h)], other_ref[:, head(h)]], axis=0)
-        far_v = jnp.concatenate([near_ref[:, head(h, cols)], other_ref[:, head(h, cols)]], axis=0)
         far_s = dot_nt(jnp.concatenate([far_k, bias], axis=1), jnp.concatenate([q, frames], axis=1))
         parts = []
-        for w in range(tokens // (2 * per_window)):
-            two = pl.ds(w * 2 * per_window, 2 * per_window)
+        for two in pairs:
             s = dot_nt(k_ref[two, head(h)], q_ref[two, head(h)])
             parts.append(jnp.where(left, s[:per_window], s[per_window:]))
-        local_s = jnp.concatenate(parts, axis=1)
+        return jnp.concatenate(parts, axis=1), far_s
+
+    def weigh(h, local_s, far_s):
         top = jnp.maximum(jnp.max(local_s, axis=0, keepdims=True), jnp.max(far_s, axis=0, keepdims=True))
         local_w = jnp.exp2((local_s - top) * SCALE)
         far_w = jnp.exp2((far_s - top) * SCALE)
-        total = jnp.sum(local_w, axis=0, keepdims=True) + jnp.sum(far_w, axis=0, keepdims=True)
-        acc = dot_tn(far_v, far_w.astype(BF16))
-        parts = []
-        for w in range(tokens // (2 * per_window)):
-            two = pl.ds(w * 2 * per_window, 2 * per_window)
-            p = local_w[:, w * 2 * per_window : (w + 1) * 2 * per_window]
+        m_ref[h : h + 1, :] = top
+        l_ref[h : h + 1, :] = jnp.sum(local_w, axis=0, keepdims=True) + jnp.sum(far_w, axis=0, keepdims=True)
+        return local_w, far_w.astype(BF16)
+
+    def mix(h, local_w, far_w):
+        far_v = jnp.concatenate([near_ref[:, head(h, cols)], other_ref[:, head(h, cols)]], axis=0)
+        acc = dot_tn(far_v, far_w)
+        for two in pairs:
+            p = local_w[:, two]
             p = jnp.concatenate([jnp.where(left, p, 0.0), jnp.where(left, 0.0, p)], axis=0).astype(BF16)
-            parts.append(dot_tn(v_ref[two, head(h)], p))
-        acc_ref[head(h), :] = acc + jnp.concatenate(parts, axis=1)
+            acc_ref[head(h), two] = acc[:, two] + dot_tn(v_ref[two, head(h)], p)
+
+    pipelined(scores, weigh, mix)
+
+
+def pipelined(scores, weigh, mix):
+    ahead = 2
+    ready = {h: scores(h) for h in range(ahead)}
+    weights = {}
+    for h in range(HEADS):
+        if h + ahead < HEADS:
+            ready[h + ahead] = scores(h + ahead)
+        weights[h] = weigh(h, *ready.pop(h))
+        if h > 0:
+            mix(h - 1, *weights.pop(h - 1))
+    mix(HEADS - 1, *weights.pop(HEADS - 1))
+
+
+def far_stages(masks, time_ref, q_ref, far_ref, m_in, l_in, acc_in, keep_state, keep_acc):
+    tokens = q_ref.shape[0]
+    cols = HEADS * HD
+    bias = mask_columns(time_ref, masks, tokens // TOKENS)
+    frames = frame_columns(tokens)
+
+    def scores(h):
+        far_k = jnp.concatenate([far_ref[:, head(h)], bias], axis=1)
+        return (dot_nt(far_k, jnp.concatenate([q_ref[:, head(h)], frames], axis=1)),)
+
+    def weigh(h, s):
+        m, l = m_in[h : h + 1, :], l_in[h : h + 1, :]
+        top = jnp.maximum(m, jnp.max(s, axis=0, keepdims=True))
+        w = jnp.exp2((s - top) * SCALE)
+        keep = jnp.exp2((m - top) * SCALE)
+        total = l * keep + jnp.sum(w, axis=0, keepdims=True)
+        return w.astype(BF16), keep, keep_state(h, top, total)
+
+    def mix(h, w, keep, state):
+        keep_acc(h, acc_in[head(h), :] * keep + dot_tn(far_ref[:, head(h, cols)], w), state)
+
+    pipelined(scores, weigh, mix)
+
+
+def middle_kernel(masks, time_ref, q_ref, far_ref, acc_in, m_in, l_in, acc_ref, m_ref, l_ref):
+    def keep_state(h, top, total):
         m_ref[h : h + 1, :] = top
         l_ref[h : h + 1, :] = total
 
-
-def far_step(h, q_ref, far_ref, bias, frames, m, l, acc):
-    cols = HEADS * HD
-    s = dot_nt(
-        jnp.concatenate([far_ref[:, head(h)], bias], axis=1),
-        jnp.concatenate([q_ref[:, head(h)], frames], axis=1),
+    def keep_acc(h, acc, _):
+        acc_ref[head(h), :] = acc
+
+    far_stages(masks, time_ref, q_ref, far_ref, m_in, l_in, acc_in, keep_state, keep_acc)
+
+
+def last_kernel(
+    masks, time_ref, q_ref, far_ref, acc_in, m_in, l_in, wo_ref, out_hbm, rows_buf, out_buf, out_sem
+):
+    tokens = q_ref.shape[0]
+    per_window = WIN * WIN
+
+    def keep_acc(h, acc, inverse):
+        mixed = jnp.transpose(acc * inverse)
+        for row in range(tokens // WW):
+            frame, rest = divmod(row, HH)
+            wr, r = divmod(rest, WIN)
+            base = frame * TOKENS + wr * (WW // WIN) * per_window + r * WIN
+            starts = [base + wc * per_window for wc in range(WW // WIN)]
+            line = jnp.concatenate([mixed[i : i + WIN] for i in starts], axis=0)
+            rows_buf[pl.ds(row * WW, WW), head(h)] = line.astype(BF16)
+
+    far_stages(
+        masks, time_ref, q_ref, far_ref, m_in, l_in, acc_in, lambda h, top, total: 1.0 / total, keep_acc
     )
-    top = jnp.maximum(m, jnp.max(s, axis=0, keepdims=True))
-    w = jnp.exp2((s - top) * SCALE)
-    keep = jnp.exp2((m - top) * SCALE)
-    l = l * keep + jnp.sum(w, axis=0, keepdims=True)
-    acc = acc * keep + dot_tn(far_ref[:, head(h, cols)], w.astype(BF16))
-    return top, l, acc
-
-
-def middle_kernel(masks, time_ref, q_ref, far_ref, acc_in, m_in, l_in, acc_ref, m_ref, l_ref):
-    tokens = q_ref.shape[0]
-    bias = mask_columns(time_ref, masks, tokens // TOKENS)
-    frames = frame_columns(tokens)
-    for h in range(HEADS):
-        m, l, acc = far_step(
-            h, q_ref, far_ref, bias, frames, m_in[h : h + 1, :], l_in[h : h + 1, :], acc_in[head(h), :]
-        )
-        acc_ref[head(h), :] = acc
-        m_ref[h : h + 1, :] = m
-        l_ref[h : h + 1, :] = l
-
-
-def last_kernel(masks, time_ref, q_ref, far_ref, acc_in, m_in, l_in, wo_ref, out_ref, mixed, rows_buf):
-    tokens = q_ref.shape[0]
-    bias = mask_columns(time_ref, masks, tokens // TOKENS)
-    frames = frame_columns(tokens)
-    for h in range(HEADS):
-        m, l, acc = far_step(
-            h, q_ref, far_ref, bias, frames, m_in[h : h + 1, :], l_in[h : h + 1, :], acc_in[head(h), :]
-        )
-        mixed[:, head(h)] = jnp.transpose(acc * (1.0 / l))
-    per_window = WIN * WIN
-    for row in range(tokens // WW):
-        frame, rest = divmod(row, HH)
-        wr, r = divmod(rest, WIN)
-        base = frame * TOKENS + wr * (WW // WIN) * per_window + r * WIN
-        line = jnp.concatenate([mixed[pl.ds(base + wc * per_window, WIN), :] for wc in range(WW // WIN)], axis=0)
-        rows_buf[pl.ds(row * WW, WW), :] = line.astype(BF16)
-    out_ref[...] = jnp.dot(rows_buf[...], wo_ref[...], preferred_element_type=F32).astype(BF16)
+    chunks = out_sem.shape[0]
+    width = out_buf.shape[1] // chunks
+    copies = []
+    for c in range(chunks):
+        part = pl.ds(c * width, width)
+        out_buf[:, part] = jnp.dot(rows_buf[...], wo_ref[:, part], preferred_element_type=F32).astype(BF16)
+        copies.append(pltpu.make_async_copy(out_buf.at[:, part], out_hbm.at[:, part], out_sem.at[c]))
+        copies[-1].start()
+    for copy in copies:
+        copy.wait()
 
 
 def on_device(n, frames_in, frame_time, norm_gain, w_query, w_key, w_value, w_output):
@@ -307,8 +334,12 @@
         functools.partial(last_kernel, far[half:]),
         out_shape=jax.ShapeDtypeStruct((rows, w_output.shape[1]), BF16),
         in_specs=[SMEM] + [VMEM] * 6,
-        out_specs=VMEM,
-        scratch_shapes=[pltpu.VMEM((rows, cols), F32), pltpu.VMEM((rows, cols), BF16)],
+        out_specs=HBM,
+        scratch_shapes=[
+            pltpu.VMEM((rows, cols), BF16),
+            pltpu.VMEM((rows, w_output.shape[1]), BF16),
+            pltpu.SemaphoreType.DMA((3,)),
+        ],
         compiler_params=params,
         cost_estimate=pl.CostEstimate(flops=1_700_000_000, bytes_accessed=8_000_000, transcendentals=400_000),
         name="last_and_output",

time: 33.8 us -> 30.7 us (0.908)
  Pallas kernels: 15.7 us -> 12 us
  waiting for transfers between devices: 5.92 us -> 6.53 us
    pallas_call x1, Pallas kernels: 4.92 us -> 3.68 us  [on_device(): pl.pallas_call(functools.partial(last_kernel, far[half:]), out_shape=jax....]
    pallas_call x1, Pallas kernels: 4.91 us -> 3.9 us  [norm_and_pool(): pl.pallas_call(norm_kernel, out_shape=(jax.ShapeDtypeStruct((rows, width)...]
    pallas_call x1, Pallas kernels: 2.56 us -> 1.7 us  [on_device(): pl.pallas_call(functools.partial(middle_kernel, own[half:]), out_shape=st...]
    ppermute x5, waiting for transfers between devices: 5.92 us -> 6.53 us  [send(): return lax.ppermute(x, 'tm', [(i, i ^ pair[i % 2]) for i in range(n)])]
    pallas_call x1, Pallas kernels: 3.35 us -> 2.74 us  [on_device(): pl.pallas_call(functools.partial(first_kernel, own[:half] + far[:half]),...]
  transfers between devices with their start and end apart: 5 -> 5, of which waited for: 3 -> 3; matrix products, arithmetic and copies ran while one was open for 12% -> 14% of each run, Pallas kernels for 18% -> 15%
where the time goes in v3:
time: 30.7 us; the launch traced here: 30.5 us
  Pallas kernels  12 us (39%)
  starting transfers between devices  7.41 us (24%)
  waiting for transfers between devices  6.53 us (21%)
  matrix products  4.14 us (13%)
    ppermute x5, starting transfers between devices, send(): return lax.ppermute(x, 'tm', [(i, i ^ pair[i % 2]) for i in range(n)])  7.41 us
    ppermute x5, waiting for transfers between devices, send(): return lax.ppermute(x, 'tm', [(i, i ^ pair[i % 2]) for i in range(n)])  6.53 us
    dot_general x3, matrix products, on_device(): jnp.dot(normed, w, preferred_element_type=F32).astype(BF16)  4.14 us
    pallas_call x1, Pallas kernels, norm_and_pool(): pl.pallas_call(norm_kernel, out_shape=(jax.ShapeDtypeStruct((rows, width)...  3.9 us
    pallas_call x1, Pallas kernels, on_device(): pl.pallas_call(functools.partial(last_kernel, far[half:]), out_shape=jax....  3.68 us
    pallas_call x1, Pallas kernels, on_device(): pl.pallas_call(functools.partial(first_kernel, own[:half] + far[:half]),...  2.74 us
    pallas_call x1, Pallas kernels, on_device(): pl.pallas_call(functools.partial(middle_kernel, own[half:]), out_shape=st...  1.7 us
  transfers between devices with their start and end apart: 5, of which 3 were waited for; matrix products, arithmetic and copies ran while one was open for 14% of the time, Pallas kernels for 15%

profile of v3, /device:TPU:0, one launch (start us, length us, event | category | flops | bytes accessed | tf_op | source)
XLA Modules:
  0.0 30.5 jit_solution(2478137091579245985)
XLA Ops:
  0.0 0.0 copy-start
  0.0 3.9 %norm_and_pool.1 = (bf16[512,1536]{1,0:T(8,128)(2,1)S(1)}, bf16[32,1536]{1,0:T(8,128)(2,1)S(1)}) custom-call(bf16[512,1536]{1,0:T(8,128)(2,1)} %frames_hbm.1, f32[1536]{0:T(1024)} %gain_hbm.1, bf16[1536,768]{1,0:T(8,128)(2,1)} %wk_hbm.1, bf16[1536,768]{1,0:T(8,128)(2,1)} %wv_hbm.1), custom_call_target="tpu_custom_call" | custom-call | flops 400000000 | bytes 8000000 | tf_op jit(solution)/shard_map/norm_and_pool/pallas_call | solution.py:99
  3.9 4.1 %collective-permute-start = (bf16[32,1536]{1,0:T(8,128)(2,1)S(1)}, bf16[32,1536]{1,0:T(8,128)(2,1)S(1)}, u32[]{:S(2)}, u32[]{:S(2)}) collective-permute-start(bf16[32,1536]{1,0:T(8,128)(2,1)S(1)} %get-tuple-element.27), channel_id=1, source_target_pairs={{0,8},{1,5},{2,10},{3,7},{4,12},{5,1},{6,14},{7,3},{8,0},{9,13},{1... | collective-permute-start | bytes 294920 | tf_op jit(solution)/shard_map/ppermute | solution.py:286
  8.0 0.0 copy-done
  8.0 0.0 copy-start.3
  8.0 1.4 %convolution_convert_fusion.2.q_ref = bf16[512,768]{1,0:T(8,128)(2,1)S(1)} fusion(bf16[512,1536]{1,0:T(8,128)(2,1)S(1)} %get-tuple-element.28, bf16[1536,768]{1,0:T(8,128)(2,1)S(1)} %copy-done), kind=kOutput, calls=%fused_computation.2 | convolution fusion | flops 1208352768 | bytes 4718592 | tf_op jit(solution)/shard_map/dot_general | solution.py:294
  9.4 0.3 copy-done.3
  9.7 0.0 copy-start.4
  9.7 1.4 %convolution_convert_fusion.1.k_ref = bf16[512,768]{1,0:T(8,128)(2,1)S(1)} fusion(bf16[512,1536]{1,0:T(8,128)(2,1)S(1)} %get-tuple-element.28, bf16[1536,768]{1,0:T(8,128)(2,1)S(1)} %copy-done.3), kind=kOutput, calls=%fused_computation.1 | convolution fusion | flops 1208352768 | bytes 4718592 | tf_op jit(solution)/shard_map/dot_general | solution.py:294
  11.1 0.0 collective-permute-done
  11.1 0.0 copy-start.2
  11.1 1.6 %collective-permute-start.1 = (bf16[64,1536]{1,0:T(8,128)(2,1)S(1)}, bf16[64,1536]{1,0:T(8,128)(2,1)S(1)}, u32[]{:S(2)}, u32[]{:S(2)}) collective-permute-start(bf16[64,1536]{1,0:T(8,128)(2,1)S(1)} %pad_maximum_fusion.1), channel_id=1, source_target_pairs={{0,2},{1,9},{2,0},{3,11},{4,6},{5,13},{6,4},{7,15},{8,10},{9,1},{1... | collective-permute-start | bytes 589832 | tf_op jit(solution)/shard_map/ppermute | solution.py:286
  12.7 0.0 copy-done.4
  12.7 1.4 %convolution_convert_fusion.v_ref = bf16[512,768]{1,0:T(8,128)(2,1)S(1)} fusion(bf16[512,1536]{1,0:T(8,128)(2,1)S(1)} %get-tuple-element.28, bf16[1536,768]{1,0:T(8,128)(2,1)S(1)} %copy-done.4), kind=kOutput, calls=%fused_computation | convolution fusion | flops 1208352768 | bytes 4718592 | tf_op jit(solution)/shard_map/dot_general | solution.py:294
  14.1 2.8 %collective-permute-done.1 = bf16[64,1536]{1,0:T(8,128)(2,1)S(1)} collective-permute-done((bf16[64,1536]{1,0:T(8,128)(2,1)S(1)}, bf16[64,1536]{1,0:T(8,128)(2,1)S(1)}, u32[]{:S(2)}, u32[]{:S(2)}) %collective-permute-start.1) | collective-permute-done | bytes 196640 | tf_op jit(solution)/shard_map/ppermute | solution.py:286
  16.9 0.5 %collective-permute-start.3 = (bf16[128,1536]{1,0:T(8,128)(2,1)S(1)}, bf16[128,1536]{1,0:T(8,128)(2,1)S(1)}, u32[]{:S(2)}, u32[]{:S(2)}) collective-permute-start(bf16[128,1536]{1,0:T(8,128)(2,1)S(1)} %pad_maximum_fusion.near_ref), channel_id=1, source_target_pairs={{0,1},{1,0},{2,3},{3,2},{4,5},{5,4},{6,7},{7,6},{8,9},{9,8},{10,11... | collective-permute-start | bytes 1179656 | tf_op jit(solution)/shard_map/ppermute | solution.py:286
  17.3 1.3 %collective-permute-start.2 = (bf16[128,1536]{1,0:T(8,128)(2,1)S(1)}, bf16[128,1536]{1,0:T(8,128)(2,1)S(1)}, u32[]{:S(2)}, u32[]{:S(2)}) collective-permute-start(bf16[128,1536]{1,0:T(8,128)(2,1)S(1)} %pad_maximum_fusion.near_ref), channel_id=1, source_target_pairs={{0,4},{1,3},{2,6},{3,1},{4,0},{5,7},{6,2},{7,5},{8,12},{9,11},{10,... | collective-permute-start | bytes 1179656 | tf_op jit(solution)/shard_map/ppermute | solution.py:286
  18.6 0.1 collective-permute-done.3.other_ref
  18.7 0.0 copy-done.2
  18.7 2.7 %local_and_first.1 = (f32[768,512]{1,0:T(8,128)S(1)}, f32[8,512]{1,0:T(8,128)S(1)}, f32[8,512]{1,0:T(8,128)S(1)}) custom-call(s32[32]{0:T(128)S(1)} %copy-done.2, bf16[512,768]{1,0:T(8,128)(2,1)S(1)} %convolution_convert_fusion.2.q_ref, bf16[512,768]{1,0:T(8,128)(2,1)S(1)} %convolution_convert_fusion.1.k_ref, ...), custom_call_target="tpu_custom_call" | custom-call | flops 900000000 | bytes 5000000 | tf_op jit(solution)/shard_map/local_and_first/pallas_call | solution.py:312
  21.4 0.0 copy-start.1
  21.5 3.7 %collective-permute-done.2.far_ref = bf16[128,1536]{1,0:T(8,128)(2,1)S(1)} collective-permute-done((bf16[128,1536]{1,0:T(8,128)(2,1)S(1)}, bf16[128,1536]{1,0:T(8,128)(2,1)S(1)}, u32[]{:S(2)}, u32[]{:S(2)}) %collective-permute-start.2) | collective-permute-done | bytes 393248 | tf_op jit(solution)/shard_map/ppermute | solution.py:286
  25.1 0.0 collective-permute-start.4
  25.1 1.7 %middle.1 = (f32[768,512]{1,0:T(8,128)S(1)}, f32[8,512]{1,0:T(8,128)S(1)}, f32[8,512]{1,0:T(8,128)S(1)}) custom-call(s32[32]{0:T(128)S(1)} %copy-done.2, bf16[512,768]{1,0:T(8,128)(2,1)S(1)} %convolution_convert_fusion.2.q_ref, bf16[128,1536]{1,0:T(8,128)(2,1)S(1)} %collective-permute-done.2.far_ref, ...), custom_call_target="tpu_custom_call", output_to_operand_aliasing={{0}: (3, {}), {1}: (4, {}), {2}: (5, {})} | custom-call | flops 500000000 | bytes 5000000 | tf_op jit(solution)/shard_map/middle/pallas_call | solution.py:323
  26.8 0.0 collective-permute-done.4.far_ref
  26.8 0.0 copy-done.1
  26.9 3.7 %last_and_output.1 = bf16[512,1536]{1,0:T(8,128)(2,1)} custom-call(s32[32]{0:T(128)S(1)} %copy-done.2, bf16[512,768]{1,0:T(8,128)(2,1)S(1)} %convolution_convert_fusion.2.q_ref, bf16[128,1536]{1,0:T(8,128)(2,1)S(1)} %collective-permute-done.4.far_ref, f32[768,512]{1,0:T(8,128)S(1)} %get-tuple-element.44.acc_in, f32[8,512]{1,0:T(8,128)S(1)} %get-tuple-element.45.m_in, ...), custom_call_target="tpu_custom_call" | custom-call | flops 1700000000 | bytes 8000000 | tf_op jit(solution)/shard_map/last_and_output/pallas_call | solution.py:333
  (2 shorter events, 0.0 us)
Async XLA Ops:
  0.0 8.0 %copy-start = (bf16[1536,768]{1,0:T(8,128)(2,1)S(1)}, bf16[1536,768]{1,0:T(8,128)(2,1)}, u32[]{:S(2)}) copy-start(bf16[1536,768]{1,0:T(8,128)(2,1)} %param.10) | copy-start | bytes 7077892
  3.9 7.2 %collective-permute-start = (bf16[32,1536]{1,0:T(8,128)(2,1)S(1)}, bf16[32,1536]{1,0:T(8,128)(2,1)S(1)}, u32[]{:S(2)}, u32[]{:S(2)}) collective-permute-start(bf16[32,1536]{1,0:T(8,128)(2,1)S(1)} %get-tuple-element.27), channel_id=1, source_target_pairs={{0,8},{1,5},{2,10},{3,7},{4,12},{5,1},{6,14},{7,3},{8,0},{9,13},{1... | collective-permute-start | bytes 294920 | tf_op jit(solution)/shard_map/ppermute | solution.py:286
  8.0 1.7 %copy-start.3 = (bf16[1536,768]{1,0:T(8,128)(2,1)S(1)}, bf16[1536,768]{1,0:T(8,128)(2,1)}, u32[]{:S(2)}) copy-start(bf16[1536,768]{1,0:T(8,128)(2,1)} %wk_hbm.1) | copy-start | bytes 7077892
  9.7 3.0 %copy-start.4 = (bf16[1536,768]{1,0:T(8,128)(2,1)S(1)}, bf16[1536,768]{1,0:T(8,128)(2,1)}, u32[]{:S(2)}) copy-start(bf16[1536,768]{1,0:T(8,128)(2,1)} %wv_hbm.1) | copy-start | bytes 7077892
  11.1 7.6 %copy-start.2 = (s32[32]{0:T(128)S(1)}, s32[32]{0:T(128)}, u32[]{:S(2)}) copy-start(s32[32]{0:T(128)} %time_ref.5) | copy-start | bytes 388
  11.1 5.7 %collective-permute-start.1 = (bf16[64,1536]{1,0:T(8,128)(2,1)S(1)}, bf16[64,1536]{1,0:T(8,128)(2,1)S(1)}, u32[]{:S(2)}, u32[]{:S(2)}) collective-permute-start(bf16[64,1536]{1,0:T(8,128)(2,1)S(1)} %pad_maximum_fusion.1), channel_id=1, source_target_pairs={{0,2},{1,9},{2,0},{3,11},{4,6},{5,13},{6,4},{7,15},{8,10},{9,1},{1... | collective-permute-start | bytes 589832 | tf_op jit(solution)/shard_map/ppermute | solution.py:286
  16.9 1.8 %collective-permute-start.3 = (bf16[128,1536]{1,0:T(8,128)(2,1)S(1)}, bf16[128,1536]{1,0:T(8,128)(2,1)S(1)}, u32[]{:S(2)}, u32[]{:S(2)}) collective-permute-start(bf16[128,1536]{1,0:T(8,128)(2,1)S(1)} %pad_maximum_fusion.near_ref), channel_id=1, source_target_pairs={{0,1},{1,0},{2,3},{3,2},{4,5},{5,4},{6,7},{7,6},{8,9},{9,8},{10,11... | collective-permute-start | bytes 1179656 | tf_op jit(solution)/shard_map/ppermute | solution.py:286
  17.3 7.8 %collective-permute-start.2 = (bf16[128,1536]{1,0:T(8,128)(2,1)S(1)}, bf16[128,1536]{1,0:T(8,128)(2,1)S(1)}, u32[]{:S(2)}, u32[]{:S(2)}) collective-permute-start(bf16[128,1536]{1,0:T(8,128)(2,1)S(1)} %pad_maximum_fusion.near_ref), channel_id=1, source_target_pairs={{0,4},{1,3},{2,6},{3,1},{4,0},{5,7},{6,2},{7,5},{8,12},{9,11},{10,... | collective-permute-start | bytes 1179656 | tf_op jit(solution)/shard_map/ppermute | solution.py:286
  21.4 5.4 %copy-start.1 = (bf16[768,1536]{1,0:T(8,128)(2,1)S(1)}, bf16[768,1536]{1,0:T(8,128)(2,1)}, u32[]{:S(2)}) copy-start(bf16[768,1536]{1,0:T(8,128)(2,1)} %wo_ref.1) | copy-start | bytes 7077892
  25.1 1.7 %collective-permute-start.4 = (bf16[128,1536]{1,0:T(8,128)(2,1)S(1)}, bf16[128,1536]{1,0:T(8,128)(2,1)S(1)}, u32[]{:S(2)}, u32[]{:S(2)}) collective-permute-start(bf16[128,1536]{1,0:T(8,128)(2,1)S(1)} %collective-permute-done.2.far_ref), channel_id=1, source_target_pairs={{0,1},{1,0},{2,3},{3,2},{4,5},{5,4},{6,7},{7,6},{8,9},{9,8},{10,11... | collective-permute-start | bytes 1179656 | tf_op jit(solution)/shard_map/ppermute | solution.py:286

commit v4 on v3

--- a/solution.py
+++ b/solution.py
@@ -21,7 +21,6 @@
 F32 = jnp.float32
 BF16 = jnp.bfloat16
 VMEM = pl.BlockSpec(memory_space=pltpu.VMEM)
-SMEM = pl.BlockSpec(memory_space=pltpu.SMEM)
 HBM = pl.BlockSpec(memory_space=pl.ANY)
 
 
@@ -36,12 +35,24 @@
 
 
 def norm_kernel(
-    frames_hbm, gain_hbm, wk_hbm, wv_hbm, normed_ref, pooled_ref, x_buf, gain_buf, wk_buf, wv_buf, x_sem, g_sem, w_sem
+    mask_groups,
+    frames_hbm,
+    time_hbm,
+    gain_hbm,
+    wk_hbm,
+    wv_hbm,
+    normed_ref,
+    pooled_ref,
+    *rest,
 ):
+    bias_refs = rest[: len(mask_groups)]
+    x_buf, time_ref, gain_buf, wk_buf, wv_buf, x_sem, t_sem, g_sem, w_sem = rest[len(mask_groups) :]
     rows, width = x_buf.shape
     parts = x_sem.shape[0]
     step = rows // parts
     gain_load = pltpu.make_async_copy(gain_hbm, gain_buf.at[0], g_sem)
+    time_load = pltpu.make_async_copy(time_hbm, time_ref, t_sem)
+    time_load.start()
     loads = [
         pltpu.make_async_copy(frames_hbm.at[pl.ds(i * step, step)], x_buf.at[pl.ds(i * step, step)], x_sem.at[i])
         for i in range(parts)
@@ -54,6 +65,9 @@
         copy.start()
     gain_load.start()
     weights[0].start()
+    time_load.wait()
+    for masks, bias_ref in zip(mask_groups, bias_refs):
+        mask_columns(time_ref, masks, rows // TOKENS, bias_ref)
     pair = 2 * WW
     per_window = WIN * WIN
     for i in range(parts):
@@ -92,31 +106,35 @@
         pooled_ref[:, i * cols : (i + 1) * cols] = (z[:out_rows] + z[out_rows:]).astype(BF16)
 
 
-def norm_and_pool(frames, gain, w_key, w_value):
+def norm_and_pool(mask_groups, frames, frame_time, gain, w_key, w_value):
     rows, width = frames.shape
     out_rows = rows // TOKENS * SLOTS
     cols = HEADS * HD
+    biases = tuple(jax.ShapeDtypeStruct((len(masks) * out_rows, HD), BF16) for masks in mask_groups)
     return pl.pallas_call(
-        norm_kernel,
+        functools.partial(norm_kernel, mask_groups),
         out_shape=(
             jax.ShapeDtypeStruct((rows, width), BF16),
             jax.ShapeDtypeStruct((out_rows, 2 * cols), BF16),
+            *biases,
         ),
-        in_specs=[HBM] * 4,
-        out_specs=(VMEM, VMEM),
+        in_specs=[HBM] * 5,
+        out_specs=(VMEM,) * (2 + len(biases)),
         scratch_shapes=[
             pltpu.VMEM((rows, width), BF16),
+            pltpu.SMEM(frame_time.shape, jnp.int32),
             pltpu.VMEM((1, width), F32),
             pltpu.VMEM((width, cols), BF16),
             pltpu.VMEM((width, cols), BF16),
             pltpu.SemaphoreType.DMA((2,)),
+            pltpu.SemaphoreType.DMA,
             pltpu.SemaphoreType.DMA,
             pltpu.SemaphoreType.DMA((2,)),
         ],
         compiler_params=pltpu.CompilerParams(vmem_limit_bytes=24 << 20),
         cost_estimate=pl.CostEstimate(flops=400_000_000, bytes_accessed=8_000_000, transcendentals=0),
         name="norm_and_pool",
-    )(*(pltpu.with_memory_space_constraint(x, pltpu.HBM) for x in (frames, gain, w_key, w_value)))
+    )(*(pltpu.with_memory_space_constraint(x, pltpu.HBM) for x in (frames, frame_time, gain, w_key, w_value)))
 
 
 def own_block(me, mask_pair):
@@ -124,20 +142,18 @@
     return me ^ (a if a == b else jnp.where(me % 2 == 0, a, b))
 
 
-def mask_columns(time_ref, masks, count):
+def mask_columns(time_ref, masks, count, bias_ref):
     me = lax.axis_index("tm")
     lane = lax.broadcasted_iota(jnp.int32, (SLOTS, HD), 1)
     own = [time_ref[me * count + f] for f in range(count)]
-    tiles = []
-    for pair in masks:
+    for i, pair in enumerate(masks):
         source = own_block(me, pair)
         for g in range(count):
             t = time_ref[source * count + g]
             tile = jnp.zeros((SLOTS, HD), F32)
             for f in range(count):
                 tile = jnp.where(lane == f, jnp.where(t < own[f], 0.0, FAR), tile)
-            tiles.append(tile)
-    return jnp.concatenate(tiles, axis=0).astype(BF16)
+            bias_ref[pl.ds((i * count + g) * SLOTS, SLOTS), :] = tile.astype(BF16)
 
 
 def frame_columns(tokens):
@@ -158,11 +174,11 @@
     return slice(base + h * HD, base + (h + 1) * HD)
 
 
-def first_kernel(masks, time_ref, q_ref, k_ref, v_ref, near_ref, other_ref, acc_ref, m_ref, l_ref):
+def first_kernel(bias_ref, q_ref, k_ref, v_ref, near_ref, other_ref, acc_ref, m_ref, l_ref):
     tokens = q_ref.shape[0]
     per_window = WIN * WIN
     cols = HEADS * HD
-    bias = mask_columns(time_ref, masks, tokens // TOKENS)
+    bias = bias_ref[...]
     frames = frame_columns(tokens)
     left = lax.broadcasted_iota(jnp.int32, (per_window, 2 * per_window), 1) < per_window
     pairs = [slice(w, w + 2 * per_window) for w in range(0, tokens, 2 * per_window)]
@@ -209,10 +225,10 @@
     mix(HEADS - 1, *weights.pop(HEADS - 1))
 
 
-def far_stages(masks, time_ref, q_ref, far_ref, m_in, l_in, acc_in, keep_state, keep_acc):
+def far_stages(bias_ref, q_ref, far_ref, m_in, l_in, acc_in, keep_state, keep_acc):
     tokens = q_ref.shape[0]
     cols = HEADS * HD
-    bias = mask_columns(time_ref, masks, tokens // TOKENS)
+    bias = bias_ref[...]
     frames = frame_columns(tokens)
 
     def scores(h):
@@ -233,7 +249,7 @@
     pipelined(scores, weigh, mix)
 
 
-def middle_kernel(masks, time_ref, q_ref, far_ref, acc_in, m_in, l_in, acc_ref, m_ref, l_ref):
+def middle_kernel(bias_ref, q_ref, far_ref, acc_in, m_in, l_in, acc_ref, m_ref, l_ref):
     def keep_state(h, top, total):
         m_ref[h : h + 1, :] = top
         l_ref[h : h + 1, :] = total
@@ -241,11 +257,11 @@
     def keep_acc(h, acc, _):
         acc_ref[head(h), :] = acc
 
-    far_stages(masks, time_ref, q_ref, far_ref, m_in, l_in, acc_in, keep_state, keep_acc)
+    far_stages(bias_ref, q_ref, far_ref, m_in, l_in, acc_in, keep_state, keep_acc)
 
 
 def last_kernel(
-    masks, time_ref, q_ref, far_ref, acc_in, m_in, l_in, wo_ref, out_hbm, rows_buf, out_buf, out_sem
+    bias_ref, q_ref, far_ref, acc_in, m_in, l_in, wo_ref, out_hbm, rows_buf, out_buf, out_sem
 ):
     tokens = q_ref.shape[0]
     per_window = WIN * WIN
@@ -261,7 +277,7 @@
             rows_buf[pl.ds(row * WW, WW), head(h)] = line.astype(BF16)
 
     far_stages(
-        masks, time_ref, q_ref, far_ref, m_in, l_in, acc_in, lambda h, top, total: 1.0 / total, keep_acc
+        bias_ref, q_ref, far_ref, m_in, l_in, acc_in, lambda h, top, total: 1.0 / total, keep_acc
     )
     chunks = out_sem.shape[0]
     width = out_buf.shape[1] // chunks
@@ -279,7 +295,11 @@
     rows = frames_in.shape[0]
     cols = HEADS * HD
     phases, held = exchange_plan(n)
-    normed, block = norm_and_pool(frames_in, norm_gain, w_key, w_value)
+    half = len(held[0]) // 2
+    own = list(zip(held[0], held[1]))
+    far = [(a ^ 1, b ^ 1) for b, a in own]
+    groups = (own[:half] + far[:half], own[half:], far[half:])
+    normed, block, *bias = norm_and_pool(groups, frames_in, frame_time, norm_gain, w_key, w_value)
     block, w_query, w_key, w_value = lax.optimization_barrier((block, w_query, w_key, w_value))
 
     def send(x, pair):
@@ -287,21 +307,18 @@
 
     projected = []
     weights = [w_query, w_key, w_value]
-    share = -(-len(weights) // max(len(phases) - 1, 1))
     for i, pair in enumerate(phases[:-1]):
-        block = jnp.concatenate([block, send(block, pair)], axis=0)
-        take = 1 if i == 0 else share
+        came = send(block, pair)
+        take = 1 if i == 0 else len(weights)
         done = [jnp.dot(normed, w, preferred_element_type=F32).astype(BF16) for w in weights[:take]]
         weights = weights[take:]
-        block, *done = lax.optimization_barrier((block, *done))
+        block = jnp.concatenate([block, came], axis=0)
+        block, normed, *done = lax.optimization_barrier((block, normed, *done))
         projected += done
     projected += [jnp.dot(normed, w, preferred_element_type=F32).astype(BF16) for w in weights]
     query, keys, values = projected
     late = send(block, phases[-1])
     other = send(block, (1, 1))
-    half = len(held[0]) // 2
-    own = list(zip(held[0], held[1]))
-    far = [(a ^ 1, b ^ 1) for b, a in own]
 
     state = (
         jax.ShapeDtypeStruct((cols, rows), F32),
@@ -310,30 +327,30 @@
     )
     params = pltpu.CompilerParams(vmem_limit_bytes=32 << 20)
     acc, m, l = pl.pallas_call(
-        functools.partial(first_kernel, own[:half] + far[:half]),
+        first_kernel,
         out_shape=state,
-        in_specs=[SMEM] + [VMEM] * 5,
+        in_specs=[VMEM] * 6,
         out_specs=(VMEM, VMEM, VMEM),
         compiler_params=params,
         cost_estimate=pl.CostEstimate(flops=900_000_000, bytes_accessed=5_000_000, transcendentals=1_000_000),
         name="local_and_first",
-    )(frame_time, query, keys, values, block, other)
+    )(bias[0], query, keys, values, block, other)
     late, acc, m, l = lax.optimization_barrier((late, acc, m, l))
     other_late = send(late, (1, 1))
     acc, m, l = pl.pallas_call(
-        functools.partial(middle_kernel, own[half:]),
+        middle_kernel,
         out_shape=state,
-        in_specs=[SMEM] + [VMEM] * 5,
+        in_specs=[VMEM] * 6,
         out_specs=(VMEM, VMEM, VMEM),
         input_output_aliases={3: 0, 4: 1, 5: 2},
         compiler_params=params,
         cost_estimate=pl.CostEstimate(flops=500_000_000, bytes_accessed=5_000_000, transcendentals=400_000),
         name="middle",
-    )(frame_time, query, late, acc, m, l)
+    )(bias[1], query, late, acc, m, l)
     return pl.pallas_call(
-        functools.partial(last_kernel, far[half:]),
+        last_kernel,
         out_shape=jax.ShapeDtypeStruct((rows, w_output.shape[1]), BF16),
-        in_specs=[SMEM] + [VMEM] * 6,
+        in_specs=[VMEM] * 7,
         out_specs=HBM,
         scratch_shapes=[
             pltpu.VMEM((rows, cols), BF16),
@@ -343,7 +360,7 @@
         compiler_params=params,
         cost_estimate=pl.CostEstimate(flops=1_700_000_000, bytes_accessed=8_000_000, transcendentals=400_000),
         name="last_and_output",
-    )(frame_time, query, other_late, acc, m, l, w_output)
+    )(bias[2], query, other_late, acc, m, l, w_output)
 
 
 def solution(mesh):

time: 30.7 us -> 29.4 us (0.958)
  Pallas kernels: 12 us -> 10.3 us
  starting transfers between devices: 7.41 us -> 8.25 us
    pallas_call x4, Pallas kernels: 12 us -> 10.3 us  [the longest x1 3.91 us: norm_and_pool(): pl.pallas_call(functools.partial(norm_kernel, mask_groups), out_shape=(ja...]
    ppermute x5, starting transfers between devices: 7.41 us -> 8.25 us  [send(): return lax.ppermute(x, 'tm', [(i, i ^ pair[i % 2]) for i in range(n)])]
  transfers between devices with their start and end apart: 5 -> 5, of which waited for: 3 -> 4; matrix products, arithmetic and copies ran while one was open for 14% -> 14% of each run, Pallas kernels for 15% -> 11%
where the time goes in v4:
time: 29.4 us; the launch traced here: 29.2 us
  Pallas kernels  10.3 us (35%)
  starting transfers between devices  8.25 us (28%)
  waiting for transfers between devices  6.33 us (22%)
  matrix products  4.14 us (14%)
    ppermute x5, starting transfers between devices, send(): return lax.ppermute(x, 'tm', [(i, i ^ pair[i % 2]) for i in range(n)])  8.25 us
    ppermute x5, waiting for transfers between devices, send(): return lax.ppermute(x, 'tm', [(i, i ^ pair[i % 2]) for i in range(n)])  6.33 us
    dot_general x3, matrix products, on_device(): jnp.dot(normed, w, preferred_element_type=F32).astype(BF16)  4.14 us
    pallas_call x1, Pallas kernels, norm_and_pool(): pl.pallas_call(functools.partial(norm_kernel, mask_groups), out_shape=(ja...  3.91 us
    pallas_call x1, Pallas kernels, on_device(): pl.pallas_call(last_kernel, out_shape=jax.ShapeDtypeStruct((rows, w_outpu...  3.08 us
    pallas_call x1, Pallas kernels, on_device(): pl.pallas_call(first_kernel, out_shape=state, in_specs=[VMEM] * 6, out_sp...  2.17 us
    pallas_call x1, Pallas kernels, on_device(): pl.pallas_call(middle_kernel, out_shape=state, in_specs=[VMEM] * 6, out_s...  1.15 us
  transfers between devices with their start and end apart: 5, of which 4 were waited for; matrix products, arithmetic and copies ran while one was open for 14% of the time, Pallas kernels for 11%

profile of v4, /device:TPU:0, one launch (start us, length us, event | category | flops | bytes accessed | tf_op | source)
XLA Modules:
  0.0 29.2 jit_solution(11578660447596499123)
XLA Ops:
  0.0 0.0 copy-start
  0.0 3.9 %norm_and_pool.1 = (bf16[512,1536]{1,0:T(8,128)(2,1)S(1)}, bf16[32,1536]{1,0:T(8,128)(2,1)S(1)}, bf16[256,128]{1,0:T(8,128)(2,1)S(1)}, bf16[128,128]{1,0:T(8,128)(2,1)S(1)}, bf16[128,128]{1,0:T(8,128)(2,1)S(1)}) custom-call(bf16[512,1536]{1,0:T(8,128)(2,1)} %frames_hbm.1, s32[32]{0:T(128)} %time_hbm.1, f32[1536]{0:T(1024)} %gain_hbm.1, ...), custom_call_target="tpu_custom_call" | custom-call | flops 400000000 | bytes 8000000 | tf_op jit(solution)/shard_map/norm_and_pool/pallas_call | solution.py:114
  3.9 4.1 %collective-permute-start = (bf16[32,1536]{1,0:T(8,128)(2,1)S(1)}, bf16[32,1536]{1,0:T(8,128)(2,1)S(1)}, u32[]{:S(2)}, u32[]{:S(2)}) collective-permute-start(bf16[32,1536]{1,0:T(8,128)(2,1)S(1)} %get-tuple-element.32), channel_id=1, source_target_pairs={{0,8},{1,5},{2,10},{3,7},{4,12},{5,1},{6,14},{7,3},{8,0},{9,13},{1... | collective-permute-start | bytes 294920 | tf_op jit(solution)/shard_map/ppermute | solution.py:306
  8.0 0.0 copy-done
  8.0 0.0 copy-start.2
  8.0 1.4 %convolution_convert_fusion.2.q_ref = bf16[512,768]{1,0:T(8,128)(2,1)S(1)} fusion(bf16[512,1536]{1,0:T(8,128)(2,1)S(1)} %get-tuple-element.37, bf16[1536,768]{1,0:T(8,128)(2,1)S(1)} %copy-done), kind=kOutput, calls=%fused_computation.2 | convolution fusion | flops 1208352768 | bytes 4718592 | tf_op jit(solution)/shard_map/dot_general | solution.py:313
  9.4 1.2 %collective-permute-done = bf16[32,1536]{1,0:T(8,128)(2,1)S(1)} collective-permute-done((bf16[32,1536]{1,0:T(8,128)(2,1)S(1)}, bf16[32,1536]{1,0:T(8,128)(2,1)S(1)}, u32[]{:S(2)}, u32[]{:S(2)}) %collective-permute-start) | collective-permute-done | bytes 98336 | tf_op jit(solution)/shard_map/ppermute | solution.py:306
  10.6 0.0 copy-start.3
  10.6 2.0 %collective-permute-start.1 = (bf16[64,1536]{1,0:T(8,128)(2,1)S(1)}, bf16[64,1536]{1,0:T(8,128)(2,1)S(1)}, u32[]{:S(2)}, u32[]{:S(2)}) collective-permute-start(bf16[64,1536]{1,0:T(8,128)(2,1)S(1)} %pad_maximum_fusion.1), channel_id=1, source_target_pairs={{0,2},{1,9},{2,0},{3,11},{4,6},{5,13},{6,4},{7,15},{8,10},{9,1},{1... | collective-permute-start | bytes 589832 | tf_op jit(solution)/shard_map/ppermute | solution.py:306
  12.6 0.0 copy-done.2
  12.6 1.4 %convolution_convert_fusion.v_ref = bf16[512,768]{1,0:T(8,128)(2,1)S(1)} fusion(bf16[512,1536]{1,0:T(8,128)(2,1)S(1)} %get-tuple-element.37, bf16[1536,768]{1,0:T(8,128)(2,1)S(1)} %copy-done.2), kind=kOutput, calls=%fused_computation | convolution fusion | flops 1208352768 | bytes 4718592 | tf_op jit(solution)/shard_map/dot_general | solution.py:313
  14.0 0.0 copy-done.3
  14.0 1.4 %convolution_convert_fusion.1.k_ref = bf16[512,768]{1,0:T(8,128)(2,1)S(1)} fusion(bf16[512,1536]{1,0:T(8,128)(2,1)S(1)} %get-tuple-element.37, bf16[1536,768]{1,0:T(8,128)(2,1)S(1)} %copy-done.3), kind=kOutput, calls=%fused_computation.1 | convolution fusion | flops 1208352768 | bytes 4718592 | tf_op jit(solution)/shard_map/dot_general | solution.py:313
  15.4 1.0 %collective-permute-done.1 = bf16[64,1536]{1,0:T(8,128)(2,1)S(1)} collective-permute-done((bf16[64,1536]{1,0:T(8,128)(2,1)S(1)}, bf16[64,1536]{1,0:T(8,128)(2,1)S(1)}, u32[]{:S(2)}, u32[]{:S(2)}) %collective-permute-start.1) | collective-permute-done | bytes 196640 | tf_op jit(solution)/shard_map/ppermute | solution.py:306
  16.4 0.1 collective-permute-start.3
  16.5 2.1 %collective-permute-start.2 = (bf16[128,1536]{1,0:T(8,128)(2,1)S(1)}, bf16[128,1536]{1,0:T(8,128)(2,1)S(1)}, u32[]{:S(2)}, u32[]{:S(2)}) collective-permute-start(bf16[128,1536]{1,0:T(8,128)(2,1)S(1)} %pad_maximum_fusion.near_ref), channel_id=1, source_target_pairs={{0,4},{1,3},{2,6},{3,1},{4,0},{5,7},{6,2},{7,5},{8,12},{9,11},{10,... | collective-permute-start | bytes 1179656 | tf_op jit(solution)/shard_map/ppermute | solution.py:306
  18.6 0.0 collective-permute-done.3.other_ref
  18.6 2.2 %local_and_first.1 = (f32[768,512]{1,0:T(8,128)S(1)}, f32[8,512]{1,0:T(8,128)S(1)}, f32[8,512]{1,0:T(8,128)S(1)}) custom-call(bf16[256,128]{1,0:T(8,128)(2,1)S(1)} %get-tuple-element.41.bias_ref, bf16[512,768]{1,0:T(8,128)(2,1)S(1)} %convolution_convert_fusion.2.q_ref, bf16[512,768]{1,0:T(8,128)(2,1)S(1)} %convolution_convert_fusion.1.k_ref, ...), custom_call_target="tpu_custom_call" | custom-call | flops 900000000 | bytes 5000000 | tf_op jit(solution)/shard_map/local_and_first/pallas_call | solution.py:329
  20.8 0.0 copy-start.1
  20.8 3.6 %collective-permute-done.2.far_ref = bf16[128,1536]{1,0:T(8,128)(2,1)S(1)} collective-permute-done((bf16[128,1536]{1,0:T(8,128)(2,1)S(1)}, bf16[128,1536]{1,0:T(8,128)(2,1)S(1)}, u32[]{:S(2)}, u32[]{:S(2)}) %collective-permute-start.2) | collective-permute-done | bytes 393248 | tf_op jit(solution)/shard_map/ppermute | solution.py:306
  24.4 0.0 collective-permute-start.4
  24.4 1.2 %middle.1 = (f32[768,512]{1,0:T(8,128)S(1)}, f32[8,512]{1,0:T(8,128)S(1)}, f32[8,512]{1,0:T(8,128)S(1)}) custom-call(bf16[128,128]{1,0:T(8,128)(2,1)S(1)} %get-tuple-element.48.bias_ref, bf16[512,768]{1,0:T(8,128)(2,1)S(1)} %convolution_convert_fusion.2.q_ref, ...), custom_call_target="tpu_custom_call", output_to_operand_aliasing={{0}: (3, {}), {1}: (4, {}), {2}: (5, {})} | custom-call | flops 500000000 | bytes 5000000 | tf_op jit(solution)/shard_map/middle/pallas_call | solution.py:340
  25.5 0.6 %collective-permute-done.4.far_ref = bf16[128,1536]{1,0:T(8,128)(2,1)S(1)} collective-permute-done((bf16[128,1536]{1,0:T(8,128)(2,1)S(1)}, bf16[128,1536]{1,0:T(8,128)(2,1)S(1)}, u32[]{:S(2)}, u32[]{:S(2)}) %collective-permute-start.4) | collective-permute-done | bytes 393248 | tf_op jit(solution)/shard_map/ppermute | solution.py:306
  26.1 0.0 copy-done.1
  26.1 3.1 %last_and_output.1 = bf16[512,1536]{1,0:T(8,128)(2,1)} custom-call(bf16[128,128]{1,0:T(8,128)(2,1)S(1)} %get-tuple-element.30.bias_ref, bf16[512,768]{1,0:T(8,128)(2,1)S(1)} %convolution_convert_fusion.2.q_ref, bf16[128,1536]{1,0:T(8,128)(2,1)S(1)} %collective-permute-done.4.far_ref, f32[768,512]{1,0:T(8,128)S(1)} %get-tuple-element.52.acc_in, ...), custom_call_target="tpu_custom_call" | custom-call | flops 1700000000 | bytes 8000000 | tf_op jit(solution)/shard_map/last_and_output/pallas_call | solution.py:350
  (2 shorter events, 0.0 us)
Async XLA Ops:
  0.0 8.0 %copy-start = (bf16[1536,768]{1,0:T(8,128)(2,1)S(1)}, bf16[1536,768]{1,0:T(8,128)(2,1)}, u32[]{:S(2)}) copy-start(bf16[1536,768]{1,0:T(8,128)(2,1)} %param.10) | copy-start | bytes 7077892
  3.9 6.7 %collective-permute-start = (bf16[32,1536]{1,0:T(8,128)(2,1)S(1)}, bf16[32,1536]{1,0:T(8,128)(2,1)S(1)}, u32[]{:S(2)}, u32[]{:S(2)}) collective-permute-start(bf16[32,1536]{1,0:T(8,128)(2,1)S(1)} %get-tuple-element.32), channel_id=1, source_target_pairs={{0,8},{1,5},{2,10},{3,7},{4,12},{5,1},{6,14},{7,3},{8,0},{9,13},{1... | collective-permute-start | bytes 294920 | tf_op jit(solution)/shard_map/ppermute | solution.py:306
  8.0 4.6 %copy-start.2 = (bf16[1536,768]{1,0:T(8,128)(2,1)S(1)}, bf16[1536,768]{1,0:T(8,128)(2,1)}, u32[]{:S(2)}) copy-start(bf16[1536,768]{1,0:T(8,128)(2,1)} %wv_hbm.1) | copy-start | bytes 7077892
  10.6 3.4 %copy-start.3 = (bf16[1536,768]{1,0:T(8,128)(2,1)S(1)}, bf16[1536,768]{1,0:T(8,128)(2,1)}, u32[]{:S(2)}) copy-start(bf16[1536,768]{1,0:T(8,128)(2,1)} %wk_hbm.1) | copy-start | bytes 7077892
  10.6 5.7 %collective-permute-start.1 = (bf16[64,1536]{1,0:T(8,128)(2,1)S(1)}, bf16[64,1536]{1,0:T(8,128)(2,1)S(1)}, u32[]{:S(2)}, u32[]{:S(2)}) collective-permute-start(bf16[64,1536]{1,0:T(8,128)(2,1)S(1)} %pad_maximum_fusion.1), channel_id=1, source_target_pairs={{0,2},{1,9},{2,0},{3,11},{4,6},{5,13},{6,4},{7,15},{8,10},{9,1},{1... | collective-permute-start | bytes 589832 | tf_op jit(solution)/shard_map/ppermute | solution.py:306
  16.4 2.2 %collective-permute-start.3 = (bf16[128,1536]{1,0:T(8,128)(2,1)S(1)}, bf16[128,1536]{1,0:T(8,128)(2,1)S(1)}, u32[]{:S(2)}, u32[]{:S(2)}) collective-permute-start(bf16[128,1536]{1,0:T(8,128)(2,1)S(1)} %pad_maximum_fusion.near_ref), channel_id=1, source_target_pairs={{0,1},{1,0},{2,3},{3,2},{4,5},{5,4},{6,7},{7,6},{8,9},{9,8},{10,11... | collective-permute-start | bytes 1179656 | tf_op jit(solution)/shard_map/ppermute | solution.py:306
  16.5 7.9 %collective-permute-start.2 = (bf16[128,1536]{1,0:T(8,128)(2,1)S(1)}, bf16[128,1536]{1,0:T(8,128)(2,1)S(1)}, u32[]{:S(2)}, u32[]{:S(2)}) collective-permute-start(bf16[128,1536]{1,0:T(8,128)(2,1)S(1)} %pad_maximum_fusion.near_ref), channel_id=1, source_target_pairs={{0,4},{1,3},{2,6},{3,1},{4,0},{5,7},{6,2},{7,5},{8,12},{9,11},{10,... | collective-permute-start | bytes 1179656 | tf_op jit(solution)/shard_map/ppermute | solution.py:306
  20.8 5.3 %copy-start.1 = (bf16[768,1536]{1,0:T(8,128)(2,1)S(1)}, bf16[768,1536]{1,0:T(8,128)(2,1)}, u32[]{:S(2)}) copy-start(bf16[768,1536]{1,0:T(8,128)(2,1)} %wo_ref.1) | copy-start | bytes 7077892
  24.4 1.7 %collective-permute-start.4 = (bf16[128,1536]{1,0:T(8,128)(2,1)S(1)}, bf16[128,1536]{1,0:T(8,128)(2,1)S(1)}, u32[]{:S(2)}, u32[]{:S(2)}) collective-permute-start(bf16[128,1536]{1,0:T(8,128)(2,1)S(1)} %collective-permute-done.2.far_ref), channel_id=1, source_target_pairs={{0,1},{1,0},{2,3},{3,2},{4,5},{5,4},{6,7},{7,6},{8,9},{9,8},{10,11... | collective-permute-start | bytes 1179656 | tf_op jit(solution)/shard_map/ppermute | solution.py:306

commit v5 on v4

--- a/solution.py
+++ b/solution.py
@@ -26,12 +26,16 @@
 
 def exchange_plan(n):
     high = [1 << b for b in range(n.bit_length() - 2, 0, -1)]
-    first = [high[0]] + high[2:] + high[1:2]
-    second = high[1:2] + high[:1] + high[2:]
-    held = [[0], [0]]
-    for a, b in zip(first, second):
-        held = [held[0] + [m ^ a for m in held[0]], held[1] + [m ^ b for m in held[1]]]
-    return list(zip(first, second)), held
+    phases = list(zip(high, high[-1:] + high[:-1]))
+    held = []
+    for core in range(2):
+        masks = [0]
+        for pair in phases[:-2]:
+            masks = masks + [m ^ pair[core] for m in masks]
+        before, last = phases[-2][core], phases[-1][core]
+        brought = [m ^ before for m in masks]
+        held.append((masks + brought + [m ^ last for m in masks], [m ^ last for m in brought]))
+    return phases, held
 
 
 def norm_kernel(
@@ -295,31 +299,31 @@
     rows = frames_in.shape[0]
     cols = HEADS * HD
     phases, held = exchange_plan(n)
-    half = len(held[0]) // 2
-    own = list(zip(held[0], held[1]))
-    far = [(a ^ 1, b ^ 1) for b, a in own]
-    groups = (own[:half] + far[:half], own[half:], far[half:])
+    own, own_late = (list(zip(x, y)) for x, y in zip(*held))
+    far, far_late = ([(y ^ 1, x ^ 1) for x, y in masks] for masks in (own, own_late))
+    groups = (own + far, own_late, far_late)
     normed, block, *bias = norm_and_pool(groups, frames_in, frame_time, norm_gain, w_key, w_value)
     block, w_query, w_key, w_value = lax.optimization_barrier((block, w_query, w_key, w_value))
 
     def send(x, pair):
         return lax.ppermute(x, "tm", [(i, i ^ pair[i % 2]) for i in range(n)])
 
-    projected = []
-    weights = [w_query, w_key, w_value]
-    for i, pair in enumerate(phases[:-1]):
+    def project(w):
+        return jnp.dot(normed, w, preferred_element_type=F32).astype(BF16)
+
+    query = None
+    for pair in phases[:-2]:
         came = send(block, pair)
-        take = 1 if i == 0 else len(weights)
-        done = [jnp.dot(normed, w, preferred_element_type=F32).astype(BF16) for w in weights[:take]]
-        weights = weights[take:]
+        query = project(w_query) if query is None else query
         block = jnp.concatenate([block, came], axis=0)
-        block, normed, *done = lax.optimization_barrier((block, normed, *done))
-        projected += done
-    projected += [jnp.dot(normed, w, preferred_element_type=F32).astype(BF16) for w in weights]
-    query, keys, values = projected
-    late = send(block, phases[-1])
+        block, normed, query = lax.optimization_barrier((block, normed, query))
+    brought = send(block, phases[-2])
+    early = send(block, phases[-1])
+    keys, values = project(w_key), project(w_value)
+    brought, early, keys, values = lax.optimization_barrier((brought, early, keys, values))
+    late = send(brought, phases[-1])
+    block = jnp.concatenate([block, brought, early], axis=0)
     other = send(block, (1, 1))
-
     state = (
         jax.ShapeDtypeStruct((cols, rows), F32),
         jax.ShapeDtypeStruct((8, rows), F32),

time: 29.4 us -> 28.7 us (0.976)
  waiting for transfers between devices: 6.33 us -> 4.6 us
  starting transfers between devices: 8.25 us -> 8.86 us
  Pallas kernels: 10.3 us -> 10.8 us
    ppermute x5 -> x6, waiting for transfers between devices: 6.33 us -> 4.6 us  [send(): return lax.ppermute(x, 'tm', [(i, i ^ pair[i % 2]) for i in range(n)])]
    pallas_call x1, Pallas kernels: 2.17 us -> 2.86 us  [on_device(): pl.pallas_call(first_kernel, out_shape=state, in_specs=[VMEM] * 6, out_sp...]
    ppermute x5 -> x6, starting transfers between devices: 8.25 us -> 8.86 us  [send(): return lax.ppermute(x, 'tm', [(i, i ^ pair[i % 2]) for i in range(n)])]
  transfers between devices with their start and end apart: 5 -> 6, of which waited for: 4 -> 5; matrix products, arithmetic and copies ran while one was open for 14% -> 15% of each run, Pallas kernels for 11% -> 14%
where the time goes in v5:
time: 28.7 us; the launch traced here: 28.6 us
  Pallas kernels  10.8 us (38%)
  starting transfers between devices  8.86 us (31%)
  waiting for transfers between devices  4.6 us (16%)
  matrix products  4.14 us (14%)
    ppermute x6, starting transfers between devices, send(): return lax.ppermute(x, 'tm', [(i, i ^ pair[i % 2]) for i in range(n)])  8.86 us
    ppermute x6, waiting for transfers between devices, send(): return lax.ppermute(x, 'tm', [(i, i ^ pair[i % 2]) for i in range(n)])  4.6 us
    dot_general x3, matrix products, project(): return jnp.dot(normed, w, preferred_element_type=F32).astype(BF16)  4.14 us
    pallas_call x1, Pallas kernels, norm_and_pool(): pl.pallas_call(functools.partial(norm_kernel, mask_groups), out_shape=(ja...  3.91 us
    pallas_call x1, Pallas kernels, on_device(): pl.pallas_call(last_kernel, out_shape=jax.ShapeDtypeStruct((rows, w_outpu...  2.97 us
    pallas_call x1, Pallas kernels, on_device(): pl.pallas_call(first_kernel, out_shape=state, in_specs=[VMEM] * 6, out_sp...  2.86 us
    pallas_call x1, Pallas kernels, on_device(): pl.pallas_call(middle_kernel, out_shape=state, in_specs=[VMEM] * 6, out_s...  1.06 us
  transfers between devices with their start and end apart: 6, of which 5 were waited for; matrix products, arithmetic and copies ran while one was open for 15% of the time, Pallas kernels for 14%

profile of v5, /device:TPU:0, one launch (start us, length us, event | category | flops | bytes accessed | tf_op | source)
XLA Modules:
  0.0 28.6 jit_solution(122634664425431451)
XLA Ops:
  0.0 0.0 copy-start
  0.0 3.9 %norm_and_pool.1 = (bf16[512,1536]{1,0:T(8,128)(2,1)S(1)}, bf16[32,1536]{1,0:T(8,128)(2,1)S(1)}, bf16[384,128]{1,0:T(8,128)(2,1)S(1)}, bf16[64,128]{1,0:T(8,128)(2,1)S(1)}, bf16[64,128]{1,0:T(8,128)(2,1)S(1)}) custom-call(bf16[512,1536]{1,0:T(8,128)(2,1)} %frames_hbm.1, s32[32]{0:T(128)} %time_hbm.1, f32[1536]{0:T(1024)} %gain_hbm.1, ...), custom_call_target="tpu_custom_call" | custom-call | flops 400000000 | bytes 8000000 | tf_op jit(solution)/shard_map/norm_and_pool/pallas_call | solution.py:118
  3.9 4.1 %collective-permute-start = (bf16[32,1536]{1,0:T(8,128)(2,1)S(1)}, bf16[32,1536]{1,0:T(8,128)(2,1)S(1)}, u32[]{:S(2)}, u32[]{:S(2)}) collective-permute-start(bf16[32,1536]{1,0:T(8,128)(2,1)S(1)} %get-tuple-element.33), channel_id=1, source_target_pairs={{0,8},{1,3},{2,10},{3,1},{4,12},{5,7},{6,14},{7,5},{8,0},{9,11},{1... | collective-permute-start | bytes 294920 | tf_op jit(solution)/shard_map/ppermute | solution.py:309
  8.0 0.0 copy-done
  8.0 0.0 copy-start.2
  8.0 1.4 %convolution_convert_fusion.2.q_ref = bf16[512,768]{1,0:T(8,128)(2,1)S(1)} fusion(bf16[512,1536]{1,0:T(8,128)(2,1)S(1)} %get-tuple-element.38, bf16[1536,768]{1,0:T(8,128)(2,1)S(1)} %copy-done), kind=kOutput, calls=%fused_computation.2 | convolution fusion | flops 1208352768 | bytes 4718592 | tf_op jit(solution)/shard_map/dot_general | solution.py:312
  9.4 1.2 %collective-permute-done = bf16[32,1536]{1,0:T(8,128)(2,1)S(1)} collective-permute-done((bf16[32,1536]{1,0:T(8,128)(2,1)S(1)}, bf16[32,1536]{1,0:T(8,128)(2,1)S(1)}, u32[]{:S(2)}, u32[]{:S(2)}) %collective-permute-start) | collective-permute-done | bytes 98336 | tf_op jit(solution)/shard_map/ppermute | solution.py:309
  10.6 0.0 copy-start.3
  10.6 1.9 %collective-permute-start.2 = (bf16[64,1536]{1,0:T(8,128)(2,1)S(1)}, bf16[64,1536]{1,0:T(8,128)(2,1)S(1)}, u32[]{:S(2)}, u32[]{:S(2)}) collective-permute-start(bf16[64,1536]{1,0:T(8,128)(2,1)S(1)} %pad_maximum_fusion), channel_id=1, source_target_pairs={{0,2},{1,5},{2,0},{3,7},{4,6},{5,1},{6,4},{7,3},{8,10},{9,13},{10,... | collective-permute-start | bytes 589832 | tf_op jit(solution)/shard_map/ppermute | solution.py:309
  12.6 1.7 %collective-permute-start.1 = (bf16[64,1536]{1,0:T(8,128)(2,1)S(1)}, bf16[64,1536]{1,0:T(8,128)(2,1)S(1)}, u32[]{:S(2)}, u32[]{:S(2)}) collective-permute-start(bf16[64,1536]{1,0:T(8,128)(2,1)S(1)} %pad_maximum_fusion), channel_id=1, source_target_pairs={{0,4},{1,9},{2,6},{3,11},{4,0},{5,13},{6,2},{7,15},{8,12},{9,1},{1... | collective-permute-start | bytes 589832 | tf_op jit(solution)/shard_map/ppermute | solution.py:309
  14.3 0.0 copy-done.2
  14.3 1.4 %convolution_convert_fusion.v_ref = bf16[512,768]{1,0:T(8,128)(2,1)S(1)} fusion(bf16[512,1536]{1,0:T(8,128)(2,1)S(1)} %get-tuple-element.38, bf16[1536,768]{1,0:T(8,128)(2,1)S(1)} %copy-done.2), kind=kOutput, calls=%fused_computation | convolution fusion | flops 1208352768 | bytes 4718592 | tf_op jit(solution)/shard_map/dot_general | solution.py:312
  15.7 0.0 copy-done.3
  15.7 1.4 %convolution_convert_fusion.1.k_ref = bf16[512,768]{1,0:T(8,128)(2,1)S(1)} fusion(bf16[512,1536]{1,0:T(8,128)(2,1)S(1)} %get-tuple-element.38, bf16[1536,768]{1,0:T(8,128)(2,1)S(1)} %copy-done.3), kind=kOutput, calls=%fused_computation.1 | convolution fusion | flops 1208352768 | bytes 4718592 | tf_op jit(solution)/shard_map/dot_general | solution.py:312
  17.1 0.0 collective-permute-done.2
  17.1 1.2 %collective-permute-done.1 = bf16[64,1536]{1,0:T(8,128)(2,1)S(1)} collective-permute-done((bf16[64,1536]{1,0:T(8,128)(2,1)S(1)}, bf16[64,1536]{1,0:T(8,128)(2,1)S(1)}, u32[]{:S(2)}, u32[]{:S(2)}) %collective-permute-start.1) | collective-permute-done | bytes 196640 | tf_op jit(solution)/shard_map/ppermute | solution.py:309
  18.3 0.1 collective-permute-start.4
  18.4 1.0 %collective-permute-start.3 = (bf16[64,1536]{1,0:T(8,128)(2,1)S(1)}, bf16[64,1536]{1,0:T(8,128)(2,1)S(1)}, u32[]{:S(2)}, u32[]{:S(2)}) collective-permute-start(bf16[64,1536]{1,0:T(8,128)(2,1)S(1)} %collective-permute-done.1), channel_id=1, source_target_pairs={{0,2},{1,5},{2,0},{3,7},{4,6},{5,1},{6,4},{7,3},{8,10},{9,13},{10,... | collective-permute-start | bytes 589832 | tf_op jit(solution)/shard_map/ppermute | solution.py:309
  19.5 0.9 %collective-permute-done.4.other_ref = bf16[192,1536]{1,0:T(8,128)(2,1)S(1)} collective-permute-done((bf16[192,1536]{1,0:T(8,128)(2,1)S(1)}, bf16[192,1536]{1,0:T(8,128)(2,1)S(1)}, u32[]{:S(2)}, u32[]{:S(2)}) %collective-permute-start.4) | collective-permute-done | bytes 589856 | tf_op jit(solution)/shard_map/ppermute | solution.py:309
  20.4 2.9 %local_and_first.1 = (f32[768,512]{1,0:T(8,128)S(1)}, f32[8,512]{1,0:T(8,128)S(1)}, f32[8,512]{1,0:T(8,128)S(1)}) custom-call(bf16[384,128]{1,0:T(8,128)(2,1)S(1)} %get-tuple-element.42.bias_ref, bf16[512,768]{1,0:T(8,128)(2,1)S(1)} %convolution_convert_fusion.2.q_ref, bf16[512,768]{1,0:T(8,128)(2,1)S(1)} %convolution_convert_fusion.1.k_ref, ...), custom_call_target="tpu_custom_call" | custom-call | flops 900000000 | bytes 5000000 | tf_op jit(solution)/shard_map/local_and_first/pallas_call | solution.py:333
  23.3 0.0 copy-start.1
  23.3 0.9 %collective-permute-done.3.far_ref = bf16[64,1536]{1,0:T(8,128)(2,1)S(1)} collective-permute-done((bf16[64,1536]{1,0:T(8,128)(2,1)S(1)}, bf16[64,1536]{1,0:T(8,128)(2,1)S(1)}, u32[]{:S(2)}, u32[]{:S(2)}) %collective-permute-start.3) | collective-permute-done | bytes 196640 | tf_op jit(solution)/shard_map/ppermute | solution.py:309
  24.2 0.0 collective-permute-start.5
  24.2 1.1 %middle.1 = (f32[768,512]{1,0:T(8,128)S(1)}, f32[8,512]{1,0:T(8,128)S(1)}, f32[8,512]{1,0:T(8,128)S(1)}) custom-call(bf16[64,128]{1,0:T(8,128)(2,1)S(1)} %get-tuple-element.50.bias_ref, bf16[512,768]{1,0:T(8,128)(2,1)S(1)} %convolution_convert_fusion.2.q_ref, ...), custom_call_target="tpu_custom_call", output_to_operand_aliasing={{0}: (3, {}), {1}: (4, {}), {2}: (5, {})} | custom-call | flops 500000000 | bytes 5000000 | tf_op jit(solution)/shard_map/middle/pallas_call | solution.py:344
  25.2 0.4 %collective-permute-done.5.far_ref = bf16[64,1536]{1,0:T(8,128)(2,1)S(1)} collective-permute-done((bf16[64,1536]{1,0:T(8,128)(2,1)S(1)}, bf16[64,1536]{1,0:T(8,128)(2,1)S(1)}, u32[]{:S(2)}, u32[]{:S(2)}) %collective-permute-start.5) | collective-permute-done | bytes 196640 | tf_op jit(solution)/shard_map/ppermute | solution.py:309
  25.6 0.0 copy-done.1
  25.6 3.0 %last_and_output.1 = bf16[512,1536]{1,0:T(8,128)(2,1)} custom-call(bf16[64,128]{1,0:T(8,128)(2,1)S(1)} %get-tuple-element.31.bias_ref, bf16[512,768]{1,0:T(8,128)(2,1)S(1)} %convolution_convert_fusion.2.q_ref, bf16[64,1536]{1,0:T(8,128)(2,1)S(1)} %collective-permute-done.5.far_ref, f32[768,512]{1,0:T(8,128)S(1)} %get-tuple-element.54.acc_in, ...), custom_call_target="tpu_custom_call" | custom-call | flops 1700000000 | bytes 8000000 | tf_op jit(solution)/shard_map/last_and_output/pallas_call | solution.py:354
  (4 shorter events, 0.1 us)
Async XLA Ops:
  0.0 8.0 %copy-start = (bf16[1536,768]{1,0:T(8,128)(2,1)S(1)}, bf16[1536,768]{1,0:T(8,128)(2,1)}, u32[]{:S(2)}) copy-start(bf16[1536,768]{1,0:T(8,128)(2,1)} %param.10) | copy-start | bytes 7077892
  3.9 6.7 %collective-permute-start = (bf16[32,1536]{1,0:T(8,128)(2,1)S(1)}, bf16[32,1536]{1,0:T(8,128)(2,1)S(1)}, u32[]{:S(2)}, u32[]{:S(2)}) collective-permute-start(bf16[32,1536]{1,0:T(8,128)(2,1)S(1)} %get-tuple-element.33), channel_id=1, source_target_pairs={{0,8},{1,3},{2,10},{3,1},{4,12},{5,7},{6,14},{7,5},{8,0},{9,11},{1... | collective-permute-start | bytes 294920 | tf_op jit(solution)/shard_map/ppermute | solution.py:309
  8.0 6.3 %copy-start.2 = (bf16[1536,768]{1,0:T(8,128)(2,1)S(1)}, bf16[1536,768]{1,0:T(8,128)(2,1)}, u32[]{:S(2)}) copy-start(bf16[1536,768]{1,0:T(8,128)(2,1)} %wv_hbm.1) | copy-start | bytes 7077892
  10.6 5.0 %copy-start.3 = (bf16[1536,768]{1,0:T(8,128)(2,1)S(1)}, bf16[1536,768]{1,0:T(8,128)(2,1)}, u32[]{:S(2)}) copy-start(bf16[1536,768]{1,0:T(8,128)(2,1)} %wk_hbm.1) | copy-start | bytes 7077892
  10.6 6.5 %collective-permute-start.2 = (bf16[64,1536]{1,0:T(8,128)(2,1)S(1)}, bf16[64,1536]{1,0:T(8,128)(2,1)S(1)}, u32[]{:S(2)}, u32[]{:S(2)}) collective-permute-start(bf16[64,1536]{1,0:T(8,128)(2,1)S(1)} %pad_maximum_fusion), channel_id=1, source_target_pairs={{0,2},{1,5},{2,0},{3,7},{4,6},{5,1},{6,4},{7,3},{8,10},{9,13},{10,... | collective-permute-start | bytes 589832 | tf_op jit(solution)/shard_map/ppermute | solution.py:309
  12.6 5.7 %collective-permute-start.1 = (bf16[64,1536]{1,0:T(8,128)(2,1)S(1)}, bf16[64,1536]{1,0:T(8,128)(2,1)S(1)}, u32[]{:S(2)}, u32[]{:S(2)}) collective-permute-start(bf16[64,1536]{1,0:T(8,128)(2,1)S(1)} %pad_maximum_fusion), channel_id=1, source_target_pairs={{0,4},{1,9},{2,6},{3,11},{4,0},{5,13},{6,2},{7,15},{8,12},{9,1},{1... | collective-permute-start | bytes 589832 | tf_op jit(solution)/shard_map/ppermute | solution.py:309
  18.3 2.1 %collective-permute-start.4 = (bf16[192,1536]{1,0:T(8,128)(2,1)S(1)}, bf16[192,1536]{1,0:T(8,128)(2,1)S(1)}, u32[]{:S(2)}, u32[]{:S(2)}) collective-permute-start(bf16[192,1536]{1,0:T(8,128)(2,1)S(1)} %constant_dynamic-update-slice_fusion.near_ref), channel_id=1, source_target_pairs={{0,1},{1,0},{2,3},{3,2},{4,5},{5,4},{6,7},{7,6},{8,9},{9,8},{10,11... | collective-permute-start | bytes 1769480 | tf_op jit(solution)/shard_map/ppermute | solution.py:309
  18.4 5.7 %collective-permute-start.3 = (bf16[64,1536]{1,0:T(8,128)(2,1)S(1)}, bf16[64,1536]{1,0:T(8,128)(2,1)S(1)}, u32[]{:S(2)}, u32[]{:S(2)}) collective-permute-start(bf16[64,1536]{1,0:T(8,128)(2,1)S(1)} %collective-permute-done.1), channel_id=1, source_target_pairs={{0,2},{1,5},{2,0},{3,7},{4,6},{5,1},{6,4},{7,3},{8,10},{9,13},{10,... | collective-permute-start | bytes 589832 | tf_op jit(solution)/shard_map/ppermute | solution.py:309
  23.3 2.3 %copy-start.1 = (bf16[768,1536]{1,0:T(8,128)(2,1)S(1)}, bf16[768,1536]{1,0:T(8,128)(2,1)}, u32[]{:S(2)}) copy-start(bf16[768,1536]{1,0:T(8,128)(2,1)} %wo_ref.1) | copy-start | bytes 7077892
  24.2 1.4 %collective-permute-start.5 = (bf16[64,1536]{1,0:T(8,128)(2,1)S(1)}, bf16[64,1536]{1,0:T(8,128)(2,1)S(1)}, u32[]{:S(2)}, u32[]{:S(2)}) collective-permute-start(bf16[64,1536]{1,0:T(8,128)(2,1)S(1)} %collective-permute-done.3.far_ref), channel_id=1, source_target_pairs={{0,1},{1,0},{2,3},{3,2},{4,5},{5,4},{6,7},{7,6},{8,9},{9,8},{10,11... | collective-permute-start | bytes 589832 | tf_op jit(solution)/shard_map/ppermute | solution.py:309

commit v6 on v5

--- a/solution.py
+++ b/solution.py
@@ -38,48 +38,29 @@
     return phases, held
 
 
-def norm_kernel(
-    mask_groups,
-    frames_hbm,
-    time_hbm,
-    gain_hbm,
-    wk_hbm,
-    wv_hbm,
-    normed_ref,
-    pooled_ref,
-    *rest,
-):
+def norm_kernel(mask_groups, frames_hbm, time_hbm, gain_hbm, normed_ref, high_ref, low_ref, *rest):
     bias_refs = rest[: len(mask_groups)]
-    x_buf, time_ref, gain_buf, wk_buf, wv_buf, x_sem, t_sem, g_sem, w_sem = rest[len(mask_groups) :]
+    x_buf, time_ref, gain_buf, x_sem, t_sem, g_sem = rest[len(mask_groups) :]
     rows, width = x_buf.shape
     parts = x_sem.shape[0]
     step = rows // parts
-    gain_load = pltpu.make_async_copy(gain_hbm, gain_buf.at[0], g_sem)
-    time_load = pltpu.make_async_copy(time_hbm, time_ref, t_sem)
-    time_load.start()
     loads = [
         pltpu.make_async_copy(frames_hbm.at[pl.ds(i * step, step)], x_buf.at[pl.ds(i * step, step)], x_sem.at[i])
         for i in range(parts)
     ]
-    weights = [
-        pltpu.make_async_copy(wk_hbm, wk_buf, w_sem.at[0]),
-        pltpu.make_async_copy(wv_hbm, wv_buf, w_sem.at[1]),
-    ]
-    for copy in loads:
+    gain_load = pltpu.make_async_copy(gain_hbm, gain_buf.at[0], g_sem)
+    time_load = pltpu.make_async_copy(time_hbm, time_ref, t_sem)
+    for copy in loads + [gain_load, time_load]:
         copy.start()
-    gain_load.start()
-    weights[0].start()
+    gain_load.wait()
+    gain = gain_buf[...]
     time_load.wait()
     for masks, bias_ref in zip(mask_groups, bias_refs):
-        mask_columns(time_ref, masks, rows // TOKENS, bias_ref)
+        mask_rows(time_ref, masks, rows // TOKENS, bias_ref)
     pair = 2 * WW
     per_window = WIN * WIN
     for i in range(parts):
         loads[i].wait()
-        if i == 0:
-            weights[1].start()
-            gain_load.wait()
-            gain = gain_buf[...]
         for g in range(i * step // pair, (i + 1) * step // pair):
             x = x_buf[pl.ds(g * pair, pair), :].astype(F32)
             scale = lax.rsqrt(jnp.mean(x * x, axis=-1, keepdims=True) + 1e-06)
@@ -101,44 +82,42 @@
     pick = jnp.where(home == slot, 1.0 / (POOL * POOL), 0.0).astype(BF16)
     mean = jnp.dot(pick, normed_ref[...], preferred_element_type=F32)
     high = mean.astype(BF16)
-    low = (mean - high.astype(F32)).astype(BF16)
-    both = jnp.concatenate([high, low], axis=0)
-    cols = HEADS * HD
-    for i, buf in enumerate((wk_buf, wv_buf)):
-        weights[i].wait()
-        z = jnp.dot(both, buf[...], preferred_element_type=F32)
-        pooled_ref[:, i * cols : (i + 1) * cols] = (z[:out_rows] + z[out_rows:]).astype(BF16)
-
-
-def norm_and_pool(mask_groups, frames, frame_time, gain, w_key, w_value):
+    high_ref[...] = high
+    low_ref[...] = (mean - high.astype(F32)).astype(BF16)
+
+
+def norm_and_pool(mask_groups, frames, frame_time, gain):
     rows, width = frames.shape
-    out_rows = rows // TOKENS * SLOTS
-    cols = HEADS * HD
-    biases = tuple(jax.ShapeDtypeStruct((len(masks) * out_rows, HD), BF16) for masks in mask_groups)
+    count = rows // TOKENS
+    pooled = jax.ShapeDtypeStruct((count * SLOTS, width), BF16)
+    biases = tuple(jax.ShapeDtypeStruct((len(masks) * count * SLOTS, count * HD), F32) for masks in mask_groups)
     return pl.pallas_call(
         functools.partial(norm_kernel, mask_groups),
-        out_shape=(
-            jax.ShapeDtypeStruct((rows, width), BF16),
-            jax.ShapeDtypeStruct((out_rows, 2 * cols), BF16),
-            *biases,
-        ),
-        in_specs=[HBM] * 5,
-        out_specs=(VMEM,) * (2 + len(biases)),
+        out_shape=(jax.ShapeDtypeStruct((rows, width), BF16), pooled, pooled, *biases),
+        in_specs=[HBM] * 3,
+        out_specs=(VMEM,) * (3 + len(biases)),
         scratch_shapes=[
             pltpu.VMEM((rows, width), BF16),
             pltpu.SMEM(frame_time.shape, jnp.int32),
             pltpu.VMEM((1, width), F32),
-            pltpu.VMEM((width, cols), BF16),
-            pltpu.VMEM((width, cols), BF16),
             pltpu.SemaphoreType.DMA((2,)),
             pltpu.SemaphoreType.DMA,
             pltpu.SemaphoreType.DMA,
-            pltpu.SemaphoreType.DMA((2,)),
         ],
-        compiler_params=pltpu.CompilerParams(vmem_limit_bytes=24 << 20),
+        compiler_params=pltpu.CompilerParams(vmem_limit_bytes=16 << 20),
         cost_estimate=pl.CostEstimate(flops=400_000_000, bytes_accessed=8_000_000, transcendentals=0),
         name="norm_and_pool",
-    )(*(pltpu.with_memory_space_constraint(x, pltpu.HBM) for x in (frames, frame_time, gain, w_key, w_value)))
+    )(*(pltpu.with_memory_space_constraint(x, pltpu.HBM) for x in (frames, frame_time, gain)))
+
+
+def pooled_kernel(high_ref, low_ref, came_ref, wk_ref, wv_ref, out_ref):
+    rows = high_ref.shape[0]
+    x = jnp.concatenate([high_ref[...], low_ref[...], came_ref[...]], axis=0)
+    cols = HEADS * HD
+    for i, w_ref in enumerate((wk_ref, wv_ref)):
+        z = jnp.dot(x, w_ref[...], preferred_element_type=F32)
+        part = slice(i * cols, (i + 1) * cols)
+        out_ref[:, part] = jnp.concatenate([z[:rows] + z[rows : 2 * rows], z[2 * rows :]], axis=0).astype(BF16)
 
 
 def own_block(me, mask_pair):
@@ -146,24 +125,22 @@
     return me ^ (a if a == b else jnp.where(me % 2 == 0, a, b))
 
 
-def mask_columns(time_ref, masks, count, bias_ref):
+def mask_rows(time_ref, masks, count, bias_ref):
     me = lax.axis_index("tm")
-    lane = lax.broadcasted_iota(jnp.int32, (SLOTS, HD), 1)
     own = [time_ref[me * count + f] for f in range(count)]
     for i, pair in enumerate(masks):
         source = own_block(me, pair)
         for g in range(count):
             t = time_ref[source * count + g]
-            tile = jnp.zeros((SLOTS, HD), F32)
             for f in range(count):
-                tile = jnp.where(lane == f, jnp.where(t < own[f], 0.0, FAR), tile)
-            bias_ref[pl.ds((i * count + g) * SLOTS, SLOTS), :] = tile.astype(BF16)
-
-
-def frame_columns(tokens):
-    frame = lax.broadcasted_iota(jnp.int32, (tokens, HD), 0) // TOKENS
-    lane = lax.broadcasted_iota(jnp.int32, (tokens, HD), 1)
-    return jnp.where(frame == lane, 1.0, 0.0).astype(BF16)
+                value = jnp.where(t < own[f], 0.0, FAR).astype(F32)
+                bias_ref[pl.ds((i * count + g) * SLOTS, SLOTS), head(f)] = jnp.full((SLOTS, HD), value, F32)
+
+
+def mask_scores(s, bias):
+    copies = TOKENS // HD
+    columns = [bias[:, head(f)] for f in range(s.shape[1] // TOKENS) for _ in range(copies)]
+    return s + jnp.concatenate(columns, axis=1)
 
 
 def dot_nt(a, b):
@@ -183,14 +160,13 @@
     per_window = WIN * WIN
     cols = HEADS * HD
     bias = bias_ref[...]
-    frames = frame_columns(tokens)
     left = lax.broadcasted_iota(jnp.int32, (per_window, 2 * per_window), 1) < per_window
     pairs = [slice(w, w + 2 * per_window) for w in range(0, tokens, 2 * per_window)]
 
     def scores(h):
         q = q_ref[:, head(h)]
         far_k = jnp.concatenate([near_ref[:, head(h)], other_ref[:, head(h)]], axis=0)
-        far_s = dot_nt(jnp.concatenate([far_k, bias], axis=1), jnp.concatenate([q, frames], axis=1))
+        far_s = mask_scores(dot_nt(far_k, q), bias)
         parts = []
         for two in pairs:
             s = dot_nt(k_ref[two, head(h)], q_ref[two, head(h)])
@@ -230,14 +206,11 @@
 
 
 def far_stages(bias_ref, q_ref, far_ref, m_in, l_in, acc_in, keep_state, keep_acc):
-    tokens = q_ref.shape[0]
     cols = HEADS * HD
     bias = bias_ref[...]
-    frames = frame_columns(tokens)
 
     def scores(h):
-        far_k = jnp.concatenate([far_ref[:, head(h)], bias], axis=1)
-        return (dot_nt(far_k, jnp.concatenate([q_ref[:, head(h)], frames], axis=1)),)
+        return (mask_scores(dot_nt(far_ref[:, head(h)], q_ref[:, head(h)]), bias),)
 
     def weigh(h, s):
         m, l = m_in[h : h + 1, :], l_in[h : h + 1, :]
@@ -302,8 +275,7 @@
     own, own_late = (list(zip(x, y)) for x, y in zip(*held))
     far, far_late = ([(y ^ 1, x ^ 1) for x, y in masks] for masks in (own, own_late))
     groups = (own + far, own_late, far_late)
-    normed, block, *bias = norm_and_pool(groups, frames_in, frame_time, norm_gain, w_key, w_value)
-    block, w_query, w_key, w_value = lax.optimization_barrier((block, w_query, w_key, w_value))
+    normed, high, low, *bias = norm_and_pool(groups, frames_in, frame_time, norm_gain)
 
     def send(x, pair):
         return lax.ppermute(x, "tm", [(i, i ^ pair[i % 2]) for i in range(n)])
@@ -311,12 +283,19 @@
     def project(w):
         return jnp.dot(normed, w, preferred_element_type=F32).astype(BF16)
 
-    query = None
-    for pair in phases[:-2]:
-        came = send(block, pair)
-        query = project(w_query) if query is None else query
-        block = jnp.concatenate([block, came], axis=0)
-        block, normed, query = lax.optimization_barrier((block, normed, query))
+    came = send(high, phases[0])
+    query = project(w_query)
+    came, normed, query = lax.optimization_barrier((came, normed, query))
+    block = pl.pallas_call(
+        pooled_kernel,
+        out_shape=jax.ShapeDtypeStruct((2 * high.shape[0], 2 * HEADS * HD), BF16),
+        in_specs=[VMEM] * 5,
+        out_specs=VMEM,
+        compiler_params=pltpu.CompilerParams(vmem_limit_bytes=16 << 20),
+        name="pooled_keys_values",
+    )(high, low, came, w_key, w_value)
+    for pair in phases[1:-2]:
+        block = jnp.concatenate([block, send(block, pair)], axis=0)
     brought = send(block, phases[-2])
     early = send(block, phases[-1])
     keys, values = project(w_key), project(w_value)

time: 28.7 us -> 27.9 us (0.972)
  Pallas kernels: 10.8 us -> 9.59 us
  waiting for transfers between devices: 4.6 us -> 4.99 us
    pallas_call x1, Pallas kernels: 3.91 us -> 2.32 us  [norm_and_pool(): pl.pallas_call(functools.partial(norm_kernel, mask_groups), out_shape=(ja...]
    pallas_call x0 -> x1, Pallas kernels: none -> 0.88 us  [on_device(): pl.pallas_call(pooled_kernel, out_shape=jax.ShapeDtypeStruct((2 * high.sh...]
    ppermute x6, waiting for transfers between devices: 4.6 us -> 4.99 us  [send(): return lax.ppermute(x, 'tm', [(i, i ^ pair[i % 2]) for i in range(n)])]
  transfers between devices with their start and end apart: 6 -> 6, of which waited for: 5 -> 5; matrix products, arithmetic and copies ran while one was open for 15% -> 15% of each run, Pallas kernels for 14% -> 13%
where the time goes in v6:
time: 27.9 us; the launch traced here: 27.7 us
  Pallas kernels  9.59 us (34%)
  starting transfers between devices  8.84 us (32%)
  waiting for transfers between devices  4.99 us (18%)
  matrix products  4.14 us (15%)
    ppermute x6, starting transfers between devices, send(): return lax.ppermute(x, 'tm', [(i, i ^ pair[i % 2]) for i in range(n)])  8.84 us
    ppermute x6, waiting for transfers between devices, send(): return lax.ppermute(x, 'tm', [(i, i ^ pair[i % 2]) for i in range(n)])  4.99 us
    dot_general x3, matrix products, project(): return jnp.dot(normed, w, preferred_element_type=F32).astype(BF16)  4.14 us
    pallas_call x1, Pallas kernels, on_device(): pl.pallas_call(last_kernel, out_shape=jax.ShapeDtypeStruct((rows, w_outpu...  2.82 us
    pallas_call x1, Pallas kernels, on_device(): pl.pallas_call(first_kernel, out_shape=state, in_specs=[VMEM] * 6, out_sp...  2.62 us
    pallas_call x1, Pallas kernels, norm_and_pool(): pl.pallas_call(functools.partial(norm_kernel, mask_groups), out_shape=(ja...  2.32 us
    pallas_call x1, Pallas kernels, on_device(): pl.pallas_call(middle_kernel, out_shape=state, in_specs=[VMEM] * 6, out_s...  0.95 us
    pallas_call x1, Pallas kernels, on_device(): pl.pallas_call(pooled_kernel, out_shape=jax.ShapeDtypeStruct((2 * high.sh...  0.88 us
  transfers between devices with their start and end apart: 6, of which 5 were waited for; matrix products, arithmetic and copies ran while one was open for 15% of the time, Pallas kernels for 13%

profile of v6, /device:TPU:0, one launch (start us, length us, event | category | flops | bytes accessed | tf_op | source)
XLA Modules:
  0.0 27.7 jit_solution(805082253537729927)
XLA Ops:
  0.0 0.0 copy-start
  0.0 2.3 %norm_and_pool.1 = (bf16[512,1536]{1,0:T(8,128)(2,1)S(1)}, bf16[32,1536]{1,0:T(8,128)(2,1)S(1)}, bf16[32,1536]{1,0:T(8,128)(2,1)S(1)}, f32[384,256]{1,0:T(8,128)...) custom-call(bf16[512,1536]{1,0:T(8,128)(2,1)} %frames_hbm.1, s32[32]{0:T(128)} %time_hbm.1, f32[1536]{0:T(1024)} %gain_hbm.1), custom_call_target="tpu_custom_call" | custom-call | flops 400000000 | bytes 8000000 | tf_op jit(solution)/shard_map/norm_and_pool/pallas_call | solution.py:94
  2.3 4.1 %collective-permute-start = (bf16[32,1536]{1,0:T(8,128)(2,1)S(1)}, bf16[32,1536]{1,0:T(8,128)(2,1)S(1)}, u32[]{:S(2)}, u32[]{:S(2)}) collective-permute-start(bf16[32,1536]{1,0:T(8,128)(2,1)S(1)} %get-tuple-element.29.high_ref), channel_id=1, source_target_pairs={{0,8},{1,3},{2,10},{3,1},{4,12},{5,7},{6,14},{7,5},{8,0},{9,11},{1... | collective-permute-start | bytes 294920 | tf_op jit(solution)/shard_map/ppermute | solution.py:281
  6.4 0.0 copy-done
  6.4 0.0 copy-start.2
  6.4 0.0 copy-start.3
  6.4 1.4 %convolution_convert_fusion.2.q_ref = bf16[512,768]{1,0:T(8,128)(2,1)S(1)} fusion(bf16[512,1536]{1,0:T(8,128)(2,1)S(1)} %get-tuple-element.34, bf16[1536,768]{1,0:T(8,128)(2,1)S(1)} %copy-done), kind=kOutput, calls=%fused_computation.2 | convolution fusion | flops 1208352768 | bytes 4718592 | tf_op jit(solution)/shard_map/dot_general | solution.py:284
  7.8 1.2 %collective-permute-done.came_ref = bf16[32,1536]{1,0:T(8,128)(2,1)S(1)} collective-permute-done((bf16[32,1536]{1,0:T(8,128)(2,1)S(1)}, bf16[32,1536]{1,0:T(8,128)(2,1)S(1)}, u32[]{:S(2)}, u32[]{:S(2)}) %collective-permute-start) | collective-permute-done | bytes 98336 | tf_op jit(solution)/shard_map/ppermute | solution.py:281
  9.0 0.0 copy-done.2
  9.0 0.0 copy-done.3
  9.0 0.9 %pooled_keys_values.1 = bf16[64,1536]{1,0:T(8,128)(2,1)S(1)} custom-call(bf16[32,1536]{1,0:T(8,128)(2,1)S(1)} %get-tuple-element.29.high_ref, bf16[32,1536]{1,0:T(8,128)(2,1)S(1)} %get-tuple-element.32.low_ref, bf16[32,1536]{1,0:T(8,128)(2,1)S(1)} %collective-permute-done.came_ref, bf16[1536,768]{1,0:T(8,128)(2,1)S(1)} %copy-done.3, ...), custom_call_target="tpu_custom_call" | custom-call | tf_op jit(solution)/shard_map/pooled_keys_values/pallas_call | solution.py:289
  9.9 1.9 %collective-permute-start.2 = (bf16[64,1536]{1,0:T(8,128)(2,1)S(1)}, bf16[64,1536]{1,0:T(8,128)(2,1)S(1)}, u32[]{:S(2)}, u32[]{:S(2)}) collective-permute-start(bf16[64,1536]{1,0:T(8,128)(2,1)S(1)} %pooled_keys_values.1), channel_id=1, source_target_pairs={{0,2},{1,5},{2,0},{3,7},{4,6},{5,1},{6,4},{7,3},{8,10},{9,13},{10,... | collective-permute-start | bytes 589832 | tf_op jit(solution)/shard_map/ppermute | solution.py:281
  11.8 1.7 %collective-permute-start.1 = (bf16[64,1536]{1,0:T(8,128)(2,1)S(1)}, bf16[64,1536]{1,0:T(8,128)(2,1)S(1)}, u32[]{:S(2)}, u32[]{:S(2)}) collective-permute-start(bf16[64,1536]{1,0:T(8,128)(2,1)S(1)} %pooled_keys_values.1), channel_id=1, source_target_pairs={{0,4},{1,9},{2,6},{3,11},{4,0},{5,13},{6,2},{7,15},{8,12},{9,1},{1... | collective-permute-start | bytes 589832 | tf_op jit(solution)/shard_map/ppermute | solution.py:281
  13.6 1.4 %convolution_convert_fusion.v_ref = bf16[512,768]{1,0:T(8,128)(2,1)S(1)} fusion(bf16[512,1536]{1,0:T(8,128)(2,1)S(1)} %get-tuple-element.34, bf16[1536,768]{1,0:T(8,128)(2,1)S(1)} %copy-done.2), kind=kOutput, calls=%fused_computation | convolution fusion | flops 1208352768 | bytes 4718592 | tf_op jit(solution)/shard_map/dot_general | solution.py:284
  14.9 1.4 %convolution_convert_fusion.1.k_ref = bf16[512,768]{1,0:T(8,128)(2,1)S(1)} fusion(bf16[512,1536]{1,0:T(8,128)(2,1)S(1)} %get-tuple-element.34, bf16[1536,768]{1,0:T(8,128)(2,1)S(1)} %copy-done.3), kind=kOutput, calls=%fused_computation.1 | convolution fusion | flops 1208352768 | bytes 4718592 | tf_op jit(solution)/shard_map/dot_general | solution.py:284
  16.3 0.0 collective-permute-done.2
  16.3 1.2 %collective-permute-done.1 = bf16[64,1536]{1,0:T(8,128)(2,1)S(1)} collective-permute-done((bf16[64,1536]{1,0:T(8,128)(2,1)S(1)}, bf16[64,1536]{1,0:T(8,128)(2,1)S(1)}, u32[]{:S(2)}, u32[]{:S(2)}) %collective-permute-start.1) | collective-permute-done | bytes 196640 | tf_op jit(solution)/shard_map/ppermute | solution.py:281
  17.6 0.1 collective-permute-start.4
  17.7 1.0 %collective-permute-start.3 = (bf16[64,1536]{1,0:T(8,128)(2,1)S(1)}, bf16[64,1536]{1,0:T(8,128)(2,1)S(1)}, u32[]{:S(2)}, u32[]{:S(2)}) collective-permute-start(bf16[64,1536]{1,0:T(8,128)(2,1)S(1)} %collective-permute-done.1), channel_id=1, source_target_pairs={{0,2},{1,5},{2,0},{3,7},{4,6},{5,1},{6,4},{7,3},{8,10},{9,13},{10,... | collective-permute-start | bytes 589832 | tf_op jit(solution)/shard_map/ppermute | solution.py:281
  18.7 1.0 %collective-permute-done.4.other_ref = bf16[192,1536]{1,0:T(8,128)(2,1)S(1)} collective-permute-done((bf16[192,1536]{1,0:T(8,128)(2,1)S(1)}, bf16[192,1536]{1,0:T(8,128)(2,1)S(1)}, u32[]{:S(2)}, u32[]{:S(2)}) %collective-permute-start.4) | collective-permute-done | bytes 589856 | tf_op jit(solution)/shard_map/ppermute | solution.py:281
  19.7 2.6 %local_and_first.1 = (f32[768,512]{1,0:T(8,128)S(1)}, f32[8,512]{1,0:T(8,128)S(1)}, f32[8,512]{1,0:T(8,128)S(1)}) custom-call(f32[384,256]{1,0:T(8,128)S(1)} %get-tuple-element.36.bias_ref, bf16[512,768]{1,0:T(8,128)(2,1)S(1)} %convolution_convert_fusion.2.q_ref, bf16[512,768]{1,0:T(8,128)(2,1)S(1)} %convolution_convert_fusion.1.k_ref, ...), custom_call_target="tpu_custom_call" | custom-call | flops 900000000 | bytes 5000000 | tf_op jit(solution)/shard_map/local_and_first/pallas_call | solution.py:312
  22.3 0.0 copy-start.1
  22.3 1.1 %collective-permute-done.3.far_ref = bf16[64,1536]{1,0:T(8,128)(2,1)S(1)} collective-permute-done((bf16[64,1536]{1,0:T(8,128)(2,1)S(1)}, bf16[64,1536]{1,0:T(8,128)(2,1)S(1)}, u32[]{:S(2)}, u32[]{:S(2)}) %collective-permute-start.3) | collective-permute-done | bytes 196640 | tf_op jit(solution)/shard_map/ppermute | solution.py:281
  23.4 0.0 collective-permute-start.5
  23.4 1.0 %middle.1 = (f32[768,512]{1,0:T(8,128)S(1)}, f32[8,512]{1,0:T(8,128)S(1)}, f32[8,512]{1,0:T(8,128)S(1)}) custom-call(f32[64,256]{1,0:T(8,128)S(1)} %get-tuple-element.44.bias_ref, bf16[512,768]{1,0:T(8,128)(2,1)S(1)} %convolution_convert_fusion.2.q_ref, ...), custom_call_target="tpu_custom_call", output_to_operand_aliasing={{0}: (3, {}), {1}: (4, {}), {2}: (5, {})} | custom-call | flops 500000000 | bytes 5000000 | tf_op jit(solution)/shard_map/middle/pallas_call | solution.py:323
  24.4 0.5 %collective-permute-done.5.far_ref = bf16[64,1536]{1,0:T(8,128)(2,1)S(1)} collective-permute-done((bf16[64,1536]{1,0:T(8,128)(2,1)S(1)}, bf16[64,1536]{1,0:T(8,128)(2,1)S(1)}, u32[]{:S(2)}, u32[]{:S(2)}) %collective-permute-start.5) | collective-permute-done | bytes 196640 | tf_op jit(solution)/shard_map/ppermute | solution.py:281
  24.9 0.0 copy-done.1
  24.9 2.8 %last_and_output.1 = bf16[512,1536]{1,0:T(8,128)(2,1)} custom-call(f32[64,256]{1,0:T(8,128)S(1)} %get-tuple-element.28.bias_ref, bf16[512,768]{1,0:T(8,128)(2,1)S(1)} %convolution_convert_fusion.2.q_ref, bf16[64,1536]{1,0:T(8,128)(2,1)S(1)} %collective-permute-done.5.far_ref, f32[768,512]{1,0:T(8,128)S(1)} %get-tuple-element.48.acc_in, ...), custom_call_target="tpu_custom_call" | custom-call | flops 1700000000 | bytes 8000000 | tf_op jit(solution)/shard_map/last_and_output/pallas_call | solution.py:333
  (1 shorter events, 0.0 us)
Async XLA Ops:
  0.0 6.4 %copy-start = (bf16[1536,768]{1,0:T(8,128)(2,1)S(1)}, bf16[1536,768]{1,0:T(8,128)(2,1)}, u32[]{:S(2)}) copy-start(bf16[1536,768]{1,0:T(8,128)(2,1)} %param.10) | copy-start | bytes 7077892
  2.3 6.7 %collective-permute-start = (bf16[32,1536]{1,0:T(8,128)(2,1)S(1)}, bf16[32,1536]{1,0:T(8,128)(2,1)S(1)}, u32[]{:S(2)}, u32[]{:S(2)}) collective-permute-start(bf16[32,1536]{1,0:T(8,128)(2,1)S(1)} %get-tuple-element.29.high_ref), channel_id=1, source_target_pairs={{0,8},{1,3},{2,10},{3,1},{4,12},{5,7},{6,14},{7,5},{8,0},{9,11},{1... | collective-permute-start | bytes 294920 | tf_op jit(solution)/shard_map/ppermute | solution.py:281
  6.4 2.6 %copy-start.2 = (bf16[1536,768]{1,0:T(8,128)(2,1)S(1)}, bf16[1536,768]{1,0:T(8,128)(2,1)}, u32[]{:S(2)}) copy-start(bf16[1536,768]{1,0:T(8,128)(2,1)} %wv_ref.1) | copy-start | bytes 7077892
  6.4 2.6 %copy-start.3 = (bf16[1536,768]{1,0:T(8,128)(2,1)S(1)}, bf16[1536,768]{1,0:T(8,128)(2,1)}, u32[]{:S(2)}) copy-start(bf16[1536,768]{1,0:T(8,128)(2,1)} %wk_ref.1) | copy-start | bytes 7077892
  9.9 6.4 %collective-permute-start.2 = (bf16[64,1536]{1,0:T(8,128)(2,1)S(1)}, bf16[64,1536]{1,0:T(8,128)(2,1)S(1)}, u32[]{:S(2)}, u32[]{:S(2)}) collective-permute-start(bf16[64,1536]{1,0:T(8,128)(2,1)S(1)} %pooled_keys_values.1), channel_id=1, source_target_pairs={{0,2},{1,5},{2,0},{3,7},{4,6},{5,1},{6,4},{7,3},{8,10},{9,13},{10,... | collective-permute-start | bytes 589832 | tf_op jit(solution)/shard_map/ppermute | solution.py:281
  11.8 5.7 %collective-permute-start.1 = (bf16[64,1536]{1,0:T(8,128)(2,1)S(1)}, bf16[64,1536]{1,0:T(8,128)(2,1)S(1)}, u32[]{:S(2)}, u32[]{:S(2)}) collective-permute-start(bf16[64,1536]{1,0:T(8,128)(2,1)S(1)} %pooled_keys_values.1), channel_id=1, source_target_pairs={{0,4},{1,9},{2,6},{3,11},{4,0},{5,13},{6,2},{7,15},{8,12},{9,1},{1... | collective-permute-start | bytes 589832 | tf_op jit(solution)/shard_map/ppermute | solution.py:281
  17.6 2.1 %collective-permute-start.4 = (bf16[192,1536]{1,0:T(8,128)(2,1)S(1)}, bf16[192,1536]{1,0:T(8,128)(2,1)S(1)}, u32[]{:S(2)}, u32[]{:S(2)}) collective-permute-start(bf16[192,1536]{1,0:T(8,128)(2,1)S(1)} %pad_maximum_fusion.near_ref), channel_id=1, source_target_pairs={{0,1},{1,0},{2,3},{3,2},{4,5},{5,4},{6,7},{7,6},{8,9},{9,8},{10,11... | collective-permute-start | bytes 1769480 | tf_op jit(solution)/shard_map/ppermute | solution.py:281
  17.7 5.7 %collective-permute-start.3 = (bf16[64,1536]{1,0:T(8,128)(2,1)S(1)}, bf16[64,1536]{1,0:T(8,128)(2,1)S(1)}, u32[]{:S(2)}, u32[]{:S(2)}) collective-permute-start(bf16[64,1536]{1,0:T(8,128)(2,1)S(1)} %collective-permute-done.1), channel_id=1, source_target_pairs={{0,2},{1,5},{2,0},{3,7},{4,6},{5,1},{6,4},{7,3},{8,10},{9,13},{10,... | collective-permute-start | bytes 589832 | tf_op jit(solution)/shard_map/ppermute | solution.py:281
  22.3 2.6 %copy-start.1 = (bf16[768,1536]{1,0:T(8,128)(2,1)S(1)}, bf16[768,1536]{1,0:T(8,128)(2,1)}, u32[]{:S(2)}) copy-start(bf16[768,1536]{1,0:T(8,128)(2,1)} %wo_ref.1) | copy-start | bytes 7077892
  23.4 1.4 %collective-permute-start.5 = (bf16[64,1536]{1,0:T(8,128)(2,1)S(1)}, bf16[64,1536]{1,0:T(8,128)(2,1)S(1)}, u32[]{:S(2)}, u32[]{:S(2)}) collective-permute-start(bf16[64,1536]{1,0:T(8,128)(2,1)S(1)} %collective-permute-done.3.far_ref), channel_id=1, source_target_pairs={{0,1},{1,0},{2,3},{3,2},{4,5},{5,4},{6,7},{7,6},{8,9},{9,8},{10,11... | collective-permute-start | bytes 589832 | tf_op jit(solution)/shard_map/ppermute | solution.py:281

commit v7 on v6

--- a/solution.py
+++ b/solution.py
@@ -38,9 +38,7 @@
     return phases, held
 
 
-def norm_kernel(mask_groups, frames_hbm, time_hbm, gain_hbm, normed_ref, high_ref, low_ref, *rest):
-    bias_refs = rest[: len(mask_groups)]
-    x_buf, time_ref, gain_buf, x_sem, t_sem, g_sem = rest[len(mask_groups) :]
+def norm_kernel(frames_hbm, gain_hbm, normed_ref, high_ref, low_ref, x_buf, gain_buf, x_sem, g_sem):
     rows, width = x_buf.shape
     parts = x_sem.shape[0]
     step = rows // parts
@@ -49,36 +47,23 @@
         for i in range(parts)
     ]
     gain_load = pltpu.make_async_copy(gain_hbm, gain_buf.at[0], g_sem)
-    time_load = pltpu.make_async_copy(time_hbm, time_ref, t_sem)
-    for copy in loads + [gain_load, time_load]:
+    for copy in loads + [gain_load]:
         copy.start()
     gain_load.wait()
     gain = gain_buf[...]
-    time_load.wait()
-    for masks, bias_ref in zip(mask_groups, bias_refs):
-        mask_rows(time_ref, masks, rows // TOKENS, bias_ref)
     pair = 2 * WW
-    per_window = WIN * WIN
     for i in range(parts):
         loads[i].wait()
         for g in range(i * step // pair, (i + 1) * step // pair):
             x = x_buf[pl.ds(g * pair, pair), :].astype(F32)
             scale = lax.rsqrt(jnp.mean(x * x, axis=-1, keepdims=True) + 1e-06)
             y = x * scale * gain
-            frame, row = divmod(2 * g, HH)
-            wr, r = divmod(row, WIN)
-            for wc in range(WW // WIN):
-                both = jnp.concatenate(
-                    [y[wc * WIN : (wc + 1) * WIN], y[WW + wc * WIN : WW + (wc + 1) * WIN]], axis=0
-                )
-                base = frame * TOKENS + (wr * (WW // WIN) + wc) * per_window + r * WIN
-                normed_ref[pl.ds(base, 2 * WIN), :] = both.astype(BF16)
+            normed_ref[pl.ds(g * pair, pair), :] = y.astype(BF16)
     count = rows // TOKENS
     out_rows = count * SLOTS
     slot = lax.broadcasted_iota(jnp.int32, (out_rows, rows), 0)
     token = lax.broadcasted_iota(jnp.int32, (out_rows, rows), 1)
-    r, c = token % per_window // WIN, token % WIN
-    home = token // per_window * 4 + r // POOL * 2 + c // POOL
+    home = token // (WW * POOL) * (WW // POOL) + token % WW // POOL
     pick = jnp.where(home == slot, 1.0 / (POOL * POOL), 0.0).astype(BF16)
     mean = jnp.dot(pick, normed_ref[...], preferred_element_type=F32)
     high = mean.astype(BF16)
@@ -86,28 +71,45 @@
     low_ref[...] = (mean - high.astype(F32)).astype(BF16)
 
 
-def norm_and_pool(mask_groups, frames, frame_time, gain):
+def mask_kernel(mask_groups, count, time_hbm, *rest):
+    bias_refs, (time_ref, t_sem) = rest[:-2], rest[-2:]
+    time_load = pltpu.make_async_copy(time_hbm, time_ref, t_sem)
+    time_load.start()
+    time_load.wait()
+    for masks, bias_ref in zip(mask_groups, bias_refs):
+        mask_rows(time_ref, masks, count, bias_ref)
+
+
+def mask_biases(mask_groups, frame_time, count):
+    return pl.pallas_call(
+        functools.partial(mask_kernel, mask_groups, count),
+        out_shape=tuple(jax.ShapeDtypeStruct((len(masks) * count * SLOTS, count * HD), F32) for masks in mask_groups),
+        in_specs=[HBM],
+        out_specs=(VMEM,) * len(mask_groups),
+        scratch_shapes=[pltpu.SMEM(frame_time.shape, jnp.int32), pltpu.SemaphoreType.DMA],
+        compiler_params=pltpu.CompilerParams(vmem_limit_bytes=16 << 20),
+        name="mask_biases",
+    )(pltpu.with_memory_space_constraint(frame_time, pltpu.HBM))
+
+
+def norm_and_pool(frames, gain):
     rows, width = frames.shape
-    count = rows // TOKENS
-    pooled = jax.ShapeDtypeStruct((count * SLOTS, width), BF16)
-    biases = tuple(jax.ShapeDtypeStruct((len(masks) * count * SLOTS, count * HD), F32) for masks in mask_groups)
+    pooled = jax.ShapeDtypeStruct((rows // TOKENS * SLOTS, width), BF16)
     return pl.pallas_call(
-        functools.partial(norm_kernel, mask_groups),
-        out_shape=(jax.ShapeDtypeStruct((rows, width), BF16), pooled, pooled, *biases),
-        in_specs=[HBM] * 3,
-        out_specs=(VMEM,) * (3 + len(biases)),
+        norm_kernel,
+        out_shape=(jax.ShapeDtypeStruct((rows, width), BF16), pooled, pooled),
+        in_specs=[HBM] * 2,
+        out_specs=(VMEM,) * 3,
         scratch_shapes=[
             pltpu.VMEM((rows, width), BF16),
-            pltpu.SMEM(frame_time.shape, jnp.int32),
             pltpu.VMEM((1, width), F32),
             pltpu.SemaphoreType.DMA((2,)),
-            pltpu.SemaphoreType.DMA,
             pltpu.SemaphoreType.DMA,
         ],
         compiler_params=pltpu.CompilerParams(vmem_limit_bytes=16 << 20),
         cost_estimate=pl.CostEstimate(flops=400_000_000, bytes_accessed=8_000_000, transcendentals=0),
         name="norm_and_pool",
-    )(*(pltpu.with_memory_space_constraint(x, pltpu.HBM) for x in (frames, frame_time, gain)))
+    )(*(pltpu.with_memory_space_constraint(x, pltpu.HBM) for x in (frames, gain)))
 
 
 def pooled_kernel(high_ref, low_ref, came_ref, wk_ref, wv_ref, out_ref):
@@ -157,20 +159,21 @@
 
 def first_kernel(bias_ref, q_ref, k_ref, v_ref, near_ref, other_ref, acc_ref, m_ref, l_ref):
     tokens = q_ref.shape[0]
-    per_window = WIN * WIN
     cols = HEADS * HD
     bias = bias_ref[...]
-    left = lax.broadcasted_iota(jnp.int32, (per_window, 2 * per_window), 1) < per_window
-    pairs = [slice(w, w + 2 * per_window) for w in range(0, tokens, 2 * per_window)]
+    band = WIN * WW
+    left = lax.broadcasted_iota(jnp.int32, (WIN, band), 1) % WW < WIN
+    bands = [slice(t, t + band) for t in range(0, tokens, band)]
 
     def scores(h):
         q = q_ref[:, head(h)]
         far_k = jnp.concatenate([near_ref[:, head(h)], other_ref[:, head(h)]], axis=0)
         far_s = mask_scores(dot_nt(far_k, q), bias)
         parts = []
-        for two in pairs:
+        for two in bands:
             s = dot_nt(k_ref[two, head(h)], q_ref[two, head(h)])
-            parts.append(jnp.where(left, s[:per_window], s[per_window:]))
+            lines = [jnp.where(left, s[r : r + WIN], s[r + WIN : r + WW]) for r in range(0, band, WW)]
+            parts.append(jnp.concatenate(lines, axis=0))
         return jnp.concatenate(parts, axis=1), far_s
 
     def weigh(h, local_s, far_s):
@@ -184,9 +187,12 @@
     def mix(h, local_w, far_w):
         far_v = jnp.concatenate([near_ref[:, head(h, cols)], other_ref[:, head(h, cols)]], axis=0)
         acc = dot_tn(far_v, far_w)
-        for two in pairs:
-            p = local_w[:, two]
-            p = jnp.concatenate([jnp.where(left, p, 0.0), jnp.where(left, 0.0, p)], axis=0).astype(BF16)
+        for two in bands:
+            lines = []
+            for r in range(0, WIN * WIN, WIN):
+                p = local_w[r : r + WIN, two]
+                lines += [jnp.where(left, p, 0.0), jnp.where(left, 0.0, p)]
+            p = jnp.concatenate(lines, axis=0).astype(BF16)
             acc_ref[head(h), two] = acc[:, two] + dot_tn(v_ref[two, head(h)], p)
 
     pipelined(scores, weigh, mix)
@@ -240,30 +246,24 @@
 def last_kernel(
     bias_ref, q_ref, far_ref, acc_in, m_in, l_in, wo_ref, out_hbm, rows_buf, out_buf, out_sem
 ):
-    tokens = q_ref.shape[0]
-    per_window = WIN * WIN
-
     def keep_acc(h, acc, inverse):
-        mixed = jnp.transpose(acc * inverse)
-        for row in range(tokens // WW):
-            frame, rest = divmod(row, HH)
-            wr, r = divmod(rest, WIN)
-            base = frame * TOKENS + wr * (WW // WIN) * per_window + r * WIN
-            starts = [base + wc * per_window for wc in range(WW // WIN)]
-            line = jnp.concatenate([mixed[i : i + WIN] for i in starts], axis=0)
-            rows_buf[pl.ds(row * WW, WW), head(h)] = line.astype(BF16)
+        rows_buf[:, head(h)] = jnp.transpose((acc * inverse).astype(BF16))
 
     far_stages(
         bias_ref, q_ref, far_ref, m_in, l_in, acc_in, lambda h, top, total: 1.0 / total, keep_acc
     )
-    chunks = out_sem.shape[0]
-    width = out_buf.shape[1] // chunks
+    tall, wide = out_sem.shape
+    height, width = out_buf.shape[0] // tall, out_buf.shape[1] // wide
     copies = []
-    for c in range(chunks):
-        part = pl.ds(c * width, width)
-        out_buf[:, part] = jnp.dot(rows_buf[...], wo_ref[:, part], preferred_element_type=F32).astype(BF16)
-        copies.append(pltpu.make_async_copy(out_buf.at[:, part], out_hbm.at[:, part], out_sem.at[c]))
-        copies[-1].start()
+    for r in range(tall):
+        for c in range(wide):
+            rows, part = pl.ds(r * height, height), pl.ds(c * width, width)
+            out = jnp.dot(rows_buf[rows, :], wo_ref[:, part], preferred_element_type=F32)
+            out_buf[rows, part] = out.astype(BF16)
+            copies.append(
+                pltpu.make_async_copy(out_buf.at[rows, part], out_hbm.at[rows, part], out_sem.at[r, c])
+            )
+            copies[-1].start()
     for copy in copies:
         copy.wait()
 
@@ -275,7 +275,7 @@
     own, own_late = (list(zip(x, y)) for x, y in zip(*held))
     far, far_late = ([(y ^ 1, x ^ 1) for x, y in masks] for masks in (own, own_late))
     groups = (own + far, own_late, far_late)
-    normed, high, low, *bias = norm_and_pool(groups, frames_in, frame_time, norm_gain)
+    normed, high, low = norm_and_pool(frames_in, norm_gain)
 
     def send(x, pair):
         return lax.ppermute(x, "tm", [(i, i ^ pair[i % 2]) for i in range(n)])
@@ -285,7 +285,7 @@
 
     came = send(high, phases[0])
     query = project(w_query)
-    came, normed, query = lax.optimization_barrier((came, normed, query))
+    came, normed, query, frame_time = lax.optimization_barrier((came, normed, query, frame_time))
     block = pl.pallas_call(
         pooled_kernel,
         out_shape=jax.ShapeDtypeStruct((2 * high.shape[0], 2 * HEADS * HD), BF16),
@@ -296,6 +296,7 @@
     )(high, low, came, w_key, w_value)
     for pair in phases[1:-2]:
         block = jnp.concatenate([block, send(block, pair)], axis=0)
+    bias = mask_biases(groups, frame_time, rows // TOKENS)
     brought = send(block, phases[-2])
     early = send(block, phases[-1])
     keys, values = project(w_key), project(w_value)
@@ -338,7 +339,7 @@
         scratch_shapes=[
             pltpu.VMEM((rows, cols), BF16),
             pltpu.VMEM((rows, w_output.shape[1]), BF16),
-            pltpu.SemaphoreType.DMA((3,)),
+            pltpu.SemaphoreType.DMA((2, 3)),
         ],
         compiler_params=params,
         cost_estimate=pl.CostEstimate(flops=1_700_000_000, bytes_accessed=8_000_000, transcendentals=400_000),

time: 27.9 us -> 27.8 us (level)
  waiting for transfers between devices: 4.99 us -> 4.17 us
  Pallas kernels: 9.59 us -> 10.3 us
    ppermute x6, waiting for transfers between devices: 4.99 us -> 4.17 us  [send(): return lax.ppermute(x, 'tm', [(i, i ^ pair[i % 2]) for i in range(n)])]
    pallas_call x1 -> x2, Pallas kernels: 2.32 us -> 2.97 us  [the longest x1 2.21 us: norm_and_pool(): pl.pallas_call(norm_kernel, out_shape=(jax.ShapeDtypeStruct((rows, width)...]
  transfers between devices with their start and end apart: 6 -> 6, of which waited for: 5 -> 5; matrix products, arithmetic and copies ran while one was open for 15% -> 15% of each run, Pallas kernels for 13% -> 16%
where the time goes in v7:
time: 27.8 us; the launch traced here: 27.6 us
  Pallas kernels  10.3 us (37%)
  starting transfers between devices  8.85 us (32%)
  waiting for transfers between devices  4.17 us (15%)
  matrix products  4.14 us (15%)
    ppermute x6, starting transfers between devices, send(): return lax.ppermute(x, 'tm', [(i, i ^ pair[i % 2]) for i in range(n)])  8.85 us
    ppermute x6, waiting for transfers between devices, send(): return lax.ppermute(x, 'tm', [(i, i ^ pair[i % 2]) for i in range(n)])  4.17 us
    dot_general x3, matrix products, project(): return jnp.dot(normed, w, preferred_element_type=F32).astype(BF16)  4.14 us
    pallas_call x1, Pallas kernels, on_device(): pl.pallas_call(last_kernel, out_shape=jax.ShapeDtypeStruct((rows, w_outpu...  2.8 us
    pallas_call x1, Pallas kernels, on_device(): pl.pallas_call(first_kernel, out_shape=state, in_specs=[VMEM] * 6, out_sp...  2.67 us
    pallas_call x1, Pallas kernels, norm_and_pool(): pl.pallas_call(norm_kernel, out_shape=(jax.ShapeDtypeStruct((rows, width)...  2.21 us
    pallas_call x1, Pallas kernels, on_device(): pl.pallas_call(middle_kernel, out_shape=state, in_specs=[VMEM] * 6, out_s...  0.94 us
    pallas_call x1, Pallas kernels, on_device(): pl.pallas_call(pooled_kernel, out_shape=jax.ShapeDtypeStruct((2 * high.sh...  0.88 us
  transfers between devices with their start and end apart: 6, of which 5 were waited for; matrix products, arithmetic and copies ran while one was open for 15% of the time, Pallas kernels for 16%

profile of v7, /device:TPU:0, one launch (start us, length us, event | category | flops | bytes accessed | tf_op | source)
XLA Modules:
  0.0 27.6 jit_solution(7536747506659985947)
XLA Ops:
  0.0 0.0 copy-start
  0.0 2.2 %norm_and_pool.1 = (bf16[512,1536]{1,0:T(8,128)(2,1)S(1)}, bf16[32,1536]{1,0:T(8,128)(2,1)S(1)}, bf16[32,1536]{1,0:T(8,128)(2,1)S(1)}) custom-call(bf16[512,1536]{1,0:T(8,128)(2,1)} %frames_hbm.1, f32[1536]{0:T(1024)} %gain_hbm.1), custom_call_target="tpu_custom_call" | custom-call | flops 400000000 | bytes 8000000 | tf_op jit(solution)/shard_map/norm_and_pool/pallas_call | solution.py:98
  2.2 4.1 %collective-permute-start = (bf16[32,1536]{1,0:T(8,128)(2,1)S(1)}, bf16[32,1536]{1,0:T(8,128)(2,1)S(1)}, u32[]{:S(2)}, u32[]{:S(2)}) collective-permute-start(bf16[32,1536]{1,0:T(8,128)(2,1)S(1)} %get-tuple-element.29.high_ref), channel_id=1, source_target_pairs={{0,8},{1,3},{2,10},{3,1},{4,12},{5,7},{6,14},{7,5},{8,0},{9,11},{1... | collective-permute-start | bytes 294920 | tf_op jit(solution)/shard_map/ppermute | solution.py:281
  6.3 0.0 copy-done
  6.3 0.0 copy-start.2
  6.3 0.0 copy-start.3
  6.3 1.4 %convolution_convert_fusion.2.q_ref = bf16[512,768]{1,0:T(8,128)(2,1)S(1)} fusion(bf16[512,1536]{1,0:T(8,128)(2,1)S(1)} %get-tuple-element.36, bf16[1536,768]{1,0:T(8,128)(2,1)S(1)} %copy-done), kind=kOutput, calls=%fused_computation.2 | convolution fusion | flops 1208352768 | bytes 4718592 | tf_op jit(solution)/shard_map/dot_general | solution.py:284
  7.7 1.2 %collective-permute-done.came_ref = bf16[32,1536]{1,0:T(8,128)(2,1)S(1)} collective-permute-done((bf16[32,1536]{1,0:T(8,128)(2,1)S(1)}, bf16[32,1536]{1,0:T(8,128)(2,1)S(1)}, u32[]{:S(2)}, u32[]{:S(2)}) %collective-permute-start) | collective-permute-done | bytes 98336 | tf_op jit(solution)/shard_map/ppermute | solution.py:281
  8.9 0.0 copy-done.2
  8.9 0.0 copy-done.3
  8.9 0.9 %pooled_keys_values.1 = bf16[64,1536]{1,0:T(8,128)(2,1)S(1)} custom-call(bf16[32,1536]{1,0:T(8,128)(2,1)S(1)} %get-tuple-element.29.high_ref, bf16[32,1536]{1,0:T(8,128)(2,1)S(1)} %get-tuple-element.34.low_ref, bf16[32,1536]{1,0:T(8,128)(2,1)S(1)} %collective-permute-done.came_ref, bf16[1536,768]{1,0:T(8,128)(2,1)S(1)} %copy-done.3, ...), custom_call_target="tpu_custom_call" | custom-call | tf_op jit(solution)/shard_map/pooled_keys_values/pallas_call | solution.py:289
  9.8 1.9 %collective-permute-start.2 = (bf16[64,1536]{1,0:T(8,128)(2,1)S(1)}, bf16[64,1536]{1,0:T(8,128)(2,1)S(1)}, u32[]{:S(2)}, u32[]{:S(2)}) collective-permute-start(bf16[64,1536]{1,0:T(8,128)(2,1)S(1)} %pooled_keys_values.1), channel_id=1, source_target_pairs={{0,2},{1,5},{2,0},{3,7},{4,6},{5,1},{6,4},{7,3},{8,10},{9,13},{10,... | collective-permute-start | bytes 589832 | tf_op jit(solution)/shard_map/ppermute | solution.py:281
  11.7 1.7 %collective-permute-start.1 = (bf16[64,1536]{1,0:T(8,128)(2,1)S(1)}, bf16[64,1536]{1,0:T(8,128)(2,1)S(1)}, u32[]{:S(2)}, u32[]{:S(2)}) collective-permute-start(bf16[64,1536]{1,0:T(8,128)(2,1)S(1)} %pooled_keys_values.1), channel_id=1, source_target_pairs={{0,4},{1,9},{2,6},{3,11},{4,0},{5,13},{6,2},{7,15},{8,12},{9,1},{1... | collective-permute-start | bytes 589832 | tf_op jit(solution)/shard_map/ppermute | solution.py:281
  13.4 1.4 %convolution_convert_fusion.v_ref = bf16[512,768]{1,0:T(8,128)(2,1)S(1)} fusion(bf16[512,1536]{1,0:T(8,128)(2,1)S(1)} %get-tuple-element.36, bf16[1536,768]{1,0:T(8,128)(2,1)S(1)} %copy-done.2), kind=kOutput, calls=%fused_computation | convolution fusion | flops 1208352768 | bytes 4718592 | tf_op jit(solution)/shard_map/dot_general | solution.py:284
  14.8 1.4 %convolution_convert_fusion.1.k_ref = bf16[512,768]{1,0:T(8,128)(2,1)S(1)} fusion(bf16[512,1536]{1,0:T(8,128)(2,1)S(1)} %get-tuple-element.36, bf16[1536,768]{1,0:T(8,128)(2,1)S(1)} %copy-done.3), kind=kOutput, calls=%fused_computation.1 | convolution fusion | flops 1208352768 | bytes 4718592 | tf_op jit(solution)/shard_map/dot_general | solution.py:284
  16.2 0.0 collective-permute-done.2
  16.2 1.2 %collective-permute-done.1 = bf16[64,1536]{1,0:T(8,128)(2,1)S(1)} collective-permute-done((bf16[64,1536]{1,0:T(8,128)(2,1)S(1)}, bf16[64,1536]{1,0:T(8,128)(2,1)S(1)}, u32[]{:S(2)}, u32[]{:S(2)}) %collective-permute-start.1) | collective-permute-done | bytes 196640 | tf_op jit(solution)/shard_map/ppermute | solution.py:281
  17.5 0.1 collective-permute-start.4
  17.6 1.0 %collective-permute-start.3 = (bf16[64,1536]{1,0:T(8,128)(2,1)S(1)}, bf16[64,1536]{1,0:T(8,128)(2,1)S(1)}, u32[]{:S(2)}, u32[]{:S(2)}) collective-permute-start(bf16[64,1536]{1,0:T(8,128)(2,1)S(1)} %collective-permute-done.1), channel_id=1, source_target_pairs={{0,2},{1,5},{2,0},{3,7},{4,6},{5,1},{6,4},{7,3},{8,10},{9,13},{10,... | collective-permute-start | bytes 589832 | tf_op jit(solution)/shard_map/ppermute | solution.py:281
  18.6 0.8 %mask_biases.1 = (f32[384,256]{1,0:T(8,128)S(1)}, f32[64,256]{1,0:T(8,128)S(1)}, f32[64,256]{1,0:T(8,128)S(1)}) custom-call(s32[32]{0:T(128)} %time_hbm), custom_call_target="tpu_custom_call" | custom-call | tf_op jit(solution)/shard_map/mask_biases/pallas_call | solution.py:84
  19.4 0.2 collective-permute-done.4.other_ref
  19.6 2.7 %local_and_first.1 = (f32[768,512]{1,0:T(8,128)S(1)}, f32[8,512]{1,0:T(8,128)S(1)}, f32[8,512]{1,0:T(8,128)S(1)}) custom-call(f32[384,256]{1,0:T(8,128)S(1)} %get-tuple-element.38.bias_ref, bf16[512,768]{1,0:T(8,128)(2,1)S(1)} %convolution_convert_fusion.2.q_ref, bf16[512,768]{1,0:T(8,128)(2,1)S(1)} %convolution_convert_fusion.1.k_ref, ...), custom_call_target="tpu_custom_call" | custom-call | flops 900000000 | bytes 5000000 | tf_op jit(solution)/shard_map/local_and_first/pallas_call | solution.py:313
  22.3 0.0 copy-start.1
  22.3 1.1 %collective-permute-done.3.far_ref = bf16[64,1536]{1,0:T(8,128)(2,1)S(1)} collective-permute-done((bf16[64,1536]{1,0:T(8,128)(2,1)S(1)}, bf16[64,1536]{1,0:T(8,128)(2,1)S(1)}, u32[]{:S(2)}, u32[]{:S(2)}) %collective-permute-start.3) | collective-permute-done | bytes 196640 | tf_op jit(solution)/shard_map/ppermute | solution.py:281
  23.3 0.0 collective-permute-start.5
  23.3 0.9 %middle.1 = (f32[768,512]{1,0:T(8,128)S(1)}, f32[8,512]{1,0:T(8,128)S(1)}, f32[8,512]{1,0:T(8,128)S(1)}) custom-call(f32[64,256]{1,0:T(8,128)S(1)} %get-tuple-element.46.bias_ref, bf16[512,768]{1,0:T(8,128)(2,1)S(1)} %convolution_convert_fusion.2.q_ref, ...), custom_call_target="tpu_custom_call", output_to_operand_aliasing={{0}: (3, {}), {1}: (4, {}), {2}: (5, {})} | custom-call | flops 500000000 | bytes 5000000 | tf_op jit(solution)/shard_map/middle/pallas_call | solution.py:324
  24.3 0.5 %collective-permute-done.5.far_ref = bf16[64,1536]{1,0:T(8,128)(2,1)S(1)} collective-permute-done((bf16[64,1536]{1,0:T(8,128)(2,1)S(1)}, bf16[64,1536]{1,0:T(8,128)(2,1)S(1)}, u32[]{:S(2)}, u32[]{:S(2)}) %collective-permute-start.5) | collective-permute-done | bytes 196640 | tf_op jit(solution)/shard_map/ppermute | solution.py:281
  24.8 0.0 copy-done.1
  24.8 2.8 %last_and_output.1 = bf16[512,1536]{1,0:T(8,128)(2,1)} custom-call(f32[64,256]{1,0:T(8,128)S(1)} %get-tuple-element.32.bias_ref, bf16[512,768]{1,0:T(8,128)(2,1)S(1)} %convolution_convert_fusion.2.q_ref, bf16[64,1536]{1,0:T(8,128)(2,1)S(1)} %collective-permute-done.5.far_ref, f32[768,512]{1,0:T(8,128)S(1)} %get-tuple-element.50.acc_in, ...), custom_call_target="tpu_custom_call" | custom-call | flops 1700000000 | bytes 8000000 | tf_op jit(solution)/shard_map/last_and_output/pallas_call | solution.py:334
  (1 shorter events, 0.0 us)
Async XLA Ops:
  0.0 6.3 %copy-start = (bf16[1536,768]{1,0:T(8,128)(2,1)S(1)}, bf16[1536,768]{1,0:T(8,128)(2,1)}, u32[]{:S(2)}) copy-start(bf16[1536,768]{1,0:T(8,128)(2,1)} %param.10) | copy-start | bytes 7077892
  2.2 6.7 %collective-permute-start = (bf16[32,1536]{1,0:T(8,128)(2,1)S(1)}, bf16[32,1536]{1,0:T(8,128)(2,1)S(1)}, u32[]{:S(2)}, u32[]{:S(2)}) collective-permute-start(bf16[32,1536]{1,0:T(8,128)(2,1)S(1)} %get-tuple-element.29.high_ref), channel_id=1, source_target_pairs={{0,8},{1,3},{2,10},{3,1},{4,12},{5,7},{6,14},{7,5},{8,0},{9,11},{1... | collective-permute-start | bytes 294920 | tf_op jit(solution)/shard_map/ppermute | solution.py:281
  6.3 2.6 %copy-start.2 = (bf16[1536,768]{1,0:T(8,128)(2,1)S(1)}, bf16[1536,768]{1,0:T(8,128)(2,1)}, u32[]{:S(2)}) copy-start(bf16[1536,768]{1,0:T(8,128)(2,1)} %wv_ref.1) | copy-start | bytes 7077892
  6.3 2.6 %copy-start.3 = (bf16[1536,768]{1,0:T(8,128)(2,1)S(1)}, bf16[1536,768]{1,0:T(8,128)(2,1)}, u32[]{:S(2)}) copy-start(bf16[1536,768]{1,0:T(8,128)(2,1)} %wk_ref.1) | copy-start | bytes 7077892
  9.8 6.4 %collective-permute-start.2 = (bf16[64,1536]{1,0:T(8,128)(2,1)S(1)}, bf16[64,1536]{1,0:T(8,128)(2,1)S(1)}, u32[]{:S(2)}, u32[]{:S(2)}) collective-permute-start(bf16[64,1536]{1,0:T(8,128)(2,1)S(1)} %pooled_keys_values.1), channel_id=1, source_target_pairs={{0,2},{1,5},{2,0},{3,7},{4,6},{5,1},{6,4},{7,3},{8,10},{9,13},{10,... | collective-permute-start | bytes 589832 | tf_op jit(solution)/shard_map/ppermute | solution.py:281
  11.7 5.7 %collective-permute-start.1 = (bf16[64,1536]{1,0:T(8,128)(2,1)S(1)}, bf16[64,1536]{1,0:T(8,128)(2,1)S(1)}, u32[]{:S(2)}, u32[]{:S(2)}) collective-permute-start(bf16[64,1536]{1,0:T(8,128)(2,1)S(1)} %pooled_keys_values.1), channel_id=1, source_target_pairs={{0,4},{1,9},{2,6},{3,11},{4,0},{5,13},{6,2},{7,15},{8,12},{9,1},{1... | collective-permute-start | bytes 589832 | tf_op jit(solution)/shard_map/ppermute | solution.py:281
  17.5 2.1 %collective-permute-start.4 = (bf16[192,1536]{1,0:T(8,128)(2,1)S(1)}, bf16[192,1536]{1,0:T(8,128)(2,1)S(1)}, u32[]{:S(2)}, u32[]{:S(2)}) collective-permute-start(bf16[192,1536]{1,0:T(8,128)(2,1)S(1)} %pad_maximum_fusion.near_ref), channel_id=1, source_target_pairs={{0,1},{1,0},{2,3},{3,2},{4,5},{5,4},{6,7},{7,6},{8,9},{9,8},{10,11... | collective-permute-start | bytes 1769480 | tf_op jit(solution)/shard_map/ppermute | solution.py:281
  17.6 5.7 %collective-permute-start.3 = (bf16[64,1536]{1,0:T(8,128)(2,1)S(1)}, bf16[64,1536]{1,0:T(8,128)(2,1)S(1)}, u32[]{:S(2)}, u32[]{:S(2)}) collective-permute-start(bf16[64,1536]{1,0:T(8,128)(2,1)S(1)} %collective-permute-done.1), channel_id=1, source_target_pairs={{0,2},{1,5},{2,0},{3,7},{4,6},{5,1},{6,4},{7,3},{8,10},{9,13},{10,... | collective-permute-start | bytes 589832 | tf_op jit(solution)/shard_map/ppermute | solution.py:281
  22.3 2.5 %copy-start.1 = (bf16[768,1536]{1,0:T(8,128)(2,1)S(1)}, bf16[768,1536]{1,0:T(8,128)(2,1)}, u32[]{:S(2)}) copy-start(bf16[768,1536]{1,0:T(8,128)(2,1)} %wo_ref.1) | copy-start | bytes 7077892
  23.3 1.4 %collective-permute-start.5 = (bf16[64,1536]{1,0:T(8,128)(2,1)S(1)}, bf16[64,1536]{1,0:T(8,128)(2,1)S(1)}, u32[]{:S(2)}, u32[]{:S(2)}) collective-permute-start(bf16[64,1536]{1,0:T(8,128)(2,1)S(1)} %collective-permute-done.3.far_ref), channel_id=1, source_target_pairs={{0,1},{1,0},{2,3},{3,2},{4,5},{5,4},{6,7},{7,6},{8,9},{9,8},{10,11... | collective-permute-start | bytes 589832 | tf_op jit(solution)/shard_map/ppermute | solution.py:281
